TPU v7x, 256 devices: a whole 4x4x8 slice. The times are simulated.
256 devices in a mesh: ep: 128 (over z, x_hi, y, core), tp: 2 (over x_lo).
Axes of the slice: x: 4 (x_hi: 2, x_lo: 2; x = x_hi * 2 + x_lo), y: 4, z: 8, core: 2. Of those that a mesh axis runs over, the one named last changes fastest.
Arguments:
- tokens: bfloat16 [256, 256, 1280], P('ep', None, 'tp'), may hold values from -400 to 400
- router: bfloat16 [1280, 128], P('tp'), may hold values from -2 to 2
- w_in: bfloat16 [128, 1280, 2560], P('ep', None, 'tp'), may hold values from -0.15625 to 0.15625
- w_out: bfloat16 [128, 2560, 1280], P('ep', 'tp'), may hold values from -0.125 to 0.125
- grad_out: bfloat16 [256, 256, 1280], P('ep', None, 'tp'), may hold values from -6 to 6
Outputs:
- grad_tokens: bfloat16 [256, 256, 1280], P('ep', None, 'tp')
- grad_router: float32 [1280, 128], P('tp')
- grad_w_in: bfloat16 [128, 1280, 2560], P('ep', None, 'tp')
All inputs are finite; a program needn't handle non-finite values.
Results may differ from a plain program's by a relative error of at most 0.0095.
Values may be sent and summed in bfloat16 or wider, within the bound.
No kernel may reach another device: no remote copies, remote signals or barrier semaphores. Data moves between devices by JAX's collectives and lax.ppermute only.
A program may use at most 64 MiB of HBM per device.

v0:
```python
from functools import partial

import jax
import jax.numpy as jnp
from jax import lax
from jax.sharding import PartitionSpec as P


def on_device(tokens, router, w_in, w_out, grad_out):
    partial_logits = jnp.einsum("bmd,de->bme", tokens, router, preferred_element_type=jnp.float32)
    logits = lax.psum(partial_logits, "tp")
    dispatch = jax.nn.softmax(logits, axis=1)
    combine = jax.nn.softmax(logits, axis=2)
    dispatch_b = dispatch.astype(jnp.bfloat16)
    combine_b = combine.astype(jnp.bfloat16)
    slot_half = jnp.einsum(
        "bme,bmd->ebd", dispatch_b, tokens, preferred_element_type=jnp.float32
    ).astype(jnp.bfloat16)
    grad_half = jnp.einsum(
        "bme,bmd->ebd", combine_b, grad_out, preferred_element_type=jnp.float32
    ).astype(jnp.bfloat16)
    sent_in, sent_grad = (
        lax.all_to_all(slot_half, "ep", split_axis=0, concat_axis=1, tiled=True),
        lax.all_to_all(grad_half, "ep", split_axis=0, concat_axis=1, tiled=True),
    )
    slot_in, slot_grad = (
        lax.all_gather(sent_in, "tp", axis=2, tiled=True),
        lax.all_gather(sent_grad, "tp", axis=2, tiled=True),
    )
    slot_in = slot_in[0]
    slot_grad = slot_grad[0]
    weight_in = w_in[0]
    weight_out = w_out[0]
    all_rows = slot_in.shape[0]
    pre = jnp.dot(slot_in, weight_in, preferred_element_type=jnp.float32)
    act, back = jax.vjp(partial(jax.nn.gelu, approximate=True), pre)
    out_part = jnp.dot(act.astype(jnp.bfloat16), weight_out, preferred_element_type=jnp.float32)
    out_share = lax.psum_scatter(out_part, "tp", scatter_dimension=1, tiled=True).astype(
        jnp.bfloat16
    )
    slot_out = lax.all_to_all(
        out_share.reshape(1, all_rows, -1), "ep", split_axis=1, concat_axis=0, tiled=True
    )
    act_grad = jnp.einsum("bd,fd->bf", slot_grad, weight_out, preferred_element_type=jnp.float32)
    pre_grad = back(act_grad)[0].astype(jnp.bfloat16)
    grad_weight = jnp.einsum(
        "bd,bf->df", slot_in, pre_grad, preferred_element_type=jnp.float32
    ).astype(jnp.bfloat16)
    in_part = jnp.einsum("bf,df->bd", pre_grad, weight_in, preferred_element_type=jnp.float32)
    in_share = lax.psum_scatter(in_part, "tp", scatter_dimension=1, tiled=True).astype(jnp.bfloat16)
    slot_in_grad = lax.all_to_all(
        in_share.reshape(1, all_rows, -1), "ep", split_axis=1, concat_axis=0, tiled=True
    )
    combine_part = jnp.einsum(
        "bmd,ebd->bme", grad_out, slot_out, preferred_element_type=jnp.float32
    )
    combine_dot = lax.psum(combine_part, "tp")
    dispatch_part = jnp.einsum(
        "bmd,ebd->bme", tokens, slot_in_grad, preferred_element_type=jnp.float32
    )
    dispatch_dot = lax.psum(dispatch_part, "tp")
    logit_grad = combine * (combine_dot - jnp.sum(combine * combine_dot, axis=2, keepdims=True))
    logit_grad = logit_grad + dispatch * (
        dispatch_dot - jnp.sum(dispatch * dispatch_dot, axis=1, keepdims=True)
    )
    logit_b = logit_grad.astype(jnp.bfloat16)
    grad_tokens = jnp.einsum(
        "bme,ebd->bmd", dispatch_b, slot_in_grad, preferred_element_type=jnp.float32
    )
    grad_tokens = grad_tokens + jnp.einsum(
        "bme,de->bmd", logit_b, router, preferred_element_type=jnp.float32
    )
    router_part = jnp.einsum("bmd,bme->de", tokens, logit_b, preferred_element_type=jnp.float32)
    grad_router = lax.psum(router_part, "ep")
    return (
        grad_tokens.astype(jnp.bfloat16),
        grad_router,
        grad_weight.reshape(1, grad_weight.shape[0], grad_weight.shape[1]),
    )


def solution(mesh):
    placed = (
        P("ep", None, "tp"),
        P("tp", None),
        P("ep", None, "tp"),
        P("ep", "tp", None),
        P("ep", None, "tp"),
    )
    return jax.shard_map(
        on_device,
        mesh=mesh,
        in_specs=placed,
        out_specs=(P("ep", None, "tp"), P("tp", None), P("ep", None, "tp")),
        check_vma=False,
    )
```

profile of v0, /device:TPU:1, one launch (start us, length us, event | category | flops | bytes accessed | tf_op | source)
XLA Modules:
  0.0 1426.5 jit_solution(3008956966342415391)
XLA Ops:
  7.2 0.0 copy-start
  7.2 0.0 all-reduce.5.cloned.1.call-start
  7.2 2.3 fusion.52
  9.5 0.0 all-reduce.5.cloned.1.call-update
  9.6 0.0 reduce-scatter.5.cloned.1.call-start
  9.6 39.8 %all-reduce.5.cloned.1.call-done = f32[2,256,128]{2,1,0:T(8,128)} async-done(((f32[2,256,128]{2,1,0:T(8,128)}), f32[2,256,128]{2,1,0:T(8,128)}) %all-reduce.5.cloned.1.call-update) | async-done | bytes 262160 | tf_op jit(solution)/shard_map/psum | solution.py:11
  49.4 1.8 fusion.63
  51.3 2.3 fusion.26
  53.6 1.3 copy.41
  54.9 31.2 %all_to_all.48 = bf16[128,2,640]{2,1,0:T(2,128)(2,1)} all-to-all(bf16[128,2,640]{2,1,0:T(2,128)(2,1)S(1)} %copy.41), channel_id=1, replica_groups=mesh['ep'=128,'tp'=2] {'ep'}, dimensions={0} | all-to-all | bytes 655360 | tf_op jit(solution)/shard_map/all_to_all | solution.py:23
  86.1 1.8 all_to_all.19
  87.9 10.3 all_gather.7
  98.2 0.9 copy-done.2
  99.1 2.9 fusion.7
  102.0 1.0 copy-done.4
  103.1 2.3 fusion.9
  105.4 0.0 reduce-scatter.5.cloned.1.call-update
  105.4 0.0 reduce-scatter.3.cloned.1.call-start
  105.5 0.9 copy-done.1
  106.4 0.8 fusion.64
  107.2 2.9 fusion.25
  110.1 1.3 copy.39
  111.4 23.2 %all_to_all.49 = bf16[128,2,640]{2,1,0:T(2,128)(2,1)} all-to-all(bf16[128,2,640]{2,1,0:T(2,128)(2,1)S(1)} %copy.39), channel_id=1, replica_groups=mesh['ep'=128,'tp'=2] {'ep'}, dimensions={0} | all-to-all | bytes 655360 | tf_op jit(solution)/shard_map/all_to_all | solution.py:24
  134.6 1.8 all_to_all.17
  136.4 10.5 all_gather.6
  146.9 2.9 fusion.20
  149.8 0.8 copy-done.5
  150.7 2.1 fusion.5
  152.8 0.0 reduce-scatter.3.cloned.1.call-update
  152.8 0.0 reduce-scatter.5.cloned.1.call-done
  152.8 1.1 convert_bitcast_fusion
  154.0 1.3 copy.66
  155.3 0.6 broadcast.45
  155.9 4.5 reduce.5
  160.4 1.8 reshape.42
  162.2 6.9 all-to-all-start.3
  169.1 6.4 reduce-scatter.3.cloned.1.call-done
  175.5 1.1 convert_bitcast_fusion.1
  176.6 1.3 copy.67
  177.9 4.3 reduce.4
  182.2 1.8 reshape.40
  184.1 2.0 all-to-all-done.3
  186.1 13.4 all-to-all-start.2
  199.5 0.3 all-reduce.9.cloned.1.call-start
  199.8 3.2 reshape.43
  203.0 3.7 bitcast_reduce_fusion
  206.7 1.8 all_to_all.43
  208.5 2.2 convolution_bitcast_fusion.2
  210.8 5.7 all-to-all-done.2
  216.4 3.2 reshape.41
  219.7 3.7 bitcast_reduce_fusion.1
  223.4 1.8 all_to_all.41
  225.2 2.2 convolution_bitcast_fusion.1
  227.4 0.0 all-reduce.9.cloned.1.call-update
  227.4 0.0 all-reduce.7.cloned.1.call-start
  227.5 4.1 fusion.4
  231.6 32.1 %all-reduce.9.cloned.1.call-done = (f32[2,256,128]{2,1,0:T(8,128)}, f32[2,256,128]{2,1,0:T(8,128)}) async-done(((f32[2,256,128]{2,1,0:T(8,128)}, f32[2,256,128]{2,1,0:T(8,128)}), (f32[2,256,128]{2,1,0:T(8,128)}, f32[2,256,128]{2,1,0:T(8,128)})) %all-reduce.9.cloned.1.call-update) | async-done | bytes 524304 | tf_op jit(solution)/shard_map/psum | solution.py:61
  263.6 2.0 fusion.31
  265.6 4.8 convolution_bitcast_fusion
  270.4 0.0 all-reduce.7.cloned.1.call-update
  270.4 2.4 fusion.48
  272.8 5.0 fusion.13
  277.8 1140.2 %all-reduce.7.cloned.1.call-done = f32[640,128]{0,1:T(8,128)} async-done(((f32[640,128]{0,1:T(8,128)}), f32[640,128]{0,1:T(8,128)}) %all-reduce.7.cloned.1.call-update) | async-done | bytes 327696 | tf_op jit(solution)/shard_map/psum | solution.py:74
  1418.1 1.9 copy.50
  (7 shorter events, 0.0 us)
Async XLA Ops:
  7.2 95.9 %copy-start = (bf16[1,1280,1280]{2,1,0:T(8,128)(2,1)S(1)}, bf16[1,1280,1280]{2,1,0:T(8,128)(2,1)}, u32[]{:S(2)}) copy-start(bf16[1,1280,1280]{2,1,0:T(8,128)(2,1)} %param.8) | copy-start | bytes 9830404
  7.2 42.3 %all-reduce.5.cloned.1.call-start = ((), (), s32[]{:S(2)}) async-start(), calls=%async_computation.6 | async-start | bytes 524288 | tf_op jit(solution)/shard_map/psum | solution.py:11
  9.6 143.3 %reduce-scatter.5.cloned.1.call-start = ((), (), s32[]{:S(2)}) async-start(), calls=%async_computation.8 | async-start | bytes 1966080 | tf_op jit(solution)/shard_map/reduce_scatter | solution.py:38
  98.2 0.9 copy-start.2
  102.0 1.1 copy-start.4
  105.4 0.9 copy-start.1
  105.4 70.0 %reduce-scatter.3.cloned.1.call-start = ((), (), s32[]{:S(2)}) async-start(), calls=%async_computation.7 | async-start | bytes 1966080 | tf_op jit(solution)/shard_map/reduce_scatter | solution.py:50
  146.9 3.8 copy-start.3
  149.8 0.8 copy-start.5
  162.2 23.9 %all-to-all-start.3 = ((bf16[128,2,640]{2,1,0:T(2,128)(2,1)}), bf16[128,2,640]{2,1,0:T(2,128)(2,1)}, u32[]{:S(2)}, u32[]{:S(2)}) async-start(bf16[128,2,640]{2,1,0:T(2,128)(2,1)} %reshape.42), calls=%async_computation.5 | async-start | bytes 655360 | tf_op jit(solution)/shard_map/all_to_all | solution.py:41
  186.1 30.4 %all-to-all-start.2 = ((bf16[128,2,640]{2,1,0:T(2,128)(2,1)}), bf16[128,2,640]{2,1,0:T(2,128)(2,1)}, u32[]{:S(2)}, u32[]{:S(2)}) async-start(bf16[128,2,640]{2,1,0:T(2,128)(2,1)} %reshape.40), calls=%async_computation.3 | async-start | bytes 655360 | tf_op jit(solution)/shard_map/all_to_all | solution.py:51
  199.5 64.1 %all-reduce.9.cloned.1.call-start = ((), (), s32[]{:S(2)}) async-start(), calls=%async_computation.10 | async-start | bytes 1048576 | tf_op jit(solution)/shard_map/psum | solution.py:61
  227.4 1190.6 %all-reduce.7.cloned.1.call-start = ((), (), s32[]{:S(2)}) async-start(), calls=%async_computation.9 | async-start | bytes 655360 | tf_op jit(solution)/shard_map/psum | solution.py:74
Sparse Core Ops, SparseCore 0:
  11.2 38.2 all-reduce.4
  105.6 24.2 reduce-scatter.4
  152.9 22.4 reduce-scatter.2
  227.6 35.9 all-reduce.8
  270.5 1147.4 all-reduce.6
where the time goes:
time: 1430 us
  waiting for transfers between devices  1230 us (86%)
  blocking collectives  75.1 us (5%)
  matrix products  38.6 us (3%)
  local copies, waits for them, and re-layouts  36.2 us (3%)
  starting transfers between devices  20.7 us (1%)
  other arithmetic  15.7 us (1%)
    psum x1, waiting for transfers between devices, on_device(): grad_router = lax.psum(router_part, 'ep')  1140 us
    psum x1, waiting for transfers between devices, on_device(): logits = lax.psum(partial_logits, 'tp')  39.8 us
    psum x1, waiting for transfers between devices, on_device(): dispatch_dot = lax.psum(dispatch_part, 'tp')  32.1 us
    all_to_all x1, blocking collectives, on_device(): lax.all_to_all(slot_half, 'ep', split_axis=0, concat_axis=1, tiled=True)  31.2 us
  transfers between devices with their start and end apart: 7, of which 6 were waited for; matrix products, arithmetic and copies ran while one was open for 3% of the time, Pallas kernels for 0%

commit v1 on v0

v1 whole, which is shorter than its diff:
```python
from functools import partial

import jax
import jax.numpy as jnp
from jax import lax
from jax.sharding import Mesh, PartitionSpec as P

AXES = ("z", "x_hi", "y", "core", "tp")
CHIPS = ("z", "x_hi", "y")
F32 = jnp.float32
BF16 = jnp.bfloat16


def swap(x, axis):
    return lax.ppermute(x, axis, [(0, 1), (1, 0)])


def pick(flag, a, b):
    return jnp.where(flag, a, b)


def to_experts(slots):
    core = lax.axis_index("core")
    by_core = slots.reshape(64, 2, 2, slots.shape[-1])
    keep = pick(core == 0, by_core[:, 0], by_core[:, 1])
    send = pick(core == 0, by_core[:, 1], by_core[:, 0])
    both = jnp.concatenate([keep, swap(send, "core")], axis=1)
    got = lax.all_to_all(both, CHIPS, split_axis=0, concat_axis=0, tiled=True)
    return got.reshape(256, slots.shape[-1])


def to_images(rows):
    core = lax.axis_index("core")
    got = lax.all_to_all(
        rows.reshape(64, 4, rows.shape[-1]), CHIPS, split_axis=0, concat_axis=0, tiled=True
    )
    keep = got[:, :2]
    other = swap(got[:, 2:], "core")
    by_core = jnp.stack([pick(core == 0, keep, other), pick(core == 0, other, keep)], axis=1)
    return by_core.reshape(128, 2, rows.shape[-1])


def widen(half):
    tp = lax.axis_index("tp")
    other = swap(half, "tp")
    return pick(
        tp == 0,
        jnp.concatenate([half, other], axis=1),
        jnp.concatenate([other, half], axis=1),
    )


def sum_halves(part):
    tp = lax.axis_index("tp")
    n = part.shape[1] // 2
    keep = pick(tp == 0, part[:, :n], part[:, n:])
    send = pick(tp == 0, part[:, n:], part[:, :n]).astype(BF16)
    return (keep + swap(send, "tp").astype(F32)).astype(BF16)


def sum_over_ep(part):
    core = lax.axis_index("core")
    n = part.shape[0] // 2
    keep = pick(core == 0, part[:n], part[n:])
    send = pick(core == 0, part[n:], part[:n])
    half = (keep + swap(send, "core")).reshape(8, n // 8, -1)
    got = lax.all_to_all(half, ("x_hi", "y"), split_axis=0, concat_axis=0, tiled=True)
    chunk = jnp.sum(got, axis=0)
    same = jnp.broadcast_to(chunk[None], (8,) + chunk.shape)
    got = lax.all_to_all(same, "z", split_axis=0, concat_axis=0, tiled=True)
    chunk = jnp.sum(got, axis=0)
    same = jnp.broadcast_to(chunk[None], (8,) + chunk.shape)
    got = lax.all_to_all(same, ("x_hi", "y"), split_axis=0, concat_axis=0, tiled=True)
    half = got.reshape(n, -1)
    other = swap(half, "core")
    return pick(
        core == 0,
        jnp.concatenate([half, other], axis=0),
        jnp.concatenate([other, half], axis=0),
    )


def on_device(tokens, router, w_in, w_out, grad_out):
    part = jnp.einsum("bmd,de->bme", tokens, router, preferred_element_type=F32)
    logits = part + swap(part, "tp")
    dispatch = jax.nn.softmax(logits, axis=1)
    combine = jax.nn.softmax(logits, axis=2)
    dispatch_b = dispatch.astype(BF16)
    combine_b = combine.astype(BF16)
    slot_half = jnp.einsum(
        "bme,bmd->ebd", dispatch_b, tokens, preferred_element_type=F32
    ).astype(BF16)
    grad_half = jnp.einsum(
        "bme,bmd->ebd", combine_b, grad_out, preferred_element_type=F32
    ).astype(BF16)
    slot_in = widen(to_experts(slot_half))
    slot_grad = widen(to_experts(grad_half))
    weight_in = w_in[0]
    weight_out = w_out[0]
    pre = jnp.dot(slot_in, weight_in, preferred_element_type=F32)
    act, back = jax.vjp(partial(jax.nn.gelu, approximate=True), pre)
    out_part = jnp.dot(act.astype(BF16), weight_out, preferred_element_type=F32)
    slot_out = to_images(sum_halves(out_part))
    act_grad = jnp.einsum("bd,fd->bf", slot_grad, weight_out, preferred_element_type=F32)
    pre_grad = back(act_grad)[0].astype(BF16)
    in_part = jnp.einsum("bf,df->bd", pre_grad, weight_in, preferred_element_type=F32)
    slot_in_grad = to_images(sum_halves(in_part))
    grad_weight = jnp.einsum(
        "bd,bf->df", slot_in, pre_grad, preferred_element_type=F32
    ).astype(BF16)
    combine_part = jnp.einsum("bmd,ebd->bme", grad_out, slot_out, preferred_element_type=F32)
    combine_dot = combine_part + swap(combine_part, "tp")
    dispatch_part = jnp.einsum("bmd,ebd->bme", tokens, slot_in_grad, preferred_element_type=F32)
    dispatch_dot = dispatch_part + swap(dispatch_part, "tp")
    logit_grad = combine * (combine_dot - jnp.sum(combine * combine_dot, axis=2, keepdims=True))
    logit_grad = logit_grad + dispatch * (
        dispatch_dot - jnp.sum(dispatch * dispatch_dot, axis=1, keepdims=True)
    )
    logit_b = logit_grad.astype(BF16)
    router_part = jnp.einsum("bmd,bme->de", tokens, logit_b, preferred_element_type=F32)
    grad_router = sum_over_ep(router_part)
    grad_tokens = jnp.einsum(
        "bme,ebd->bmd", dispatch_b, slot_in_grad, preferred_element_type=F32
    )
    grad_tokens = grad_tokens + jnp.einsum(
        "bme,de->bmd", logit_b, router, preferred_element_type=F32
    )
    return grad_tokens.astype(BF16), grad_router, grad_weight[None]


def solution(mesh):
    fine = Mesh(mesh.devices.reshape(8, 2, 4, 2, 2), AXES)
    ep = ("z", "x_hi", "y", "core")
    return jax.shard_map(
        on_device,
        mesh=fine,
        in_specs=(
            P(ep, None, "tp"),
            P("tp", None),
            P(ep, None, "tp"),
            P(ep, "tp", None),
            P(ep, None, "tp"),
        ),
        out_specs=(P(ep, None, "tp"), P("tp", None), P(ep, None, "tp")),
        check_vma=False,
    )
```

time: 1430 us -> 239 us (0.17)
  waiting for transfers between devices: 1230 us -> 67.1 us
  blocking collectives: 75.1 us -> 11.1 us
  starting transfers between devices: 20.7 us -> 72.4 us
    psum x3 -> x0, waiting for transfers between devices: 1210 us -> none  [the longest x1 1140 us: on_device(): grad_router = lax.psum(router_part, 'ep')]
    all_to_all x2 -> x1, blocking collectives: 54.4 us -> 11.1 us  [sum_over_ep(): lax.all_to_all(half, ('x_hi', 'y'), split_axis=0, concat_axis=0, tiled=True)]
    ppermute x0 -> x13, waiting for transfers between devices: none -> 31.8 us  [swap(): return lax.ppermute(x, axis, [(0, 1), (1, 0)])]
    all_to_all x2 -> x6, starting transfers between devices: 20.3 us -> 49.8 us  [the longest x2 21.7 us: to_experts(): got = lax.all_to_all(both, CHIPS, split_axis=0, concat_axis=0, tiled=True)]
    all_to_all x2 -> x6, waiting for transfers between devices: 7.66 us -> 35.3 us  [the longest x2 19 us: to_experts(): got = lax.all_to_all(both, CHIPS, split_axis=0, concat_axis=0, tiled=True)]
    ppermute x0 -> x13, starting transfers between devices: none -> 22.6 us  [swap(): return lax.ppermute(x, axis, [(0, 1), (1, 0)])]
    all_gather x2 -> x0, blocking collectives: 20.7 us -> none  [the longest x1 10.5 us: on_device(): lax.all_gather(sent_grad, 'tp', axis=2, tiled=True)]
    unnamed x18 -> x20, local copies, waits for them, and re-layouts: 16.2 us -> 1.43 us
  transfers between devices with their start and end apart: 7 -> 19, of which waited for: 6 -> 12; matrix products, arithmetic and copies ran while one was open for 3% -> 19% of each run, Pallas kernels for 0% -> 0%
where the time goes in v1:
time: 239 us; the launch traced here: 238 us
  starting transfers between devices  72.4 us (30%)
  waiting for transfers between devices  67.1 us (28%)
  matrix products  33.7 us (14%)
  local copies, waits for them, and re-layouts  31.3 us (13%)
  other arithmetic  21.1 us (9%)
  blocking collectives  11.1 us (5%)
    ppermute x13, waiting for transfers between devices, swap(): return lax.ppermute(x, axis, [(0, 1), (1, 0)])  31.8 us
    ppermute x13, starting transfers between devices, swap(): return lax.ppermute(x, axis, [(0, 1), (1, 0)])  22.6 us
    all_to_all x2, starting transfers between devices, to_experts(): got = lax.all_to_all(both, CHIPS, split_axis=0, concat_axis=0, tiled=True)  21.7 us
    all_to_all x2, starting transfers between devices, to_images(): lax.all_to_all(rows.reshape(64, 4, rows.shape[-1]), CHIPS, split_axis=0,...  20 us
    all_to_all x2, waiting for transfers between devices, to_experts(): got = lax.all_to_all(both, CHIPS, split_axis=0, concat_axis=0, tiled=True)  19 us
    all_to_all x1, blocking collectives, sum_over_ep(): lax.all_to_all(half, ('x_hi', 'y'), split_axis=0, concat_axis=0, tiled=True)  11.1 us
    all_to_all x2, waiting for transfers between devices, to_images(): lax.all_to_all(rows.reshape(64, 4, rows.shape[-1]), CHIPS, split_axis=0,...  7.59 us
    dot_general x1, matrix products, on_device(): jnp.einsum('bme,de->bmd', logit_b, router, preferred_element_type=F32)  5.18 us
  transfers between devices with their start and end apart: 19, of which 12 were waited for; matrix products, arithmetic and copies ran while one was open for 19% of the time, Pallas kernels for 0%

profile of v1, /device:TPU:1, one launch (start us, length us, event | category | flops | bytes accessed | tf_op | source)
XLA Modules:
  0.0 237.7 jit_solution(4612362169392978269)
XLA Ops:
  0.6 1.6 fusion.55
  2.3 2.1 collective-permute-start
  4.4 4.7 %collective-permute-done = f32[2,256,128]{2,1,0:T(8,128)} collective-permute-done((f32[2,256,128]{2,1,0:T(8,128)S(1)}, f32[2,256,128]{2,1,0:T(8,128)}, u32[]{:S(2)}, u32[]{:S(2)}) %collective-permute-start) | collective-permute-done | bytes 262176 | tf_op jit(solution)/shard_map/ppermute | solution.py:15
  11.8 2.2 fusion.26
  14.0 1.8 reshape.54
  15.8 1.7 fusion.76
  18.2 3.0 %collective-permute-start.3 = (bf16[64,2,640]{2,0,1:T(8,128)(2,1)}, bf16[64,2,640]{2,0,1:T(8,128)(2,1)}, u32[]{:S(2)}, u32[]{:S(2)}) collective-permute-start(bf16[64,2,640]{2,0,1:T(8,128)(2,1)} %get-tuple-element.6), channel_id=1, source_target_pairs={{0,2},{2,0},{1,3},{3,1},{4,6},{6,4},{5,7},{7,5},{8,10},{10,8},{9,1... | collective-permute-start | bytes 491528 | tf_op jit(solution)/shard_map/ppermute | solution.py:15
  21.2 2.9 %fusion.25 = bf16[128,2,640]{2,0,1:T(8,128)(2,1)} fusion(bf16[2,256,640]{2,1,0:T(8,128)(2,1)} %param.9, f32[2,256]{1,0:T(2,128)S(1)} %get-tuple-element.17, f32[2,256,128]{2,1,0:T(8,128)S(1)} %add.31), kind=kOutput, calls=%fused_computation.30 | convolution fusion | flops 84247168 | bytes 1247232 | tf_op jit(solution)/shard_map/bme,bmd->ebd/dot_general | solution.py:93
  24.1 1.8 reshape.52
  27.9 14.5 %all-to-all-start.1 = ((bf16[64,4,640]{2,1,0:T(4,128)(2,1)}), bf16[64,4,640]{2,1,0:T(4,128)(2,1)}, u32[]{:S(2)}, u32[]{:S(2)}) async-start(bf16[64,4,640]{2,1,0:T(4,128)(2,1)} %copy.56), calls=%async_computation.1 | async-start | bytes 655360 | tf_op jit(solution)/shard_map/all_to_all | solution.py:28
  42.4 1.7 fusion.75
  44.5 1.1 collective-permute-done.1
  46.6 9.0 %all-to-all-done.1 = bf16[64,4,640]{2,1,0:T(4,128)(2,1)} async-done(((bf16[64,4,640]{2,1,0:T(4,128)(2,1)}), bf16[64,4,640]{2,1,0:T(4,128)(2,1)}, u32[]{:S(2)}, u32[]{:S(2)}) %all-to-all-start.1) | async-done | bytes 327712 | tf_op jit(solution)/shard_map/all_to_all | solution.py:28
  55.6 7.3 %all-to-all-start = ((bf16[64,4,640]{2,1,0:T(4,128)(2,1)}), bf16[64,4,640]{2,1,0:T(4,128)(2,1)}, u32[]{:S(2)}, u32[]{:S(2)}) async-start(bf16[64,4,640]{2,1,0:T(4,128)(2,1)} %copy.52), calls=%async_computation | async-start | bytes 655360 | tf_op jit(solution)/shard_map/all_to_all | solution.py:28
  62.9 1.8 reshape.55
  65.0 10.0 %all-to-all-done = bf16[64,4,640]{2,1,0:T(4,128)(2,1)} async-done(((bf16[64,4,640]{2,1,0:T(4,128)(2,1)}), bf16[64,4,640]{2,1,0:T(4,128)(2,1)}, u32[]{:S(2)}, u32[]{:S(2)}) %all-to-all-start) | async-done | bytes 327712 | tf_op jit(solution)/shard_map/all_to_all | solution.py:28
  75.0 1.8 reshape.53
  77.1 3.4 %fusion.7 = f32[256,1280]{1,0:T(8,128)S(1)} fusion(bf16[1,1280,1280]{2,1,0:T(8,128)(2,1)} %param.7, bf16[256,640]{1,0:T(8,128)(2,1)} %collective-permute-done.4, bf16[256,640]{1,0:T(8,128)(2,1)} %reshape.55, pred[]{:T(512)S(6)} %eq.5), kind=kOutput, calls=%fused_computation.8 | convolution fusion | flops 841809920 | bytes 5242881 | tf_op jit(solution)/shard_map/dot_general | solution.py:100
  80.5 1.3 fusion.9
  81.8 1.4 collective-permute-start.7
  83.3 1.5 fusion.20
  84.8 2.1 fusion.5
  86.9 4.9 %collective-permute-done.7 = bf16[256,640]{1,0:T(8,128)(2,1)S(1)} collective-permute-done((bf16[256,640]{1,0:T(8,128)(2,1)S(1)}, bf16[256,640]{1,0:T(8,128)(2,1)S(1)}, u32[]{:S(2)}, u32[]{:S(2)}) %collective-permute-start.7) | collective-permute-done | bytes 327712 | tf_op jit(solution)/shard_map/ppermute | solution.py:15
  92.6 1.8 reshape.58
  94.4 8.3 %all-to-all-start.3 = ((bf16[64,4,640]{2,1,0:T(4,128)(2,1)}), bf16[64,4,640]{2,1,0:T(4,128)(2,1)}, u32[]{:S(2)}, u32[]{:S(2)}) async-start(bf16[64,4,640]{2,1,0:T(4,128)(2,1)} %reshape.58), calls=%async_computation.3 | async-start | bytes 655360 | tf_op jit(solution)/shard_map/all_to_all | solution.py:34
  102.6 1.4 select_convert_fusion.1
  104.0 1.2 collective-permute-start.5
  105.2 9.8 %collective-permute-done.5 = bf16[256,640]{1,0:T(8,128)(2,1)S(1)} collective-permute-done((bf16[256,640]{1,0:T(8,128)(2,1)S(1)}, bf16[256,640]{1,0:T(8,128)(2,1)S(1)}, u32[]{:S(2)}, u32[]{:S(2)}) %collective-permute-start.5) | collective-permute-done | bytes 327712 | tf_op jit(solution)/shard_map/ppermute | solution.py:15
  115.0 2.1 add_convert_fusion.1
  117.1 1.8 reshape.56
  118.8 11.8 %all-to-all-start.2 = ((bf16[64,4,640]{2,1,0:T(4,128)(2,1)}), bf16[64,4,640]{2,1,0:T(4,128)(2,1)}, u32[]{:S(2)}, u32[]{:S(2)}) async-start(bf16[64,4,640]{2,1,0:T(4,128)(2,1)} %reshape.56), calls=%async_computation.2 | async-start | bytes 655360 | tf_op jit(solution)/shard_map/all_to_all | solution.py:34
  130.6 1.8 slice.77
  132.4 2.7 %collective-permute-start.8 = (bf16[64,2,640]{2,1,0:T(2,128)(2,1)}, bf16[64,2,640]{2,1,0:T(2,128)(2,1)}, u32[]{:S(2)}, u32[]{:S(2)}) collective-permute-start(bf16[64,2,640]{2,1,0:T(2,128)(2,1)} %slice.77), channel_id=1, source_target_pairs={{0,2},{2,0},{1,3},{3,1},{4,6},{6,4},{5,7},{7,5},{8,10},{10,8},{9,1... | collective-permute-start | bytes 491528 | tf_op jit(solution)/shard_map/ppermute | solution.py:15
  135.1 7.6 %all-to-all-done.2 = bf16[64,4,640]{2,1,0:T(4,128)(2,1)} async-done(((bf16[64,4,640]{2,1,0:T(4,128)(2,1)}), bf16[64,4,640]{2,1,0:T(4,128)(2,1)}, u32[]{:S(2)}, u32[]{:S(2)}) %all-to-all-start.2) | async-done | bytes 327712 | tf_op jit(solution)/shard_map/all_to_all | solution.py:34
  142.7 1.8 slice.73
  144.5 4.8 %collective-permute-start.6 = (bf16[64,2,640]{2,1,0:T(2,128)(2,1)}, bf16[64,2,640]{2,1,0:T(2,128)(2,1)}, u32[]{:S(2)}, u32[]{:S(2)}) collective-permute-start(bf16[64,2,640]{2,1,0:T(2,128)(2,1)} %slice.73), channel_id=1, source_target_pairs={{0,2},{2,0},{1,3},{3,1},{4,6},{6,4},{5,7},{7,5},{8,10},{10,8},{9,1... | collective-permute-start | bytes 491528 | tf_op jit(solution)/shard_map/ppermute | solution.py:15
  149.4 1.3 fusion.52
  152.2 1.8 reshape.59
  154.0 1.3 fusion.50
  156.9 1.8 reshape.57
  158.7 1.6 convolution_bitcast_fusion.1
  161.6 1.3 collective-permute-start.9
  163.0 5.4 %collective-permute-done.10 = f32[2,256,128]{2,1,0:T(8,128)S(1)} collective-permute-done((f32[2,256,128]{2,1,0:T(8,128)S(1)}, f32[2,256,128]{2,1,0:T(8,128)S(1)}, u32[]{:S(2)}, u32[]{:S(2)}) %collective-permute-start.10) | collective-permute-done | bytes 262176 | tf_op jit(solution)/shard_map/ppermute | solution.py:15
  169.2 4.8 %collective-permute-done.9 = f32[2,256,128]{2,1,0:T(8,128)S(1)} collective-permute-done((f32[2,256,128]{2,1,0:T(8,128)S(1)}, f32[2,256,128]{2,1,0:T(8,128)S(1)}, u32[]{:S(2)}, u32[]{:S(2)}) %collective-permute-start.9) | collective-permute-done | bytes 262176 | tf_op jit(solution)/shard_map/ppermute | solution.py:15
  174.7 4.9 %convolution_bitcast_fusion = f32[640,128]{0,1:T(8,128)} fusion(bf16[2,256,640]{2,1,0:T(8,128)(2,1)} %param.5, f32[2,256,128]{2,1,0:T(8,128)} %fusion.31, f32[2,256,128]{2,1,0:T(8,128)} %copy-done.5, f32[2,256,128]{2,1,0:T(8,128)} %copy-done.7, f32[2,256,128]{2,1,0:T(8,128)} %get-tuple-element.18, f32[2,256]{1,0:T(2,128)S(1)} %get-tuple-element.17), kind=kOutput, calls=%fused_computation.32 | convolution fusion | flops 84476544 | bytes 2033664 | tf_op jit(solution)/shard_map/bmd,bme->de/dot_general | solution.py:120
  179.6 1.1 slice_select_fusion
  180.8 1.1 collective-permute-start.11
  181.9 1.1 collective-permute-done.11
  182.9 1.8 select_add_fusion
  184.8 1.7 copy.62
  186.5 11.1 %all_to_all.35 = f32[8,40,128]{2,1,0:T(8,128)} all-to-all(f32[8,40,128]{2,1,0:T(8,128)} %bitcast.73), channel_id=1, replica_groups=mesh['z'=8,'x_hi'=2,'y'=4,'core'=2,'tp'=2] {'x_hi','y'}, dimensions={0} | all-to-all | bytes 327680 | tf_op jit(solution)/shard_map/all_to_all | solution.py:67
  197.6 1.5 reduce_sum.58
  199.1 1.4 broadcast_in_dim.6
  200.5 4.0 %all-to-all-start.5 = ((f32[8,40,128]{2,1,0:T(8,128)}), f32[8,40,128]{2,1,0:T(8,128)}, u32[]{:S(2)}, u32[]{:S(2)}) async-start(f32[8,40,128]{2,1,0:T(8,128)} %broadcast_in_dim.6), calls=%async_computation.5 | async-start | bytes 327680 | tf_op jit(solution)/shard_map/all_to_all | solution.py:70
  204.5 4.4 %fusion.4 = bf16[1,1280,1280]{2,1,0:T(8,128)(2,1)} fusion(bf16[256,1280]{1,0:T(8,128)(2,1)} %copy-done.9, bf16[256,640]{1,0:T(8,128)(2,1)} %collective-permute-done.4, bf16[256,640]{1,0:T(8,128)(2,1)} %reshape.55, pred[]{:T(512)S(6)} %eq.5), kind=kOutput, calls=%fused_computation.5 | convolution fusion | flops 843448320 | bytes 4587521 | tf_op jit(solution)/shard_map/bd,bf->df/dot_general | solution.py:108
  208.9 4.0 %all-to-all-done.5 = f32[8,40,128]{2,1,0:T(8,128)} async-done(((f32[8,40,128]{2,1,0:T(8,128)}), f32[8,40,128]{2,1,0:T(8,128)}, u32[]{:S(2)}, u32[]{:S(2)}) %all-to-all-start.5) | async-done | bytes 163872 | tf_op jit(solution)/shard_map/all_to_all | solution.py:70
  212.9 1.5 reduce_sum.59
  214.4 1.4 broadcast_in_dim.7
  215.8 4.0 %all-to-all-start.6 = ((f32[8,40,128]{2,1,0:T(8,128)}), f32[8,40,128]{2,1,0:T(8,128)}, u32[]{:S(2)}, u32[]{:S(2)}) async-start(f32[8,40,128]{2,1,0:T(8,128)} %broadcast_in_dim.7), calls=%async_computation.6 | async-start | bytes 327680 | tf_op jit(solution)/shard_map/all_to_all | solution.py:73
  219.8 2.4 %fusion.59 = f32[2,256,640]{2,1,0:T(8,128)} fusion(bf16[128,2,640]{2,0,1:T(8,128)(2,1)} %reshape.57, f32[2,128]{1,0:T(2,128)S(1)} %get-tuple-element.15, f32[2,256,128]{2,1,0:T(8,128)S(1)} %add.31), kind=kOutput, calls=%fused_computation.90 | convolution fusion | flops 84083200 | bytes 1901568 | tf_op jit(solution)/shard_map/bme,ebd->bmd/dot_general | solution.py:122
  222.2 4.7 %all-to-all-done.6 = f32[8,40,128]{2,1,0:T(8,128)} async-done(((f32[8,40,128]{2,1,0:T(8,128)}), f32[8,40,128]{2,1,0:T(8,128)}, u32[]{:S(2)}, u32[]{:S(2)}) %all-to-all-start.6) | async-done | bytes 163872 | tf_op jit(solution)/shard_map/all_to_all | solution.py:73
  227.0 3.8 %collective-permute-start.12 = (f32[320,128]{1,0:T(8,128)}, f32[320,128]{1,0:T(8,128)S(1)}, u32[]{:S(2)}, u32[]{:S(2)}) collective-permute-start(f32[320,128]{1,0:T(8,128)} %bitcast.19), channel_id=1, source_target_pairs={{0,2},{2,0},{1,3},{3,1},{4,6},{6,4},{5,7},{7,5},{8,10},{10,8},{9,1... | collective-permute-start | bytes 491528 | tf_op jit(solution)/shard_map/ppermute | solution.py:15
  230.8 5.2 %fusion.13 = bf16[2,256,640]{2,1,0:T(8,128)(2,1)} fusion(f32[2,256,640]{2,1,0:T(8,128)} %fusion.59, f32[2,256,128]{2,1,0:T(8,128)} %fusion.31, bf16[640,128]{1,0:T(8,128)(2,1)} %param.6, f32[2,256,128]{2,1,0:T(8,128)} %copy-done.5, f32[2,256,128]{2,1,0:T(8,128)} %copy-done.7, f32[2,256,128]{2,1,0:T(8,128)} %get-tuple-element.18, ...), kind=kOutput, calls=%fused_computation.17 | convolution fusion | flops 85131904 | bytes 3180544 | tf_op jit(solution)/shard_map/bme,de->bmd/dot_general | solution.py:125
  235.9 1.7 maximum_select_fusion.3
  (48 shorter events, 14.3 us)
Async XLA Ops:
  0.6 79.8 %copy-start = (bf16[1,1280,1280]{2,1,0:T(8,128)(2,1)S(1)}, bf16[1,1280,1280]{2,1,0:T(8,128)(2,1)}, u32[]{:S(2)}) copy-start(bf16[1,1280,1280]{2,1,0:T(8,128)(2,1)} %param.8) | copy-start | bytes 9830404
  2.2 2.1 copy-start.2
  2.3 6.8 %collective-permute-start = (f32[2,256,128]{2,1,0:T(8,128)S(1)}, f32[2,256,128]{2,1,0:T(8,128)}, u32[]{:S(2)}, u32[]{:S(2)}) collective-permute-start(f32[2,256,128]{2,1,0:T(8,128)S(1)} %fusion.55), channel_id=1, source_target_pairs={{0,1},{1,0},{2,3},{3,2},{4,5},{5,4},{6,7},{7,6},{8,9},{9,8},{10,11... | collective-permute-start | bytes 786440 | tf_op jit(solution)/shard_map/ppermute | solution.py:15
  18.2 7.7 %collective-permute-start.3 = (bf16[64,2,640]{2,0,1:T(8,128)(2,1)}, bf16[64,2,640]{2,0,1:T(8,128)(2,1)}, u32[]{:S(2)}, u32[]{:S(2)}) collective-permute-start(bf16[64,2,640]{2,0,1:T(8,128)(2,1)} %get-tuple-element.6), channel_id=1, source_target_pairs={{0,2},{2,0},{1,3},{3,1},{4,6},{6,4},{5,7},{7,5},{8,10},{10,8},{9,1... | collective-permute-start | bytes 491528 | tf_op jit(solution)/shard_map/ppermute | solution.py:15
  27.9 27.7 %all-to-all-start.1 = ((bf16[64,4,640]{2,1,0:T(4,128)(2,1)}), bf16[64,4,640]{2,1,0:T(4,128)(2,1)}, u32[]{:S(2)}, u32[]{:S(2)}) async-start(bf16[64,4,640]{2,1,0:T(4,128)(2,1)} %copy.56), calls=%async_computation.1 | async-start | bytes 655360 | tf_op jit(solution)/shard_map/all_to_all | solution.py:28
  44.1 1.5 collective-permute-start.1
  55.6 19.4 %all-to-all-start = ((bf16[64,4,640]{2,1,0:T(4,128)(2,1)}), bf16[64,4,640]{2,1,0:T(4,128)(2,1)}, u32[]{:S(2)}, u32[]{:S(2)}) async-start(bf16[64,4,640]{2,1,0:T(4,128)(2,1)} %copy.52), calls=%async_computation | async-start | bytes 655360 | tf_op jit(solution)/shard_map/all_to_all | solution.py:28
  64.7 12.4 %collective-permute-start.4 = (bf16[256,640]{1,0:T(8,128)(2,1)}, bf16[256,640]{1,0:T(8,128)(2,1)}, u32[]{:S(2)}, u32[]{:S(2)}) collective-permute-start(bf16[256,640]{1,0:T(8,128)(2,1)} %reshape.55), channel_id=1, source_target_pairs={{0,1},{1,0},{2,3},{3,2},{4,5},{5,4},{6,7},{7,6},{8,9},{9,8},{10,11... | collective-permute-start | bytes 983048 | tf_op jit(solution)/shard_map/ppermute | solution.py:15
  76.8 6.5 %collective-permute-start.2 = (bf16[256,640]{1,0:T(8,128)(2,1)}, bf16[256,640]{1,0:T(8,128)(2,1)S(1)}, u32[]{:S(2)}, u32[]{:S(2)}) collective-permute-start(bf16[256,640]{1,0:T(8,128)(2,1)} %reshape.53), channel_id=1, source_target_pairs={{0,1},{1,0},{2,3},{3,2},{4,5},{5,4},{6,7},{7,6},{8,9},{9,8},{10,11... | collective-permute-start | bytes 983048 | tf_op jit(solution)/shard_map/ppermute | solution.py:15
  80.5 2.8 %copy-start.4 = (bf16[256,640]{1,0:T(8,128)(2,1)S(1)}, bf16[256,640]{1,0:T(8,128)(2,1)}, u32[]{:S(2)}) copy-start(bf16[256,640]{1,0:T(8,128)(2,1)} %reshape.53) | copy-start | bytes 983044
  81.8 2.9 %copy-start.8 = (bf16[1,1280,1280]{2,1,0:T(8,128)(2,1)S(1)}, bf16[1,1280,1280]{2,1,0:T(8,128)(2,1)}, u32[]{:S(2)}) copy-start(bf16[1,1280,1280]{2,1,0:T(8,128)(2,1)} %param.7) | copy-start | bytes 9830404
  81.8 9.9 %collective-permute-start.7 = (bf16[256,640]{1,0:T(8,128)(2,1)S(1)}, bf16[256,640]{1,0:T(8,128)(2,1)S(1)}, u32[]{:S(2)}, u32[]{:S(2)}) collective-permute-start(bf16[256,640]{1,0:T(8,128)(2,1)S(1)} %select_convert_fusion), channel_id=1, source_target_pairs={{0,1},{1,0},{2,3},{3,2},{4,5},{5,4},{6,7},{7,6},{8,9},{9,8},{10,11... | collective-permute-start | bytes 983048 | tf_op jit(solution)/shard_map/ppermute | solution.py:15
  84.8 2.1 copy-start.9
  94.4 24.5 %all-to-all-start.3 = ((bf16[64,4,640]{2,1,0:T(4,128)(2,1)}), bf16[64,4,640]{2,1,0:T(4,128)(2,1)}, u32[]{:S(2)}, u32[]{:S(2)}) async-start(bf16[64,4,640]{2,1,0:T(4,128)(2,1)} %reshape.58), calls=%async_computation.3 | async-start | bytes 655360 | tf_op jit(solution)/shard_map/all_to_all | solution.py:34
  104.0 11.0 %collective-permute-start.5 = (bf16[256,640]{1,0:T(8,128)(2,1)S(1)}, bf16[256,640]{1,0:T(8,128)(2,1)S(1)}, u32[]{:S(2)}, u32[]{:S(2)}) collective-permute-start(bf16[256,640]{1,0:T(8,128)(2,1)S(1)} %select_convert_fusion.1), channel_id=1, source_target_pairs={{0,1},{1,0},{2,3},{3,2},{4,5},{5,4},{6,7},{7,6},{8,9},{9,8},{10,11... | collective-permute-start | bytes 983048 | tf_op jit(solution)/shard_map/ppermute | solution.py:15
  118.8 23.9 %all-to-all-start.2 = ((bf16[64,4,640]{2,1,0:T(4,128)(2,1)}), bf16[64,4,640]{2,1,0:T(4,128)(2,1)}, u32[]{:S(2)}, u32[]{:S(2)}) async-start(bf16[64,4,640]{2,1,0:T(4,128)(2,1)} %reshape.56), calls=%async_computation.2 | async-start | bytes 655360 | tf_op jit(solution)/shard_map/all_to_all | solution.py:34
  132.4 16.9 %collective-permute-start.8 = (bf16[64,2,640]{2,1,0:T(2,128)(2,1)}, bf16[64,2,640]{2,1,0:T(2,128)(2,1)}, u32[]{:S(2)}, u32[]{:S(2)}) collective-permute-start(bf16[64,2,640]{2,1,0:T(2,128)(2,1)} %slice.77), channel_id=1, source_target_pairs={{0,2},{2,0},{1,3},{3,1},{4,6},{6,4},{5,7},{7,5},{8,10},{10,8},{9,1... | collective-permute-start | bytes 491528 | tf_op jit(solution)/shard_map/ppermute | solution.py:15
  144.5 9.5 %collective-permute-start.6 = (bf16[64,2,640]{2,1,0:T(2,128)(2,1)}, bf16[64,2,640]{2,1,0:T(2,128)(2,1)}, u32[]{:S(2)}, u32[]{:S(2)}) collective-permute-start(bf16[64,2,640]{2,1,0:T(2,128)(2,1)} %slice.73), channel_id=1, source_target_pairs={{0,2},{2,0},{1,3},{3,1},{4,6},{6,4},{5,7},{7,5},{8,10},{10,8},{9,1... | collective-permute-start | bytes 491528 | tf_op jit(solution)/shard_map/ppermute | solution.py:15
  158.7 1.8 copy-start.1
  158.7 1.8 copy-start.3
  158.7 9.6 %copy-start.6 = (f32[2,256,128]{2,1,0:T(8,128)S(1)}, f32[2,256,128]{2,1,0:T(8,128)}, u32[]{:S(2)}) copy-start(f32[2,256,128]{2,1,0:T(8,128)} %get-tuple-element.16) | copy-start | bytes 786436
  160.4 8.0 %collective-permute-start.10 = (f32[2,256,128]{2,1,0:T(8,128)S(1)}, f32[2,256,128]{2,1,0:T(8,128)S(1)}, u32[]{:S(2)}, u32[]{:S(2)}) collective-permute-start(f32[2,256,128]{2,1,0:T(8,128)S(1)} %convolution_bitcast_fusion.1), channel_id=1, source_target_pairs={{0,1},{1,0},{2,3},{3,2},{4,5},{5,4},{6,7},{7,6},{8,9},{9,8},{10,11... | collective-permute-start | bytes 786440 | tf_op jit(solution)/shard_map/ppermute | solution.py:15
  160.9 0.7 copy-start.5
  161.6 12.4 %collective-permute-start.9 = (f32[2,256,128]{2,1,0:T(8,128)S(1)}, f32[2,256,128]{2,1,0:T(8,128)S(1)}, u32[]{:S(2)}, u32[]{:S(2)}) collective-permute-start(f32[2,256,128]{2,1,0:T(8,128)S(1)} %convolution_bitcast_fusion.2), channel_id=1, source_target_pairs={{0,1},{1,0},{2,3},{3,2},{4,5},{5,4},{6,7},{7,6},{8,9},{9,8},{10,11... | collective-permute-start | bytes 786440 | tf_op jit(solution)/shard_map/ppermute | solution.py:15
  174.0 0.7 copy-start.7
  180.8 2.2 collective-permute-start.11
  200.5 12.4 %all-to-all-start.5 = ((f32[8,40,128]{2,1,0:T(8,128)}), f32[8,40,128]{2,1,0:T(8,128)}, u32[]{:S(2)}, u32[]{:S(2)}) async-start(f32[8,40,128]{2,1,0:T(8,128)} %broadcast_in_dim.6), calls=%async_computation.5 | async-start | bytes 327680 | tf_op jit(solution)/shard_map/all_to_all | solution.py:70
  215.8 11.2 %all-to-all-start.6 = ((f32[8,40,128]{2,1,0:T(8,128)}), f32[8,40,128]{2,1,0:T(8,128)}, u32[]{:S(2)}, u32[]{:S(2)}) async-start(f32[8,40,128]{2,1,0:T(8,128)} %broadcast_in_dim.7), calls=%async_computation.6 | async-start | bytes 327680 | tf_op jit(solution)/shard_map/all_to_all | solution.py:73
  227.0 8.9 %collective-permute-start.12 = (f32[320,128]{1,0:T(8,128)}, f32[320,128]{1,0:T(8,128)S(1)}, u32[]{:S(2)}, u32[]{:S(2)}) collective-permute-start(f32[320,128]{1,0:T(8,128)} %bitcast.19), channel_id=1, source_target_pairs={{0,2},{2,0},{1,3},{3,1},{4,6},{6,4},{5,7},{7,5},{8,10},{10,8},{9,1... | collective-permute-start | bytes 491528 | tf_op jit(solution)/shard_map/ppermute | solution.py:15

commit v2 on v0

v2 whole, which is shorter than its diff:
```python
import jax
import jax.numpy as jnp
from jax import lax
from jax.experimental import pallas as pl
from jax.experimental.pallas import tpu as pltpu
from jax.sharding import Mesh, PartitionSpec as P

AXES = ("z", "x_hi", "y", "core", "tp")
CHIPS = ("z", "x_hi", "y")
F32 = jnp.float32
BF16 = jnp.bfloat16
I32 = jnp.int32
NQ = 64
B = 2
M = 256
E = 128
H = 640
D = 1280
FH = 1280
CH = 256
MIB = 1 << 20

SMEM = pl.BlockSpec(memory_space=pltpu.SMEM)
VMEM = pl.BlockSpec(memory_space=pltpu.VMEM)


def dot(a, b):
    return jnp.dot(a, b, preferred_element_type=F32)


def dot_t(a, b):
    return lax.dot_general(a, b, (((1,), (1,)), ((), ())), preferred_element_type=F32)


def t_dot(a, b):
    return lax.dot_general(a, b, (((0,), (0,)), ((), ())), preferred_element_type=F32)


def rows_cols(rows, cols):
    return (
        lax.broadcasted_iota(I32, (rows, cols), 0),
        lax.broadcasted_iota(I32, (rows, cols), 1),
    )


def ones_where(mask):
    return jnp.where(mask, 1.0, 0.0).astype(BF16)


def expert_order(core):
    e, p = rows_cols(E, E)
    return ones_where(e == 2 * (p & 63) + (core ^ (p >> 6)))


def call(kernel, outs, flops, nbytes, limit=None):
    def run(*args):
        return pl.pallas_call(
            kernel,
            out_shape=[jax.ShapeDtypeStruct(s, d) for s, d in outs],
            in_specs=[SMEM if a.dtype == I32 else VMEM for a in args],
            out_specs=[VMEM for _ in outs],
            cost_estimate=pl.CostEstimate(
                flops=int(flops), bytes_accessed=int(nbytes), transcendentals=0
            ),
            compiler_params=pltpu.CompilerParams(vmem_limit_bytes=(limit or 24) * MIB),
        )(*args)

    return run


def logits_kernel(ids, tokens, router, part, ordered):
    r = dot(router[...], expert_order(ids[0])).astype(BF16)
    ordered[...] = r
    for b in range(B):
        part[b * M : (b + 1) * M, :] = dot(tokens[b], r)


def slots_kernel(part, other, tokens, grad, dispatch, combine, keep, send):
    for b in range(B):
        rows = slice(b * M, (b + 1) * M)
        logits = part[rows, :] + other[rows, :]
        up = jnp.exp(logits - jnp.max(logits, axis=0, keepdims=True))
        d = up / jnp.sum(up, axis=0, keepdims=True)
        up = jnp.exp(logits - jnp.max(logits, axis=1, keepdims=True))
        c = up / jnp.sum(up, axis=1, keepdims=True)
        dispatch[rows, :] = d
        combine[rows, :] = c
        for a, (w, x) in enumerate(((d, tokens), (c, grad))):
            s = t_dot(w.astype(BF16), x[b]).astype(BF16)
            k = 2 * a + b
            keep[k * NQ : (k + 1) * NQ, :] = s[:NQ]
            send[k * NQ : (k + 1) * NQ, :] = s[NQ:]


def pack_kernel(keep, got, out):
    i, j = rows_cols(8 * NQ, 4 * NQ)
    for s, x in enumerate((keep, got)):
        to = ones_where((j == (i & 3) * NQ + (i >> 3)) & (((i >> 2) & 1) == s))
        part = dot(to, x[...])
        total = part if s == 0 else total + part
    out[...] = total.astype(BF16)


def split_kernel(rows, slot_in, slot_grad):
    n, i = rows_cols(4 * NQ, 8 * NQ)
    for a, out in enumerate((slot_in, slot_grad)):
        src = (n & 63) * 8 + ((n >> 7) & 1) * 4 + a * 2 + ((n >> 6) & 1)
        out[...] = dot(ones_where(i == src), rows[...]).astype(BF16)


def both_halves(ids):
    t = ids[1]
    return (
        pl.ds(pl.multiple_of(t * H, 128), H),
        pl.ds(pl.multiple_of((1 - t) * H, 128), H),
    )


def up_kernel(ids, own, other, w_in, w_out, slope, out_keep, out_send):
    mine, theirs = both_halves(ids)
    x, y = own[...], other[...]
    keep = jnp.zeros((4 * NQ, H), F32)
    sent = jnp.zeros((4 * NQ, H), F32)
    for f in range(0, FH, CH):
        cols = slice(f, f + CH)
        v = dot(x, w_in[0, mine, cols]) + dot(y, w_in[0, theirs, cols])
        sq = v * v
        t = jnp.tanh(0.7978845608 * (v + 0.044715 * v * sq))
        act = (0.5 * v * (1.0 + t)).astype(BF16)
        slope[:, cols] = 0.5 * (1.0 + t) + 0.5 * v * (1.0 - t * t) * (
            0.7978845608 * (1.0 + 0.134145 * sq)
        )
        keep = keep + dot(act, w_out[0, cols, mine])
        sent = sent + dot(act, w_out[0, cols, theirs])
    out_keep[...] = keep
    out_send[...] = sent.astype(BF16)


def down_kernel(ids, own, other, slope, w_in, w_out, pre_grad, in_keep, in_send):
    mine, theirs = both_halves(ids)
    x, y = own[...], other[...]
    keep = jnp.zeros((4 * NQ, H), F32)
    sent = jnp.zeros((4 * NQ, H), F32)
    for f in range(0, FH, CH):
        cols = slice(f, f + CH)
        g = dot_t(x, w_out[0, cols, mine]) + dot_t(y, w_out[0, cols, theirs])
        g = (g * slope[:, cols]).astype(BF16)
        pre_grad[:, cols] = g
        keep = keep + dot_t(g, w_in[0, mine, cols])
        sent = sent + dot_t(g, w_in[0, theirs, cols])
    in_keep[...] = keep
    in_send[...] = sent.astype(BF16)


def weight_kernel(ids, own, other, pre_grad, out):
    for x, rows in zip((own, other), both_halves(ids)):
        out[0, rows, :] = t_dot(x[...], pre_grad[...]).astype(BF16)


def merge_kernel(out_keep, out_got, in_keep, in_got, out):
    i, n = rows_cols(8 * NQ, 4 * NQ)
    for a, (x, y) in enumerate(((out_keep, out_got), (in_keep, in_got))):
        r = (x[...] + y[...].astype(F32)).astype(BF16)
        src = ((i >> 2) & 1) * 128 + (i & 1) * 64 + (i >> 3)
        part = dot(ones_where((n == src) & (((i >> 1) & 1) == a)), r)
        total = part if a == 0 else total + part
    out[...] = total.astype(BF16)


def unpack_kernel(rows, own, send):
    n, i = rows_cols(4 * NQ, 8 * NQ)
    for s, out in enumerate((own, send)):
        src = (n & 63) * 8 + s * 4 + (n >> 6)
        out[...] = dot(ones_where(i == src), rows[...]).astype(BF16)


def slots_of(own, got, a, b):
    rows = slice((2 * a + b) * NQ, (2 * a + b + 1) * NQ)
    return jnp.concatenate([own[rows, :], got[rows, :]], axis=0)


def dots_kernel(own, got, tokens, grad, part, send):
    for a, x in enumerate((grad, tokens)):
        for b in range(B):
            p = dot_t(x[b], slots_of(own, got, a, b))
            rows = slice((2 * a + b) * M, (2 * a + b + 1) * M)
            part[rows, :] = p
            send[rows, :] = p.astype(BF16)


def first_kernel(own, got, dispatch, out):
    for b in range(B):
        w = dispatch[b * M : (b + 1) * M, :].astype(BF16)
        out[b] = dot(w, slots_of(own, got, 1, b))


def logit_kernel(ids, part, got, dispatch, combine, tokens, logit, keep, send, whole):
    back = expert_order(ids[0])
    total = jnp.zeros((E, H), F32)
    for b in range(B):
        rows = slice(b * M, (b + 1) * M)
        c, d = combine[rows, :], dispatch[rows, :]
        x = part[rows, :] + got[rows, :].astype(F32)
        low = slice((B + b) * M, (B + b + 1) * M)
        y = part[low, :] + got[low, :].astype(F32)
        g = c * (x - jnp.sum(c * x, axis=1, keepdims=True))
        g = (g + d * (y - jnp.sum(d * y, axis=0, keepdims=True))).astype(BF16)
        logit[rows, :] = g
        plain = dot_t(g, back).astype(BF16)
        total = total + t_dot(plain, tokens[b])
    whole[...] = jnp.transpose(total)
    c = ids[0]
    n = H // 2
    keep[...] = whole[pl.ds(pl.multiple_of(c * n, 8), n), :]
    send[...] = whole[pl.ds(pl.multiple_of((1 - c) * n, 8), n), :]


def tokens_kernel(first, logit, router, out):
    for b in range(B):
        g = first[b] + dot_t(logit[b * M : (b + 1) * M, :], router[...])
        out[b] = g.astype(BF16)


def add_kernel(x, y, out):
    out[...] = x[...] + y[...]


def spread_kernel(x, out):
    total = x[0]
    for i in range(1, 8):
        total = total + x[i]
    for i in range(8):
        out[i] = total


def join_kernel(ids, half, other, out):
    c = ids[0]
    n = H // 2
    out[pl.ds(pl.multiple_of(c * n, 8), n), :] = half[...]
    out[pl.ds(pl.multiple_of((1 - c) * n, 8), n), :] = other[...]


def swap(x, axis):
    return lax.ppermute(x, axis, [(0, 1), (1, 0)])


def exchange(x, axes):
    return lax.all_to_all(x, axes, split_axis=0, concat_axis=0, tiled=True)


def on_device(tokens, router, w_in, w_out, grad_out):
    ids = jnp.stack([lax.axis_index("core"), lax.axis_index("tp")]).astype(I32)
    part, ordered = call(
        logits_kernel, [((B * M, E), F32), ((H, E), BF16)], 2 * 512 * H * E, 1e6
    )(ids, tokens, router)
    other = swap(part, "tp")
    half = ((4 * NQ, H), BF16)
    half32 = ((4 * NQ, H), F32)
    dispatch, combine, keep, send = call(
        slots_kernel, [((B * M, E), F32)] * 2 + [half] * 2, 4 * 512 * H * E, 3e6
    )(part, other, tokens, grad_out)
    got = swap(send, "core")
    (packed,) = call(pack_kernel, [((8 * NQ, H), BF16)], 3e8, 1.3e6)(keep, got)
    rows = exchange(packed.reshape(NQ, 8, H), CHIPS).reshape(8 * NQ, H)
    in_own, grad_own = call(split_kernel, [half] * 2, 3e8, 1.3e6)(rows)
    in_other = swap(in_own, "tp")
    grad_other = swap(grad_own, "tp")
    slope, out_keep, out_send = call(
        up_kernel, [((4 * NQ, FH), F32), half32, half], 1.7e9, 1e7
    )(ids, in_own, in_other, w_in, w_out)
    out_got = swap(out_send, "tp")
    pre_grad, in_keep, in_send = call(
        down_kernel, [((4 * NQ, FH), BF16), half32, half], 1.7e9, 1e7
    )(ids, grad_own, grad_other, slope, w_in, w_out)
    in_got = swap(in_send, "tp")
    (merged,) = call(merge_kernel, [((8 * NQ, H), BF16)], 3e8, 2.6e6)(
        out_keep, out_got, in_keep, in_got
    )
    rows = exchange(merged.reshape(NQ, 8, H), CHIPS).reshape(8 * NQ, H)
    (grad_weight,) = call(weight_kernel, [((1, D, FH), BF16)], 8.4e8, 5e6)(
        ids, in_own, in_other, pre_grad
    )
    own, send = call(unpack_kernel, [half] * 2, 3e8, 1.3e6)(rows)
    got = swap(send, "core")
    part, send = call(
        dots_kernel, [((2 * B * M, E), F32), ((2 * B * M, E), BF16)], 4 * 512 * H * E, 3e6
    )(own, got, tokens, grad_out)
    dots_got = swap(send, "tp")
    (first,) = call(first_kernel, [((B, M, H), F32)], 2 * 512 * H * E, 2e6)(own, got, dispatch)
    third = ((H // 2, E), F32)
    logit, keep, send = pl.pallas_call(
        logit_kernel,
        out_shape=[
            jax.ShapeDtypeStruct((B * M, E), BF16),
            jax.ShapeDtypeStruct(*third),
            jax.ShapeDtypeStruct(*third),
        ],
        in_specs=[SMEM] + [VMEM] * 5,
        out_specs=[VMEM] * 3,
        scratch_shapes=[pltpu.VMEM((H, E), F32)],
        cost_estimate=pl.CostEstimate(
            flops=2 * 512 * H * E, bytes_accessed=3000000, transcendentals=0
        ),
        compiler_params=pltpu.CompilerParams(vmem_limit_bytes=24 * MIB),
    )(ids, part, dots_got, dispatch, combine, tokens)
    got = swap(send, "core")
    (summed,) = call(add_kernel, [third], 1e5, 5e5)(keep, got)
    eight = ((8, H // 16, E), F32)
    summed = exchange(summed.reshape(eight[0]), ("x_hi", "y"))
    (summed,) = call(spread_kernel, [eight], 1e5, 5e5)(summed)
    summed = exchange(summed, "z")
    (summed,) = call(spread_kernel, [eight], 1e5, 5e5)(summed)
    summed = exchange(summed, ("x_hi", "y")).reshape(H // 2, E)
    (grad_tokens,) = call(tokens_kernel, [((B, M, H), BF16)], 2 * 512 * H * E, 3e6)(
        first, logit, ordered
    )
    (grad_router,) = call(join_kernel, [((H, E), F32)], 1e5, 7e5)(
        ids, summed, swap(summed, "core")
    )
    return grad_tokens, grad_router, grad_weight


def solution(mesh):
    fine = Mesh(mesh.devices.reshape(8, 2, 4, 2, 2), AXES)
    ep = ("z", "x_hi", "y", "core")
    return jax.shard_map(
        on_device,
        mesh=fine,
        in_specs=(
            P(ep, None, "tp"),
            P("tp", None),
            P(ep, None, "tp"),
            P(ep, "tp", None),
            P(ep, None, "tp"),
        ),
        out_specs=(P(ep, None, "tp"), P("tp", None), P(ep, None, "tp")),
        check_vma=False,
    )
```

time: 1430 us -> 168 us (0.12)
  waiting for transfers between devices: 1230 us -> 26.5 us
  matrix products: 38.6 us -> 0 us
  local copies, waits for them, and re-layouts: 36.2 us -> 6.27 us
  Pallas kernels: 0 us -> 20.3 us
  blocking collectives: 75.1 us -> 93.1 us
  other arithmetic: 15.7 us -> 0.08 us
    psum x3 -> x0, waiting for transfers between devices: 1210 us -> none  [the longest x1 1140 us: on_device(): grad_router = lax.psum(router_part, 'ep')]
    all_to_all x2 -> x5, blocking collectives: 54.4 us -> 93.1 us  [exchange(): return lax.all_to_all(x, axes, split_axis=0, concat_axis=0, tiled=True)]
    dot_general x13 -> x0, matrix products: 38.6 us -> none  [the longest x1 5.02 us: on_device(): jnp.einsum('bme,de->bmd', logit_b, router, preferred_element_type=jnp.flo...]
    ppermute x0 -> x10, waiting for transfers between devices: none -> 26.5 us  [swap(): return lax.ppermute(x, axis, [(0, 1), (1, 0)])]
    ppermute x0 -> x10, starting transfers between devices: none -> 21 us  [swap(): return lax.ppermute(x, axis, [(0, 1), (1, 0)])]
    all_gather x2 -> x0, blocking collectives: 20.7 us -> none  [the longest x1 10.5 us: on_device(): lax.all_gather(sent_grad, 'tp', axis=2, tiled=True)]
    pallas_call x0 -> x17, Pallas kernels: none -> 20.3 us  [the longest x16 19.1 us: run(): pl.pallas_call(kernel, out_shape=[jax.ShapeDtypeStruct(s, d) for s, d in...]
    all_to_all x2 -> x0, starting transfers between devices: 20.3 us -> none  [the longest x1 13.4 us: on_device(): lax.all_to_all(in_share.reshape(1, all_rows, -1), 'ep', split_axis=1, con...]
  transfers between devices with their start and end apart: 7 -> 10, of which waited for: 6 -> 8; matrix products, arithmetic and copies ran while one was open for 3% -> 0% of each run, Pallas kernels for 0% -> 8%
where the time goes in v2:
time: 168 us
  blocking collectives  93.1 us (55%)
  waiting for transfers between devices  26.5 us (16%)
  starting transfers between devices  21 us (12%)
  Pallas kernels  20.3 us (12%)
  local copies, waits for them, and re-layouts  6.27 us (4%)
    all_to_all x5, blocking collectives, exchange(): return lax.all_to_all(x, axes, split_axis=0, concat_axis=0, tiled=True)  93.1 us
    ppermute x10, waiting for transfers between devices, swap(): return lax.ppermute(x, axis, [(0, 1), (1, 0)])  26.5 us
    ppermute x10, starting transfers between devices, swap(): return lax.ppermute(x, axis, [(0, 1), (1, 0)])  21 us
    pallas_call x16, Pallas kernels, run(): pl.pallas_call(kernel, out_shape=[jax.ShapeDtypeStruct(s, d) for s, d in...  19.1 us
    unnamed x16, local copies, waits for them, and re-layouts  6.27 us
  transfers between devices with their start and end apart: 10, of which 8 were waited for; matrix products, arithmetic and copies ran while one was open for 0% of the time, Pallas kernels for 8%

profile of v2, /device:TPU:1, one launch (start us, length us, event | category | flops | bytes accessed | tf_op | source)
XLA Modules:
  0.0 168.0 jit_solution(9793616562008882763)
XLA Ops:
  0.6 0.0 copy-start
  0.6 0.1 pad_add_fusion.ids
  0.7 0.0 copy-start.2
  0.7 1.2 copy-done.2
  2.0 0.0 copy-start.7
  2.0 0.9 copy-done.7
  2.9 1.0 shard_map.76
  3.9 2.1 %collective-permute-start = (f32[512,128]{1,0:T(8,128)S(1)}, f32[512,128]{1,0:T(8,128)S(1)}, u32[]{:S(2)}, u32[]{:S(2)}) collective-permute-start(f32[512,128]{1,0:T(8,128)S(1)} %get-tuple-element.24.part), channel_id=1, source_target_pairs={{0,1},{1,0},{2,3},{3,2},{4,5},{5,4},{6,7},{7,6},{8,9},{9,8},{10,11... | collective-permute-start | bytes 786440 | tf_op jit(solution)/shard_map/ppermute | solution.py:244
  6.0 4.7 %collective-permute-done.other = f32[512,128]{1,0:T(8,128)S(1)} collective-permute-done((f32[512,128]{1,0:T(8,128)S(1)}, f32[512,128]{1,0:T(8,128)S(1)}, u32[]{:S(2)}, u32[]{:S(2)}) %collective-permute-start) | collective-permute-done | bytes 262176 | tf_op jit(solution)/shard_map/ppermute | solution.py:244
  10.7 0.0 copy-start.3
  10.7 1.1 copy-done.3
  11.8 0.0 copy-start.5
  11.8 1.1 copy-done.5
  12.9 0.7 shard_map.77
  13.6 3.0 %collective-permute-start.1 = (bf16[256,640]{1,0:T(8,128)(2,1)S(1)}, bf16[256,640]{1,0:T(8,128)(2,1)S(1)}, u32[]{:S(2)}, u32[]{:S(2)}) collective-permute-start(bf16[256,640]{1,0:T(8,128)(2,1)S(1)} %get-tuple-element.26), channel_id=1, source_target_pairs={{0,2},{2,0},{1,3},{3,1},{4,6},{6,4},{5,7},{7,5},{8,10},{10,8},{9,1... | collective-permute-start | bytes 983048 | tf_op jit(solution)/shard_map/ppermute | solution.py:244
  16.6 1.3 collective-permute-done.1.got
  17.8 0.6 shard_map.78
  18.4 32.7 %all_to_all.25 = bf16[64,8,640]{2,1,0:T(8,128)(2,1)S(1)} all-to-all(bf16[64,8,640]{2,1,0:T(8,128)(2,1)S(1)} %bitcast.9), channel_id=1, replica_groups=mesh['z'=8,'x_hi'=2,'y'=4,'core'=2,'tp'=2] {'z','x_hi','y'}, dimensions={0} | all-to-all | bytes 1310720 | tf_op jit(solution)/shard_map/all_to_all | solution.py:248
  51.1 0.6 shard_map.79
  51.7 0.4 collective-permute-start.2
  52.1 1.2 collective-permute-start.4
  53.3 4.5 %collective-permute-done.2.other = bf16[256,640]{1,0:T(8,128)(2,1)S(1)} collective-permute-done((bf16[256,640]{1,0:T(8,128)(2,1)S(1)}, bf16[256,640]{1,0:T(8,128)(2,1)S(1)}, u32[]{:S(2)}, u32[]{:S(2)}) %collective-permute-start.2) | collective-permute-done | bytes 327712 | tf_op jit(solution)/shard_map/ppermute | solution.py:244
  57.7 0.0 copy-done
  57.7 0.0 copy-start.1
  57.7 1.9 %copy-done.1 = bf16[1,1280,1280]{2,1,0:T(8,128)(2,1)S(1)} copy-done((bf16[1,1280,1280]{2,1,0:T(8,128)(2,1)S(1)}, bf16[1,1280,1280]{2,1,0:T(8,128)(2,1)}, u32[]{:S(2)}) %copy-start.1) | copy-done | bytes 3276824
  59.6 4.4 %shard_map.80 = (f32[256,1280]{1,0:T(8,128)S(1)}, f32[256,640]{1,0:T(8,128)S(1)}, bf16[256,640]{1,0:T(8,128)(2,1)S(1)}) custom-call(s32[2]{0:T(128)S(1)} %pad_add_fusion.ids, bf16[256,640]{1,0:T(8,128)(2,1)S(1)} %get-tuple-element.27.own, bf16[256,640]{1,0:T(8,128)(2,1)S(1)} %collective-permute-done.2.other, bf16[1,1280,1280]{2,1,0:T(8,128)(2,1)S(1)} %copy-done, ...), custom_call_target="tpu_custom_call" | custom-call | flops 1700000000 | bytes 10000000 | tf_op jit(solution)/shard_map/pallas_call | solution.py:57
  64.0 0.4 collective-permute-start.3
  64.4 0.0 collective-permute-done.4.other
  64.4 3.9 %shard_map.81 = (bf16[256,1280]{1,0:T(8,128)(2,1)S(1)}, f32[256,640]{1,0:T(8,128)S(1)}, bf16[256,640]{1,0:T(8,128)(2,1)S(1)}) custom-call(s32[2]{0:T(128)S(1)} %pad_add_fusion.ids, bf16[256,640]{1,0:T(8,128)(2,1)S(1)} %get-tuple-element.30.own, bf16[256,640]{1,0:T(8,128)(2,1)S(1)} %collective-permute-done.4.other, f32[256,1280]{1,0:T(8,128)S(1)} %get-tuple-element.31.slope, ...), custom_call_target="tpu_custom_call" | custom-call | flops 1700000000 | bytes 10000000 | tf_op jit(solution)/shard_map/pallas_call | solution.py:57
  68.3 0.0 copy-start.4
  68.3 0.0 copy-start.6
  68.3 1.3 collective-permute-start.5
  69.6 2.2 %collective-permute-done.3.out_got = bf16[256,640]{1,0:T(8,128)(2,1)S(1)} collective-permute-done((bf16[256,640]{1,0:T(8,128)(2,1)S(1)}, bf16[256,640]{1,0:T(8,128)(2,1)S(1)}, u32[]{:S(2)}, u32[]{:S(2)}) %collective-permute-start.3) | collective-permute-done | bytes 327712 | tf_op jit(solution)/shard_map/ppermute | solution.py:244
  71.8 4.3 %collective-permute-done.5.in_got = bf16[256,640]{1,0:T(8,128)(2,1)S(1)} collective-permute-done((bf16[256,640]{1,0:T(8,128)(2,1)S(1)}, bf16[256,640]{1,0:T(8,128)(2,1)S(1)}, u32[]{:S(2)}, u32[]{:S(2)}) %collective-permute-start.5) | collective-permute-done | bytes 327712 | tf_op jit(solution)/shard_map/ppermute | solution.py:244
  76.1 0.7 shard_map.82
  76.8 28.7 %all_to_all.26 = bf16[64,8,640]{2,1,0:T(8,128)(2,1)S(1)} all-to-all(bf16[64,8,640]{2,1,0:T(8,128)(2,1)S(1)} %bitcast.8), channel_id=1, replica_groups=mesh['z'=8,'x_hi'=2,'y'=4,'core'=2,'tp'=2] {'z','x_hi','y'}, dimensions={0} | all-to-all | bytes 1310720 | tf_op jit(solution)/shard_map/all_to_all | solution.py:248
  105.4 0.6 shard_map.83
  106.0 7.1 %collective-permute-start.6 = (bf16[256,640]{1,0:T(8,128)(2,1)S(1)}, bf16[256,640]{1,0:T(8,128)(2,1)S(1)}, u32[]{:S(2)}, u32[]{:S(2)}) collective-permute-start(bf16[256,640]{1,0:T(8,128)(2,1)S(1)} %get-tuple-element.35), channel_id=1, source_target_pairs={{0,2},{2,0},{1,3},{3,1},{4,6},{6,4},{5,7},{7,5},{8,10},{10,8},{9,1... | collective-permute-start | bytes 983048 | tf_op jit(solution)/shard_map/ppermute | solution.py:244
  113.2 1.3 collective-permute-done.6.got
  114.4 0.0 copy-done.4
  114.4 0.0 copy-done.6
  114.4 0.5 shard_map.85
  114.9 0.3 collective-permute-start.7
  115.2 7.3 %collective-permute-done.7.got = bf16[1024,128]{1,0:T(8,128)(2,1)S(1)} collective-permute-done((bf16[1024,128]{1,0:T(8,128)(2,1)S(1)}, bf16[1024,128]{1,0:T(8,128)(2,1)S(1)}, u32[]{:S(2)}, u32[]{:S(2)}) %collective-permute-start.7) | collective-permute-done | bytes 262176 | tf_op jit(solution)/shard_map/ppermute | solution.py:244
  122.5 1.2 shard_map.86
  123.7 1.3 collective-permute-start.8
  125.0 1.0 collective-permute-done.8.y
  126.1 11.3 %all_to_all.27.x = f32[8,40,128]{2,1,0:T(8,128)S(1)} all-to-all(f32[8,40,128]{2,1,0:T(8,128)S(1)} %bitcast.14), channel_id=1, replica_groups=mesh['z'=8,'x_hi'=2,'y'=4,'core'=2,'tp'=2] {'x_hi','y'}, dimensions={0} | all-to-all | bytes 327680 | tf_op jit(solution)/shard_map/all_to_all | solution.py:248
  137.4 10.7 %all_to_all.28.x = f32[8,40,128]{2,1,0:T(8,128)S(1)} all-to-all(f32[8,40,128]{2,1,0:T(8,128)S(1)} %shard_map.89), channel_id=1, replica_groups=mesh['z'=8,'x_hi'=2,'y'=4,'core'=2,'tp'=2] {'z'}, dimensions={0} | all-to-all | bytes 327680 | tf_op jit(solution)/shard_map/all_to_all | solution.py:248
  148.2 9.7 %all_to_all.29 = f32[8,40,128]{2,1,0:T(8,128)S(1)} all-to-all(f32[8,40,128]{2,1,0:T(8,128)S(1)} %shard_map.90), channel_id=1, replica_groups=mesh['z'=8,'x_hi'=2,'y'=4,'core'=2,'tp'=2] {'x_hi','y'}, dimensions={0} | all-to-all | bytes 327680 | tf_op jit(solution)/shard_map/all_to_all | solution.py:248
  157.9 4.0 %collective-permute-start.9 = (f32[320,128]{1,0:T(8,128)S(1)}, f32[320,128]{1,0:T(8,128)S(1)}, u32[]{:S(2)}, u32[]{:S(2)}) collective-permute-start(f32[320,128]{1,0:T(8,128)S(1)} %bitcast.12), channel_id=1, source_target_pairs={{0,2},{2,0},{1,3},{3,1},{4,6},{6,4},{5,7},{7,5},{8,10},{10,8},{9,1... | collective-permute-start | bytes 491528 | tf_op jit(solution)/shard_map/ppermute | solution.py:244
  161.9 3.4 %shard_map.92 = bf16[1,1280,1280]{2,1,0:T(8,128)(2,1)} custom-call(s32[2]{0:T(128)S(1)} %pad_add_fusion.ids, bf16[256,640]{1,0:T(8,128)(2,1)S(1)} %get-tuple-element.27.own, bf16[256,640]{1,0:T(8,128)(2,1)S(1)} %collective-permute-done.2.other, bf16[256,1280]{1,0:T(8,128)(2,1)S(1)} %get-tuple-element.44.pre_grad), custom_call_target="tpu_custom_call" | custom-call | flops 840000000 | bytes 5000000 | tf_op jit(solution)/shard_map/pallas_call | solution.py:57
  165.2 0.3 shard_map.84.first
  165.5 1.2 shard_map.87
  166.7 0.0 collective-permute-done.9.other
  166.7 1.3 shard_map.91
  (3 shorter events, 0.1 us)
Async XLA Ops:
  0.6 57.1 %copy-start = (bf16[1,1280,1280]{2,1,0:T(8,128)(2,1)S(1)}, bf16[1,1280,1280]{2,1,0:T(8,128)(2,1)}, u32[]{:S(2)}) copy-start(bf16[1,1280,1280]{2,1,0:T(8,128)(2,1)} %w_in.3) | copy-start | bytes 9830404
  0.7 1.2 copy-start.2
  2.0 0.9 copy-start.7
  3.9 6.8 %collective-permute-start = (f32[512,128]{1,0:T(8,128)S(1)}, f32[512,128]{1,0:T(8,128)S(1)}, u32[]{:S(2)}, u32[]{:S(2)}) collective-permute-start(f32[512,128]{1,0:T(8,128)S(1)} %get-tuple-element.24.part), channel_id=1, source_target_pairs={{0,1},{1,0},{2,3},{3,2},{4,5},{5,4},{6,7},{7,6},{8,9},{9,8},{10,11... | collective-permute-start | bytes 786440 | tf_op jit(solution)/shard_map/ppermute | solution.py:244
  10.7 1.1 copy-start.3
  11.8 1.1 copy-start.5
  13.6 4.2 %collective-permute-start.1 = (bf16[256,640]{1,0:T(8,128)(2,1)S(1)}, bf16[256,640]{1,0:T(8,128)(2,1)S(1)}, u32[]{:S(2)}, u32[]{:S(2)}) collective-permute-start(bf16[256,640]{1,0:T(8,128)(2,1)S(1)} %get-tuple-element.26), channel_id=1, source_target_pairs={{0,2},{2,0},{1,3},{3,1},{4,6},{6,4},{5,7},{7,5},{8,10},{10,8},{9,1... | collective-permute-start | bytes 983048 | tf_op jit(solution)/shard_map/ppermute | solution.py:244
  51.7 6.0 %collective-permute-start.2 = (bf16[256,640]{1,0:T(8,128)(2,1)S(1)}, bf16[256,640]{1,0:T(8,128)(2,1)S(1)}, u32[]{:S(2)}, u32[]{:S(2)}) collective-permute-start(bf16[256,640]{1,0:T(8,128)(2,1)S(1)} %get-tuple-element.27.own), channel_id=1, source_target_pairs={{0,1},{1,0},{2,3},{3,2},{4,5},{5,4},{6,7},{7,6},{8,9},{9,8},{10,11... | collective-permute-start | bytes 983048 | tf_op jit(solution)/shard_map/ppermute | solution.py:244
  52.1 12.3 %collective-permute-start.4 = (bf16[256,640]{1,0:T(8,128)(2,1)S(1)}, bf16[256,640]{1,0:T(8,128)(2,1)S(1)}, u32[]{:S(2)}, u32[]{:S(2)}) collective-permute-start(bf16[256,640]{1,0:T(8,128)(2,1)S(1)} %get-tuple-element.30.own), channel_id=1, source_target_pairs={{0,1},{1,0},{2,3},{3,2},{4,5},{5,4},{6,7},{7,6},{8,9},{9,8},{10,11... | collective-permute-start | bytes 983048 | tf_op jit(solution)/shard_map/ppermute | solution.py:244
  57.7 1.9 %copy-start.1 = (bf16[1,1280,1280]{2,1,0:T(8,128)(2,1)S(1)}, bf16[1,1280,1280]{2,1,0:T(8,128)(2,1)}, u32[]{:S(2)}) copy-start(bf16[1,1280,1280]{2,1,0:T(8,128)(2,1)} %w_out.3) | copy-start | bytes 9830404
  64.0 7.7 %collective-permute-start.3 = (bf16[256,640]{1,0:T(8,128)(2,1)S(1)}, bf16[256,640]{1,0:T(8,128)(2,1)S(1)}, u32[]{:S(2)}, u32[]{:S(2)}) collective-permute-start(bf16[256,640]{1,0:T(8,128)(2,1)S(1)} %get-tuple-element.29), channel_id=1, source_target_pairs={{0,1},{1,0},{2,3},{3,2},{4,5},{5,4},{6,7},{7,6},{8,9},{9,8},{10,11... | collective-permute-start | bytes 983048 | tf_op jit(solution)/shard_map/ppermute | solution.py:244
  68.3 46.1 %copy-start.4 = (bf16[2,256,640]{2,1,0:T(8,128)(2,1)S(1)}, bf16[2,256,640]{2,1,0:T(8,128)(2,1)}, u32[]{:S(2)}) copy-start(bf16[2,256,640]{2,1,0:T(8,128)(2,1)} %tokens.7) | copy-start | bytes 1966084
  68.3 46.1 %copy-start.6 = (bf16[2,256,640]{2,1,0:T(8,128)(2,1)S(1)}, bf16[2,256,640]{2,1,0:T(8,128)(2,1)}, u32[]{:S(2)}) copy-start(bf16[2,256,640]{2,1,0:T(8,128)(2,1)} %grad.3) | copy-start | bytes 1966084
  68.3 7.8 %collective-permute-start.5 = (bf16[256,640]{1,0:T(8,128)(2,1)S(1)}, bf16[256,640]{1,0:T(8,128)(2,1)S(1)}, u32[]{:S(2)}, u32[]{:S(2)}) collective-permute-start(bf16[256,640]{1,0:T(8,128)(2,1)S(1)} %get-tuple-element.33), channel_id=1, source_target_pairs={{0,1},{1,0},{2,3},{3,2},{4,5},{5,4},{6,7},{7,6},{8,9},{9,8},{10,11... | collective-permute-start | bytes 983048 | tf_op jit(solution)/shard_map/ppermute | solution.py:244
  106.0 8.4 %collective-permute-start.6 = (bf16[256,640]{1,0:T(8,128)(2,1)S(1)}, bf16[256,640]{1,0:T(8,128)(2,1)S(1)}, u32[]{:S(2)}, u32[]{:S(2)}) collective-permute-start(bf16[256,640]{1,0:T(8,128)(2,1)S(1)} %get-tuple-element.35), channel_id=1, source_target_pairs={{0,2},{2,0},{1,3},{3,1},{4,6},{6,4},{5,7},{7,5},{8,10},{10,8},{9,1... | collective-permute-start | bytes 983048 | tf_op jit(solution)/shard_map/ppermute | solution.py:244
  114.9 7.6 %collective-permute-start.7 = (bf16[1024,128]{1,0:T(8,128)(2,1)S(1)}, bf16[1024,128]{1,0:T(8,128)(2,1)S(1)}, u32[]{:S(2)}, u32[]{:S(2)}) collective-permute-start(bf16[1024,128]{1,0:T(8,128)(2,1)S(1)} %get-tuple-element.38), channel_id=1, source_target_pairs={{0,1},{1,0},{2,3},{3,2},{4,5},{5,4},{6,7},{7,6},{8,9},{9,8},{10,11... | collective-permute-start | bytes 786440 | tf_op jit(solution)/shard_map/ppermute | solution.py:244
  123.7 2.3 %collective-permute-start.8 = (f32[320,128]{1,0:T(8,128)S(1)}, f32[320,128]{1,0:T(8,128)S(1)}, u32[]{:S(2)}, u32[]{:S(2)}) collective-permute-start(f32[320,128]{1,0:T(8,128)S(1)} %get-tuple-element.43), channel_id=1, source_target_pairs={{0,2},{2,0},{1,3},{3,1},{4,6},{6,4},{5,7},{7,5},{8,10},{10,8},{9,1... | collective-permute-start | bytes 491528 | tf_op jit(solution)/shard_map/ppermute | solution.py:244
  157.9 8.8 %collective-permute-start.9 = (f32[320,128]{1,0:T(8,128)S(1)}, f32[320,128]{1,0:T(8,128)S(1)}, u32[]{:S(2)}, u32[]{:S(2)}) collective-permute-start(f32[320,128]{1,0:T(8,128)S(1)} %bitcast.12), channel_id=1, source_target_pairs={{0,2},{2,0},{1,3},{3,1},{4,6},{6,4},{5,7},{7,5},{8,10},{10,8},{9,1... | collective-permute-start | bytes 491528 | tf_op jit(solution)/shard_map/ppermute | solution.py:244

commit v3 on v2

--- a/solution.py
+++ b/solution.py
@@ -22,6 +22,7 @@
 
 SMEM = pl.BlockSpec(memory_space=pltpu.SMEM)
 VMEM = pl.BlockSpec(memory_space=pltpu.VMEM)
+HBM = pl.BlockSpec(memory_space=pltpu.HBM)
 
 
 def dot(a, b):
@@ -52,27 +53,53 @@
     return ones_where(e == 2 * (p & 63) + (core ^ (p >> 6)))
 
 
-def call(kernel, outs, flops, nbytes, limit=None):
+def call(kernel, outs, flops, nbytes, hbm=(), scratch=(), limit=24):
     def run(*args):
+        args = [
+            pltpu.with_memory_space_constraint(a, pltpu.HBM) if i in hbm else a
+            for i, a in enumerate(args)
+        ]
         return pl.pallas_call(
             kernel,
             out_shape=[jax.ShapeDtypeStruct(s, d) for s, d in outs],
-            in_specs=[SMEM if a.dtype == I32 else VMEM for a in args],
+            in_specs=[
+                SMEM if a.dtype == I32 else HBM if i in hbm else VMEM for i, a in enumerate(args)
+            ],
             out_specs=[VMEM for _ in outs],
+            scratch_shapes=list(scratch),
             cost_estimate=pl.CostEstimate(
                 flops=int(flops), bytes_accessed=int(nbytes), transcendentals=0
             ),
-            compiler_params=pltpu.CompilerParams(vmem_limit_bytes=(limit or 24) * MIB),
+            compiler_params=pltpu.CompilerParams(vmem_limit_bytes=limit * MIB),
         )(*args)
 
     return run
 
 
-def logits_kernel(ids, tokens, router, part, ordered):
-    r = dot(router[...], expert_order(ids[0])).astype(BF16)
+def logits_kernel(ids, tokens_hbm, router_hbm, part, ordered, tokens, router, sems):
+    copies = [
+        pltpu.make_async_copy(tokens_hbm, tokens, sems.at[0]),
+        pltpu.make_async_copy(router_hbm, router, sems.at[1]),
+    ]
+    for c in copies:
+        c.start()
+    order = expert_order(ids[0])
+    copies[1].wait()
+    r = dot(router[...], order).astype(BF16)
     ordered[...] = r
+    copies[0].wait()
     for b in range(B):
         part[b * M : (b + 1) * M, :] = dot(tokens[b], r)
+
+
+def fetch_kernel(*refs):
+    n = len(refs) // 2
+    sems = refs[-1]
+    copies = [pltpu.make_async_copy(refs[i], refs[n + i], sems.at[i]) for i in range(n)]
+    for c in copies:
+        c.start()
+    for c in copies:
+        c.wait()
 
 
 def slots_kernel(part, other, tokens, grad, dispatch, combine, keep, send):
@@ -152,12 +179,13 @@
     in_send[...] = sent.astype(BF16)
 
 
-def weight_kernel(ids, own, other, pre_grad, out):
+def weight_kernel(ids, own, other, pre_grad, out, done):
     for x, rows in zip((own, other), both_halves(ids)):
         out[0, rows, :] = t_dot(x[...], pre_grad[...]).astype(BF16)
-
-
-def merge_kernel(out_keep, out_got, in_keep, in_got, out):
+    done[...] = jnp.zeros(done.shape, F32)
+
+
+def merge_kernel(out_keep, out_got, in_keep, in_got, done, out):
     i, n = rows_cols(8 * NQ, 4 * NQ)
     for a, (x, y) in enumerate(((out_keep, out_got), (in_keep, in_got))):
         r = (x[...] + y[...].astype(F32)).astype(BF16)
@@ -179,49 +207,46 @@
     return jnp.concatenate([own[rows, :], got[rows, :]], axis=0)
 
 
-def dots_kernel(own, got, tokens, grad, part, send):
-    for a, x in enumerate((grad, tokens)):
-        for b in range(B):
-            p = dot_t(x[b], slots_of(own, got, a, b))
-            rows = slice((2 * a + b) * M, (2 * a + b + 1) * M)
-            part[rows, :] = p
-            send[rows, :] = p.astype(BF16)
-
-
-def first_kernel(own, got, dispatch, out):
+def dots_kernel(own, got, tokens, grad, dispatch, combine, part, send):
+    for b in range(B):
+        rows = slice(b * M, (b + 1) * M)
+        c, d = combine[rows, :], dispatch[rows, :]
+        x = dot_t(grad[b], slots_of(own, got, 0, b))
+        y = dot_t(tokens[b], slots_of(own, got, 1, b))
+        g = c * (x - jnp.sum(c * x, axis=1, keepdims=True))
+        g = g + d * (y - jnp.sum(d * y, axis=0, keepdims=True))
+        part[rows, :] = g
+        send[rows, :] = g.astype(BF16)
+
+
+def first_kernel(own, got, dispatch, out, done):
     for b in range(B):
         w = dispatch[b * M : (b + 1) * M, :].astype(BF16)
         out[b] = dot(w, slots_of(own, got, 1, b))
-
-
-def logit_kernel(ids, part, got, dispatch, combine, tokens, logit, keep, send, whole):
-    back = expert_order(ids[0])
-    total = jnp.zeros((E, H), F32)
-    for b in range(B):
-        rows = slice(b * M, (b + 1) * M)
-        c, d = combine[rows, :], dispatch[rows, :]
-        x = part[rows, :] + got[rows, :].astype(F32)
-        low = slice((B + b) * M, (B + b + 1) * M)
-        y = part[low, :] + got[low, :].astype(F32)
-        g = c * (x - jnp.sum(c * x, axis=1, keepdims=True))
-        g = (g + d * (y - jnp.sum(d * y, axis=0, keepdims=True))).astype(BF16)
-        logit[rows, :] = g
-        plain = dot_t(g, back).astype(BF16)
-        total = total + t_dot(plain, tokens[b])
+    done[...] = jnp.zeros(done.shape, F32)
+
+
+def logit_kernel(ids, part, got, tokens, done, logit, keep, send, whole):
+    g = (part[...] + got[...].astype(F32)).astype(BF16)
+    logit[...] = g
+    plain = dot_t(g, expert_order(ids[0])).astype(BF16)
+    total = t_dot(plain[:M], tokens[0]) + t_dot(plain[M:], tokens[1])
     whole[...] = jnp.transpose(total)
     c = ids[0]
-    n = H // 2
-    keep[...] = whole[pl.ds(pl.multiple_of(c * n, 8), n), :]
-    send[...] = whole[pl.ds(pl.multiple_of((1 - c) * n, 8), n), :]
-
-
-def tokens_kernel(first, logit, router, out):
+    n = H // 16
+    for i in range(8):
+        keep[i] = whole[pl.ds(pl.multiple_of((2 * i + c) * n, 8), n), :]
+        send[i] = whole[pl.ds(pl.multiple_of((2 * i + 1 - c) * n, 8), n), :]
+
+
+def tokens_kernel(first, logit, router, out, done):
     for b in range(B):
         g = first[b] + dot_t(logit[b * M : (b + 1) * M, :], router[...])
         out[b] = g.astype(BF16)
-
-
-def add_kernel(x, y, out):
+    done[...] = jnp.zeros(done.shape, F32)
+
+
+def add_kernel(x, y, done, out):
     out[...] = x[...] + y[...]
 
 
@@ -229,15 +254,8 @@
     total = x[0]
     for i in range(1, 8):
         total = total + x[i]
-    for i in range(8):
+    for i in range(out.shape[0]):
         out[i] = total
-
-
-def join_kernel(ids, half, other, out):
-    c = ids[0]
-    n = H // 2
-    out[pl.ds(pl.multiple_of(c * n, 8), n), :] = half[...]
-    out[pl.ds(pl.multiple_of((1 - c) * n, 8), n), :] = other[...]
 
 
 def swap(x, axis):
@@ -250,14 +268,29 @@
 
 def on_device(tokens, router, w_in, w_out, grad_out):
     ids = jnp.stack([lax.axis_index("core"), lax.axis_index("tp")]).astype(I32)
-    part, ordered = call(
-        logits_kernel, [((B * M, E), F32), ((H, E), BF16)], 2 * 512 * H * E, 1e6
+    half = ((4 * NQ, H), BF16)
+    half32 = ((4 * NQ, H), F32)
+    done = ((8, E), F32)
+    small = 2 * B * M * H * E
+    part, ordered, tokens = call(
+        logits_kernel,
+        [((B * M, E), F32), ((H, E), BF16), ((B, M, H), BF16)],
+        small,
+        1e6,
+        hbm=(1, 2),
+        scratch=[pltpu.VMEM((H, E), BF16), pltpu.SemaphoreType.DMA((2,))],
     )(ids, tokens, router)
     other = swap(part, "tp")
-    half = ((4 * NQ, H), BF16)
-    half32 = ((4 * NQ, H), F32)
+    grad_out, w_in, w_out = call(
+        fetch_kernel,
+        [((B, M, H), BF16), ((1, D, FH), BF16), ((1, FH, D), BF16)],
+        0,
+        1.4e7,
+        hbm=(0, 1, 2),
+        scratch=[pltpu.SemaphoreType.DMA((3,))],
+    )(grad_out, w_in, w_out)
     dispatch, combine, keep, send = call(
-        slots_kernel, [((B * M, E), F32)] * 2 + [half] * 2, 4 * 512 * H * E, 3e6
+        slots_kernel, [((B * M, E), F32)] * 2 + [half] * 2, 2 * small, 3e6
     )(part, other, tokens, grad_out)
     got = swap(send, "core")
     (packed,) = call(pack_kernel, [((8 * NQ, H), BF16)], 3e8, 1.3e6)(keep, got)
@@ -273,50 +306,40 @@
         down_kernel, [((4 * NQ, FH), BF16), half32, half], 1.7e9, 1e7
     )(ids, grad_own, grad_other, slope, w_in, w_out)
     in_got = swap(in_send, "tp")
+    grad_weight, weight_done = call(weight_kernel, [((1, D, FH), BF16), done], 8.4e8, 5e6)(
+        ids, in_own, in_other, pre_grad
+    )
     (merged,) = call(merge_kernel, [((8 * NQ, H), BF16)], 3e8, 2.6e6)(
-        out_keep, out_got, in_keep, in_got
+        out_keep, out_got, in_keep, in_got, weight_done
     )
     rows = exchange(merged.reshape(NQ, 8, H), CHIPS).reshape(8 * NQ, H)
-    (grad_weight,) = call(weight_kernel, [((1, D, FH), BF16)], 8.4e8, 5e6)(
-        ids, in_own, in_other, pre_grad
-    )
     own, send = call(unpack_kernel, [half] * 2, 3e8, 1.3e6)(rows)
     got = swap(send, "core")
     part, send = call(
-        dots_kernel, [((2 * B * M, E), F32), ((2 * B * M, E), BF16)], 4 * 512 * H * E, 3e6
-    )(own, got, tokens, grad_out)
-    dots_got = swap(send, "tp")
-    (first,) = call(first_kernel, [((B, M, H), F32)], 2 * 512 * H * E, 2e6)(own, got, dispatch)
-    third = ((H // 2, E), F32)
-    logit, keep, send = pl.pallas_call(
+        dots_kernel, [((B * M, E), F32), ((B * M, E), BF16)], 2 * small, 3e6
+    )(own, got, tokens, grad_out, dispatch, combine)
+    logit_got = swap(send, "tp")
+    first, first_done = call(first_kernel, [((B, M, H), F32), done], small, 2e6)(
+        own, got, dispatch
+    )
+    eight = ((8, H // 16, E), F32)
+    logit, keep, send = call(
         logit_kernel,
-        out_shape=[
-            jax.ShapeDtypeStruct((B * M, E), BF16),
-            jax.ShapeDtypeStruct(*third),
-            jax.ShapeDtypeStruct(*third),
-        ],
-        in_specs=[SMEM] + [VMEM] * 5,
-        out_specs=[VMEM] * 3,
-        scratch_shapes=[pltpu.VMEM((H, E), F32)],
-        cost_estimate=pl.CostEstimate(
-            flops=2 * 512 * H * E, bytes_accessed=3000000, transcendentals=0
-        ),
-        compiler_params=pltpu.CompilerParams(vmem_limit_bytes=24 * MIB),
-    )(ids, part, dots_got, dispatch, combine, tokens)
+        [((B * M, E), BF16), eight, eight],
+        small,
+        3e6,
+        scratch=[pltpu.VMEM((H, E), F32)],
+    )(ids, part, logit_got, tokens, first_done)
     got = swap(send, "core")
-    (summed,) = call(add_kernel, [third], 1e5, 5e5)(keep, got)
-    eight = ((8, H // 16, E), F32)
-    summed = exchange(summed.reshape(eight[0]), ("x_hi", "y"))
+    grad_tokens, tokens_done = call(
+        tokens_kernel, [((B, M, H), BF16), done], small, 3e6
+    )(first, logit, ordered)
+    (summed,) = call(add_kernel, [eight], 1e5, 5e5)(keep, got, tokens_done)
+    summed = exchange(summed, ("x_hi", "y"))
     (summed,) = call(spread_kernel, [eight], 1e5, 5e5)(summed)
     summed = exchange(summed, "z")
-    (summed,) = call(spread_kernel, [eight], 1e5, 5e5)(summed)
-    summed = exchange(summed, ("x_hi", "y")).reshape(H // 2, E)
-    (grad_tokens,) = call(tokens_kernel, [((B, M, H), BF16)], 2 * 512 * H * E, 3e6)(
-        first, logit, ordered
-    )
-    (grad_router,) = call(join_kernel, [((H, E), F32)], 1e5, 7e5)(
-        ids, summed, swap(summed, "core")
-    )
+    (summed,) = call(spread_kernel, [((16, H // 16, E), F32)], 1e5, 5e5)(summed)
+    grad_router = exchange(summed, ("x_hi", "y", "core")).reshape(H, E)
     return grad_tokens, grad_router, grad_weight
 
 

time: 168 us -> 157 us (0.935)
  waiting for transfers between devices: 26.5 us -> 20.3 us
  starting transfers between devices: 21 us -> 15.3 us
  local copies, waits for them, and re-layouts: 6.27 us -> 0.72 us
  blocking collectives: 93.1 us -> 96.6 us
  Pallas kernels: 20.3 us -> 23.4 us
    ppermute x10 -> x9, waiting for transfers between devices: 26.5 us -> 20.3 us  [swap(): return lax.ppermute(x, axis, [(0, 1), (1, 0)])]
    ppermute x10 -> x9, starting transfers between devices: 21 us -> 15.3 us  [swap(): return lax.ppermute(x, axis, [(0, 1), (1, 0)])]
    unnamed x16 -> x1, local copies, waits for them, and re-layouts: 6.27 us -> 0.72 us
    pallas_call x16 -> x17, Pallas kernels: 19.1 us -> 23.4 us  [run(): pl.pallas_call(kernel, out_shape=[jax.ShapeDtypeStruct(s, d) for s, d in...]
    all_to_all x5, blocking collectives: 93.1 us -> 96.6 us  [exchange(): return lax.all_to_all(x, axes, split_axis=0, concat_axis=0, tiled=True)]
  transfers between devices with their start and end apart: 10 -> 9, of which waited for: 8 -> 7; matrix products, arithmetic and copies ran while one was open for 0% -> 0% of each run, Pallas kernels for 8% -> 10%
where the time goes in v3:
time: 157 us
  blocking collectives  96.6 us (62%)
  Pallas kernels  23.4 us (15%)
  waiting for transfers between devices  20.3 us (13%)
  starting transfers between devices  15.3 us (10%)
    all_to_all x5, blocking collectives, exchange(): return lax.all_to_all(x, axes, split_axis=0, concat_axis=0, tiled=True)  96.6 us
    pallas_call x17, Pallas kernels, run(): pl.pallas_call(kernel, out_shape=[jax.ShapeDtypeStruct(s, d) for s, d in...  23.4 us
    ppermute x9, waiting for transfers between devices, swap(): return lax.ppermute(x, axis, [(0, 1), (1, 0)])  20.3 us
    ppermute x9, starting transfers between devices, swap(): return lax.ppermute(x, axis, [(0, 1), (1, 0)])  15.3 us
  transfers between devices with their start and end apart: 9, of which 7 were waited for; matrix products, arithmetic and copies ran while one was open for 0% of the time, Pallas kernels for 10%

profile of v3, /device:TPU:1, one launch (start us, length us, event | category | flops | bytes accessed | tf_op | source)
XLA Modules:
  0.0 157.1 jit_solution(11708240931019859718)
XLA Ops:
  0.6 0.1 pad_add_fusion.ids
  0.7 2.2 %shard_map.76 = (f32[512,128]{1,0:T(8,128)S(1)}, bf16[640,128]{1,0:T(8,128)(2,1)S(1)}, bf16[2,256,640]{2,1,0:T(8,128)(2,1)S(1)}) custom-call(s32[2]{0:T(128)S(1)} %pad_add_fusion.ids, bf16[2,256,640]{2,1,0:T(8,128)(2,1)} %tokens_hbm.1, bf16[640,128]{1,0:T(8,128)(2,1)} %router_hbm.1), custom_call_target="tpu_custom_call" | custom-call | flops 83886080 | bytes 1000000 | tf_op jit(solution)/shard_map/pallas_call | solution.py:62
  3.0 2.1 %collective-permute-start = (f32[512,128]{1,0:T(8,128)S(1)}, f32[512,128]{1,0:T(8,128)S(1)}, u32[]{:S(2)}, u32[]{:S(2)}) collective-permute-start(f32[512,128]{1,0:T(8,128)S(1)} %get-tuple-element.34.part), channel_id=1, source_target_pairs={{0,1},{1,0},{2,3},{3,2},{4,5},{5,4},{6,7},{7,6},{8,9},{9,8},{10,11... | collective-permute-start | bytes 786440 | tf_op jit(solution)/shard_map/ppermute | solution.py:262
  5.1 3.2 %shard_map.77 = (bf16[2,256,640]{2,1,0:T(8,128)(2,1)S(1)}, bf16[1,1280,1280]{2,1,0:T(8,128)(2,1)S(1)}, bf16[1,1280,1280]{2,1,0:T(8,128)(2,1)S(1)}) custom-call(bf16[2,256,640]{2,1,0:T(8,128)(2,1)} %refs_0_.1, bf16[1,1280,1280]{2,1,0:T(8,128)(2,1)} %refs_1_.1, bf16[1,1280,1280]{2,1,0:T(8,128)(2,1)} %refs_2_.1), custom_call_target="tpu_custom_call" | custom-call | bytes 14000000 | tf_op jit(solution)/shard_map/pallas_call | solution.py:62
  8.3 1.5 collective-permute-done.other
  9.8 0.7 shard_map.78
  10.4 3.0 %collective-permute-start.1 = (bf16[256,640]{1,0:T(8,128)(2,1)S(1)}, bf16[256,640]{1,0:T(8,128)(2,1)S(1)}, u32[]{:S(2)}, u32[]{:S(2)}) collective-permute-start(bf16[256,640]{1,0:T(8,128)(2,1)S(1)} %get-tuple-element.38), channel_id=1, source_target_pairs={{0,2},{2,0},{1,3},{3,1},{4,6},{6,4},{5,7},{7,5},{8,10},{10,8},{9,1... | collective-permute-start | bytes 983048 | tf_op jit(solution)/shard_map/ppermute | solution.py:262
  13.4 1.3 collective-permute-done.1.got
  14.7 0.6 shard_map.79
  15.3 32.7 %all_to_all.25 = bf16[64,8,640]{2,1,0:T(8,128)(2,1)S(1)} all-to-all(bf16[64,8,640]{2,1,0:T(8,128)(2,1)S(1)} %bitcast.8), channel_id=1, replica_groups=mesh['z'=8,'x_hi'=2,'y'=4,'core'=2,'tp'=2] {'z','x_hi','y'}, dimensions={0} | all-to-all | bytes 1310720 | tf_op jit(solution)/shard_map/all_to_all | solution.py:266
  48.0 0.6 shard_map.80
  48.6 0.4 collective-permute-start.2
  48.9 1.2 collective-permute-start.4
  50.1 4.5 %collective-permute-done.2.other = bf16[256,640]{1,0:T(8,128)(2,1)S(1)} collective-permute-done((bf16[256,640]{1,0:T(8,128)(2,1)S(1)}, bf16[256,640]{1,0:T(8,128)(2,1)S(1)}, u32[]{:S(2)}, u32[]{:S(2)}) %collective-permute-start.2) | collective-permute-done | bytes 327712 | tf_op jit(solution)/shard_map/ppermute | solution.py:262
  54.6 4.4 %shard_map.81 = (f32[256,1280]{1,0:T(8,128)S(1)}, f32[256,640]{1,0:T(8,128)S(1)}, bf16[256,640]{1,0:T(8,128)(2,1)S(1)}) custom-call(s32[2]{0:T(128)S(1)} %pad_add_fusion.ids, bf16[256,640]{1,0:T(8,128)(2,1)S(1)} %get-tuple-element.39.own, bf16[256,640]{1,0:T(8,128)(2,1)S(1)} %collective-permute-done.2.other, ...), custom_call_target="tpu_custom_call" | custom-call | flops 1700000000 | bytes 10000000 | tf_op jit(solution)/shard_map/pallas_call | solution.py:62
  59.0 0.4 collective-permute-start.3
  59.3 1.9 %collective-permute-done.4.other = bf16[256,640]{1,0:T(8,128)(2,1)S(1)} collective-permute-done((bf16[256,640]{1,0:T(8,128)(2,1)S(1)}, bf16[256,640]{1,0:T(8,128)(2,1)S(1)}, u32[]{:S(2)}, u32[]{:S(2)}) %collective-permute-start.4) | collective-permute-done | bytes 327712 | tf_op jit(solution)/shard_map/ppermute | solution.py:262
  61.2 3.9 %shard_map.82 = (bf16[256,1280]{1,0:T(8,128)(2,1)S(1)}, f32[256,640]{1,0:T(8,128)S(1)}, bf16[256,640]{1,0:T(8,128)(2,1)S(1)}) custom-call(s32[2]{0:T(128)S(1)} %pad_add_fusion.ids, bf16[256,640]{1,0:T(8,128)(2,1)S(1)} %get-tuple-element.44.own, bf16[256,640]{1,0:T(8,128)(2,1)S(1)} %collective-permute-done.4.other, f32[256,1280]{1,0:T(8,128)S(1)} %get-tuple-element.45.slope, ...), custom_call_target="tpu_custom_call" | custom-call | flops 1700000000 | bytes 10000000 | tf_op jit(solution)/shard_map/pallas_call | solution.py:62
  65.1 0.5 collective-permute-start.5
  65.6 3.4 %shard_map.83 = (bf16[1,1280,1280]{2,1,0:T(8,128)(2,1)}, f32[8,128]{1,0:T(8,128)S(1)}) custom-call(s32[2]{0:T(128)S(1)} %pad_add_fusion.ids, bf16[256,640]{1,0:T(8,128)(2,1)S(1)} %get-tuple-element.39.own, bf16[256,640]{1,0:T(8,128)(2,1)S(1)} %collective-permute-done.2.other, bf16[256,1280]{1,0:T(8,128)(2,1)S(1)} %get-tuple-element.48.pre_grad), custom_call_target="tpu_custom_call" | custom-call | flops 840000000 | bytes 5000000 | tf_op jit(solution)/shard_map/pallas_call | solution.py:62
  69.0 0.0 collective-permute-done.3.out_got
  69.0 5.8 %collective-permute-done.5.in_got = bf16[256,640]{1,0:T(8,128)(2,1)S(1)} collective-permute-done((bf16[256,640]{1,0:T(8,128)(2,1)S(1)}, bf16[256,640]{1,0:T(8,128)(2,1)S(1)}, u32[]{:S(2)}, u32[]{:S(2)}) %collective-permute-start.5) | collective-permute-done | bytes 327712 | tf_op jit(solution)/shard_map/ppermute | solution.py:262
  74.8 0.7 shard_map.84
  75.5 27.1 %all_to_all.26 = bf16[64,8,640]{2,1,0:T(8,128)(2,1)S(1)} all-to-all(bf16[64,8,640]{2,1,0:T(8,128)(2,1)S(1)} %bitcast.7), channel_id=1, replica_groups=mesh['z'=8,'x_hi'=2,'y'=4,'core'=2,'tp'=2] {'z','x_hi','y'}, dimensions={0} | all-to-all | bytes 1310720 | tf_op jit(solution)/shard_map/all_to_all | solution.py:266
  102.5 0.6 shard_map.85
  103.1 6.0 %collective-permute-start.6 = (bf16[256,640]{1,0:T(8,128)(2,1)S(1)}, bf16[256,640]{1,0:T(8,128)(2,1)S(1)}, u32[]{:S(2)}, u32[]{:S(2)}) collective-permute-start(bf16[256,640]{1,0:T(8,128)(2,1)S(1)} %get-tuple-element.51), channel_id=1, source_target_pairs={{0,2},{2,0},{1,3},{3,1},{4,6},{6,4},{5,7},{7,5},{8,10},{10,8},{9,1... | collective-permute-start | bytes 983048 | tf_op jit(solution)/shard_map/ppermute | solution.py:262
  109.2 1.3 collective-permute-done.6.got
  110.4 0.6 shard_map.87
  111.0 0.4 collective-permute-start.7
  111.4 0.3 shard_map.86
  111.7 4.1 %collective-permute-done.7.got = bf16[512,128]{1,0:T(8,128)(2,1)S(1)} collective-permute-done((bf16[512,128]{1,0:T(8,128)(2,1)S(1)}, bf16[512,128]{1,0:T(8,128)(2,1)S(1)}, u32[]{:S(2)}, u32[]{:S(2)}) %collective-permute-start.7) | collective-permute-done | bytes 131104 | tf_op jit(solution)/shard_map/ppermute | solution.py:262
  115.8 1.2 shard_map.88
  117.0 1.3 collective-permute-start.8
  118.3 1.2 shard_map.89
  119.4 0.0 collective-permute-done.8.y
  119.5 11.6 %all_to_all.27.x = f32[8,40,128]{2,1,0:T(8,128)S(1)} all-to-all(f32[8,40,128]{2,1,0:T(8,128)S(1)} %shard_map.90), channel_id=1, replica_groups=mesh['z'=8,'x_hi'=2,'y'=4,'core'=2,'tp'=2] {'x_hi','y'}, dimensions={0} | all-to-all | bytes 327680 | tf_op jit(solution)/shard_map/all_to_all | solution.py:266
  131.1 10.8 %all_to_all.28.x = f32[8,40,128]{2,1,0:T(8,128)S(1)} all-to-all(f32[8,40,128]{2,1,0:T(8,128)S(1)} %shard_map.91), channel_id=1, replica_groups=mesh['z'=8,'x_hi'=2,'y'=4,'core'=2,'tp'=2] {'z'}, dimensions={0} | all-to-all | bytes 327680 | tf_op jit(solution)/shard_map/all_to_all | solution.py:266
  141.9 14.4 %all_to_all.29 = f32[16,40,128]{2,1,0:T(8,128)S(1)} all-to-all(f32[16,40,128]{2,1,0:T(8,128)S(1)} %shard_map.92), channel_id=1, replica_groups=mesh['z'=8,'x_hi'=2,'y'=4,'core'=2,'tp'=2] {'x_hi','y','core'}, dimensions={0} | all-to-all | bytes 655360 | tf_op jit(solution)/shard_map/all_to_all | solution.py:266
  156.4 0.7 copy.9
  (3 shorter events, 0.1 us)
Async XLA Ops:
  3.0 6.8 %collective-permute-start = (f32[512,128]{1,0:T(8,128)S(1)}, f32[512,128]{1,0:T(8,128)S(1)}, u32[]{:S(2)}, u32[]{:S(2)}) collective-permute-start(f32[512,128]{1,0:T(8,128)S(1)} %get-tuple-element.34.part), channel_id=1, source_target_pairs={{0,1},{1,0},{2,3},{3,2},{4,5},{5,4},{6,7},{7,6},{8,9},{9,8},{10,11... | collective-permute-start | bytes 786440 | tf_op jit(solution)/shard_map/ppermute | solution.py:262
  10.4 4.2 %collective-permute-start.1 = (bf16[256,640]{1,0:T(8,128)(2,1)S(1)}, bf16[256,640]{1,0:T(8,128)(2,1)S(1)}, u32[]{:S(2)}, u32[]{:S(2)}) collective-permute-start(bf16[256,640]{1,0:T(8,128)(2,1)S(1)} %get-tuple-element.38), channel_id=1, source_target_pairs={{0,2},{2,0},{1,3},{3,1},{4,6},{6,4},{5,7},{7,5},{8,10},{10,8},{9,1... | collective-permute-start | bytes 983048 | tf_op jit(solution)/shard_map/ppermute | solution.py:262
  48.6 6.0 %collective-permute-start.2 = (bf16[256,640]{1,0:T(8,128)(2,1)S(1)}, bf16[256,640]{1,0:T(8,128)(2,1)S(1)}, u32[]{:S(2)}, u32[]{:S(2)}) collective-permute-start(bf16[256,640]{1,0:T(8,128)(2,1)S(1)} %get-tuple-element.39.own), channel_id=1, source_target_pairs={{0,1},{1,0},{2,3},{3,2},{4,5},{5,4},{6,7},{7,6},{8,9},{9,8},{10,11... | collective-permute-start | bytes 983048 | tf_op jit(solution)/shard_map/ppermute | solution.py:262
  48.9 12.3 %collective-permute-start.4 = (bf16[256,640]{1,0:T(8,128)(2,1)S(1)}, bf16[256,640]{1,0:T(8,128)(2,1)S(1)}, u32[]{:S(2)}, u32[]{:S(2)}) collective-permute-start(bf16[256,640]{1,0:T(8,128)(2,1)S(1)} %get-tuple-element.44.own), channel_id=1, source_target_pairs={{0,1},{1,0},{2,3},{3,2},{4,5},{5,4},{6,7},{7,6},{8,9},{9,8},{10,11... | collective-permute-start | bytes 983048 | tf_op jit(solution)/shard_map/ppermute | solution.py:262
  59.0 10.0 %collective-permute-start.3 = (bf16[256,640]{1,0:T(8,128)(2,1)S(1)}, bf16[256,640]{1,0:T(8,128)(2,1)S(1)}, u32[]{:S(2)}, u32[]{:S(2)}) collective-permute-start(bf16[256,640]{1,0:T(8,128)(2,1)S(1)} %get-tuple-element.43), channel_id=1, source_target_pairs={{0,1},{1,0},{2,3},{3,2},{4,5},{5,4},{6,7},{7,6},{8,9},{9,8},{10,11... | collective-permute-start | bytes 983048 | tf_op jit(solution)/shard_map/ppermute | solution.py:262
  65.1 9.7 %collective-permute-start.5 = (bf16[256,640]{1,0:T(8,128)(2,1)S(1)}, bf16[256,640]{1,0:T(8,128)(2,1)S(1)}, u32[]{:S(2)}, u32[]{:S(2)}) collective-permute-start(bf16[256,640]{1,0:T(8,128)(2,1)S(1)} %get-tuple-element.47), channel_id=1, source_target_pairs={{0,1},{1,0},{2,3},{3,2},{4,5},{5,4},{6,7},{7,6},{8,9},{9,8},{10,11... | collective-permute-start | bytes 983048 | tf_op jit(solution)/shard_map/ppermute | solution.py:262
  103.1 7.3 %collective-permute-start.6 = (bf16[256,640]{1,0:T(8,128)(2,1)S(1)}, bf16[256,640]{1,0:T(8,128)(2,1)S(1)}, u32[]{:S(2)}, u32[]{:S(2)}) collective-permute-start(bf16[256,640]{1,0:T(8,128)(2,1)S(1)} %get-tuple-element.51), channel_id=1, source_target_pairs={{0,2},{2,0},{1,3},{3,1},{4,6},{6,4},{5,7},{7,5},{8,10},{10,8},{9,1... | collective-permute-start | bytes 983048 | tf_op jit(solution)/shard_map/ppermute | solution.py:262
  111.0 4.8 %collective-permute-start.7 = (bf16[512,128]{1,0:T(8,128)(2,1)S(1)}, bf16[512,128]{1,0:T(8,128)(2,1)S(1)}, u32[]{:S(2)}, u32[]{:S(2)}) collective-permute-start(bf16[512,128]{1,0:T(8,128)(2,1)S(1)} %get-tuple-element.56), channel_id=1, source_target_pairs={{0,1},{1,0},{2,3},{3,2},{4,5},{5,4},{6,7},{7,6},{8,9},{9,8},{10,11... | collective-permute-start | bytes 393224 | tf_op jit(solution)/shard_map/ppermute | solution.py:262
  117.0 2.5 %collective-permute-start.8 = (f32[8,40,128]{2,1,0:T(8,128)S(1)}, f32[8,40,128]{2,1,0:T(8,128)S(1)}, u32[]{:S(2)}, u32[]{:S(2)}) collective-permute-start(f32[8,40,128]{2,1,0:T(8,128)S(1)} %get-tuple-element.62), channel_id=1, source_target_pairs={{0,2},{2,0},{1,3},{3,1},{4,6},{6,4},{5,7},{7,5},{8,10},{10,8},{9,1... | collective-permute-start | bytes 491528 | tf_op jit(solution)/shard_map/ppermute | solution.py:262

commit v4 on v3

--- a/solution.py
+++ b/solution.py
@@ -5,8 +5,8 @@
 from jax.experimental.pallas import tpu as pltpu
 from jax.sharding import Mesh, PartitionSpec as P
 
-AXES = ("z", "x_hi", "y", "core", "tp")
-CHIPS = ("z", "x_hi", "y")
+AXES = ("z2", "z1", "z0", "x_hi", "y", "core", "tp")
+CHIPS = ("z2", "z1", "z0", "x_hi", "y")
 F32 = jnp.float32
 BF16 = jnp.bfloat16
 I32 = jnp.int32
@@ -77,27 +77,43 @@
 
 
 def logits_kernel(ids, tokens_hbm, router_hbm, part, ordered, tokens, router, sems):
-    copies = [
-        pltpu.make_async_copy(tokens_hbm, tokens, sems.at[0]),
-        pltpu.make_async_copy(router_hbm, router, sems.at[1]),
-    ]
+    load = pltpu.make_async_copy(router_hbm, router, sems.at[4])
+    load.start()
+    copies = []
+    for i in range(4):
+        at = (i // 2, pl.ds((i % 2) * (M // 2), M // 2))
+        copies.append(pltpu.make_async_copy(tokens_hbm.at[at], tokens.at[at], sems.at[i]))
+        copies[i].start()
+    order = expert_order(ids[0])
+    load.wait()
+    r = dot(router[...], order).astype(BF16)
+    ordered[...] = r
+    for b in range(B):
+        copies[2 * b].wait()
+        copies[2 * b + 1].wait()
+        part[b * M : (b + 1) * M, :] = dot(tokens[b], r)
+
+
+def fetch_kernel(grad_hbm, in_hbm, out_hbm, tokens, grad, w_in, w_out, turned, *rest):
+    packing, splitting, merging, unpacking, sems = rest
+    pairs = ((grad_hbm, grad), (in_hbm, w_in), (out_hbm, w_out))
+    copies = [pltpu.make_async_copy(x, y, sems.at[i]) for i, (x, y) in enumerate(pairs)]
     for c in copies:
         c.start()
-    order = expert_order(ids[0])
-    copies[1].wait()
-    r = dot(router[...], order).astype(BF16)
-    ordered[...] = r
-    copies[0].wait()
-    for b in range(B):
-        part[b * M : (b + 1) * M, :] = dot(tokens[b], r)
-
-
-def fetch_kernel(*refs):
-    n = len(refs) // 2
-    sems = refs[-1]
-    copies = [pltpu.make_async_copy(refs[i], refs[n + i], sems.at[i]) for i in range(n)]
-    for c in copies:
-        c.start()
+    for b in range(B):
+        turned[:, b * M : (b + 1) * M] = jnp.transpose(tokens[b])
+    i, j = rows_cols(8 * NQ, 8 * NQ)
+
+    def packed_of_plain(j):
+        return (j & 63) * 8 + (j >> 6)
+
+    def packed_of_split(j):
+        return (j & 63) * 8 + ((j >> 7) & 1) * 4 + (j >> 8) * 2 + ((j >> 6) & 1)
+
+    packing[...] = ones_where(i == packed_of_plain(j))
+    unpacking[...] = ones_where(j == packed_of_plain(i))
+    merging[...] = ones_where(i == packed_of_split(j))
+    splitting[...] = ones_where(j == packed_of_split(i))
     for c in copies:
         c.wait()
 
@@ -119,20 +135,15 @@
             send[k * NQ : (k + 1) * NQ, :] = s[NQ:]
 
 
-def pack_kernel(keep, got, out):
-    i, j = rows_cols(8 * NQ, 4 * NQ)
-    for s, x in enumerate((keep, got)):
-        to = ones_where((j == (i & 3) * NQ + (i >> 3)) & (((i >> 2) & 1) == s))
-        part = dot(to, x[...])
-        total = part if s == 0 else total + part
-    out[...] = total.astype(BF16)
-
-
-def split_kernel(rows, slot_in, slot_grad):
-    n, i = rows_cols(4 * NQ, 8 * NQ)
-    for a, out in enumerate((slot_in, slot_grad)):
-        src = (n & 63) * 8 + ((n >> 7) & 1) * 4 + a * 2 + ((n >> 6) & 1)
-        out[...] = dot(ones_where(i == src), rows[...]).astype(BF16)
+def pack_kernel(packing, keep, got, out):
+    n = 4 * NQ
+    out[...] = (dot(packing[:, :n], keep[...]) + dot(packing[:, n:], got[...])).astype(BF16)
+
+
+def split_kernel(splitting, rows, slot_in, slot_grad):
+    n = 4 * NQ
+    slot_in[...] = dot(splitting[:n, :], rows[...]).astype(BF16)
+    slot_grad[...] = dot(splitting[n:, :], rows[...]).astype(BF16)
 
 
 def both_halves(ids):
@@ -185,21 +196,17 @@
     done[...] = jnp.zeros(done.shape, F32)
 
 
-def merge_kernel(out_keep, out_got, in_keep, in_got, done, out):
-    i, n = rows_cols(8 * NQ, 4 * NQ)
-    for a, (x, y) in enumerate(((out_keep, out_got), (in_keep, in_got))):
-        r = (x[...] + y[...].astype(F32)).astype(BF16)
-        src = ((i >> 2) & 1) * 128 + (i & 1) * 64 + (i >> 3)
-        part = dot(ones_where((n == src) & (((i >> 1) & 1) == a)), r)
-        total = part if a == 0 else total + part
-    out[...] = total.astype(BF16)
-
-
-def unpack_kernel(rows, own, send):
-    n, i = rows_cols(4 * NQ, 8 * NQ)
-    for s, out in enumerate((own, send)):
-        src = (n & 63) * 8 + s * 4 + (n >> 6)
-        out[...] = dot(ones_where(i == src), rows[...]).astype(BF16)
+def merge_kernel(merging, out_keep, out_got, in_keep, in_got, done, out):
+    n = 4 * NQ
+    x = (out_keep[...] + out_got[...].astype(F32)).astype(BF16)
+    y = (in_keep[...] + in_got[...].astype(F32)).astype(BF16)
+    out[...] = (dot(merging[:, :n], x) + dot(merging[:, n:], y)).astype(BF16)
+
+
+def unpack_kernel(unpacking, rows, own, send):
+    n = 4 * NQ
+    own[...] = dot(unpacking[:n, :], rows[...]).astype(BF16)
+    send[...] = dot(unpacking[n:, :], rows[...]).astype(BF16)
 
 
 def slots_of(own, got, a, b):
@@ -226,17 +233,16 @@
     done[...] = jnp.zeros(done.shape, F32)
 
 
-def logit_kernel(ids, part, got, tokens, done, logit, keep, send, whole):
+def logit_kernel(ids, part, got, turned, done, logit, keep, send, whole):
     g = (part[...] + got[...].astype(F32)).astype(BF16)
     logit[...] = g
     plain = dot_t(g, expert_order(ids[0])).astype(BF16)
-    total = t_dot(plain[:M], tokens[0]) + t_dot(plain[M:], tokens[1])
-    whole[...] = jnp.transpose(total)
+    whole[...] = dot(turned[...], plain)
     c = ids[0]
     n = H // 16
     for i in range(8):
         keep[i] = whole[pl.ds(pl.multiple_of((2 * i + c) * n, 8), n), :]
-        send[i] = whole[pl.ds(pl.multiple_of((2 * i + 1 - c) * n, 8), n), :]
+        send[i] = whole[pl.ds(pl.multiple_of((2 * i + 1 - c) * n, 8), n), :].astype(BF16)
 
 
 def tokens_kernel(first, logit, router, out, done):
@@ -247,15 +253,22 @@
 
 
 def add_kernel(x, y, done, out):
-    out[...] = x[...] + y[...]
+    out[...] = (x[...] + y[...].astype(F32)).astype(BF16)
 
 
 def spread_kernel(x, out):
-    total = x[0]
+    total = x[0].astype(F32)
     for i in range(1, 8):
-        total = total + x[i]
+        total = total + x[i].astype(F32)
+    total = total.astype(BF16)
     for i in range(out.shape[0]):
         out[i] = total
+
+
+def widen_kernel(x, out):
+    n = H // 16
+    for i in range(16):
+        out[i * n : (i + 1) * n, :] = x[i].astype(F32)
 
 
 def swap(x, axis):
@@ -278,24 +291,26 @@
         small,
         1e6,
         hbm=(1, 2),
-        scratch=[pltpu.VMEM((H, E), BF16), pltpu.SemaphoreType.DMA((2,))],
+        scratch=[pltpu.VMEM((H, E), BF16), pltpu.SemaphoreType.DMA((5,))],
     )(ids, tokens, router)
     other = swap(part, "tp")
-    grad_out, w_in, w_out = call(
+    onehot = ((8 * NQ, 8 * NQ), BF16)
+    grad_out, w_in, w_out, turned, packing, splitting, merging, unpacking = call(
         fetch_kernel,
-        [((B, M, H), BF16), ((1, D, FH), BF16), ((1, FH, D), BF16)],
+        [((B, M, H), BF16), ((1, D, FH), BF16), ((1, FH, D), BF16), ((H, B * M), BF16)]
+        + [onehot] * 4,
         0,
         1.4e7,
         hbm=(0, 1, 2),
         scratch=[pltpu.SemaphoreType.DMA((3,))],
-    )(grad_out, w_in, w_out)
+    )(grad_out, w_in, w_out, tokens)
     dispatch, combine, keep, send = call(
         slots_kernel, [((B * M, E), F32)] * 2 + [half] * 2, 2 * small, 3e6
     )(part, other, tokens, grad_out)
     got = swap(send, "core")
-    (packed,) = call(pack_kernel, [((8 * NQ, H), BF16)], 3e8, 1.3e6)(keep, got)
+    (packed,) = call(pack_kernel, [((8 * NQ, H), BF16)], 3e8, 1.3e6)(packing, keep, got)
     rows = exchange(packed.reshape(NQ, 8, H), CHIPS).reshape(8 * NQ, H)
-    in_own, grad_own = call(split_kernel, [half] * 2, 3e8, 1.3e6)(rows)
+    in_own, grad_own = call(split_kernel, [half] * 2, 3e8, 1.3e6)(splitting, rows)
     in_other = swap(in_own, "tp")
     grad_other = swap(grad_own, "tp")
     slope, out_keep, out_send = call(
@@ -310,10 +325,10 @@
         ids, in_own, in_other, pre_grad
     )
     (merged,) = call(merge_kernel, [((8 * NQ, H), BF16)], 3e8, 2.6e6)(
-        out_keep, out_got, in_keep, in_got, weight_done
+        merging, out_keep, out_got, in_keep, in_got, weight_done
     )
     rows = exchange(merged.reshape(NQ, 8, H), CHIPS).reshape(8 * NQ, H)
-    own, send = call(unpack_kernel, [half] * 2, 3e8, 1.3e6)(rows)
+    own, send = call(unpack_kernel, [half] * 2, 3e8, 1.3e6)(unpacking, rows)
     got = swap(send, "core")
     part, send = call(
         dots_kernel, [((B * M, E), F32), ((B * M, E), BF16)], 2 * small, 3e6
@@ -322,14 +337,15 @@
     first, first_done = call(first_kernel, [((B, M, H), F32), done], small, 2e6)(
         own, got, dispatch
     )
-    eight = ((8, H // 16, E), F32)
+    eight = ((8, H // 16, E), BF16)
+    eight32 = ((8, H // 16, E), F32)
     logit, keep, send = call(
         logit_kernel,
-        [((B * M, E), BF16), eight, eight],
+        [((B * M, E), BF16), eight32, eight],
         small,
         3e6,
         scratch=[pltpu.VMEM((H, E), F32)],
-    )(ids, part, logit_got, tokens, first_done)
+    )(ids, part, logit_got, turned, first_done)
     got = swap(send, "core")
     grad_tokens, tokens_done = call(
         tokens_kernel, [((B, M, H), BF16), done], small, 3e6
@@ -337,15 +353,16 @@
     (summed,) = call(add_kernel, [eight], 1e5, 5e5)(keep, got, tokens_done)
     summed = exchange(summed, ("x_hi", "y"))
     (summed,) = call(spread_kernel, [eight], 1e5, 5e5)(summed)
-    summed = exchange(summed, "z")
-    (summed,) = call(spread_kernel, [((16, H // 16, E), F32)], 1e5, 5e5)(summed)
-    grad_router = exchange(summed, ("x_hi", "y", "core")).reshape(H, E)
+    summed = exchange(summed, ("z0", "z1", "z2"))
+    (summed,) = call(spread_kernel, [((16, H // 16, E), BF16)], 1e5, 5e5)(summed)
+    summed = exchange(summed, ("x_hi", "y", "core"))
+    (grad_router,) = call(widen_kernel, [((H, E), F32)], 1e5, 5e5)(summed)
     return grad_tokens, grad_router, grad_weight
 
 
 def solution(mesh):
-    fine = Mesh(mesh.devices.reshape(8, 2, 4, 2, 2), AXES)
-    ep = ("z", "x_hi", "y", "core")
+    fine = Mesh(mesh.devices.reshape(2, 2, 2, 2, 4, 2, 2), AXES)
+    ep = CHIPS + ("core",)
     return jax.shard_map(
         on_device,
         mesh=fine,

time: 157 us -> 154 us (0.981)
  blocking collectives: 96.6 us -> 93.1 us
    all_to_all x5, blocking collectives: 96.6 us -> 93.1 us  [exchange(): return lax.all_to_all(x, axes, split_axis=0, concat_axis=0, tiled=True)]
    pallas_call x17 -> x18, Pallas kernels: 23.4 us -> 24 us  [run(): pl.pallas_call(kernel, out_shape=[jax.ShapeDtypeStruct(s, d) for s, d in...]
  transfers between devices with their start and end apart: 9 -> 9, of which waited for: 7 -> 7; matrix products, arithmetic and copies ran while one was open for 0% -> 0% of each run, Pallas kernels for 10% -> 11%
where the time goes in v4:
time: 154 us; the launch traced here: 153 us
  blocking collectives  93.1 us (60%)
  Pallas kernels  24 us (16%)
  waiting for transfers between devices  20.3 us (13%)
  starting transfers between devices  15.2 us (10%)
    all_to_all x5, blocking collectives, exchange(): return lax.all_to_all(x, axes, split_axis=0, concat_axis=0, tiled=True)  93.1 us
    pallas_call x18, Pallas kernels, run(): pl.pallas_call(kernel, out_shape=[jax.ShapeDtypeStruct(s, d) for s, d in...  24 us
    ppermute x9, waiting for transfers between devices, swap(): return lax.ppermute(x, axis, [(0, 1), (1, 0)])  20.3 us
    ppermute x9, starting transfers between devices, swap(): return lax.ppermute(x, axis, [(0, 1), (1, 0)])  15.2 us
  transfers between devices with their start and end apart: 9, of which 7 were waited for; matrix products, arithmetic and copies ran while one was open for 0% of the time, Pallas kernels for 11%

profile of v4, /device:TPU:1, one launch (start us, length us, event | category | flops | bytes accessed | tf_op | source)
XLA Modules:
  0.0 153.5 jit_solution(3054034391158457633)
XLA Ops:
  0.6 0.1 pad_add_fusion.ids
  0.7 2.2 %shard_map.76 = (f32[512,128]{1,0:T(8,128)S(1)}, bf16[640,128]{1,0:T(8,128)(2,1)S(1)}, bf16[2,256,640]{2,1,0:T(8,128)(2,1)S(1)}) custom-call(s32[2]{0:T(128)S(1)} %pad_add_fusion.ids, bf16[2,256,640]{2,1,0:T(8,128)(2,1)} %tokens_hbm.1, bf16[640,128]{1,0:T(8,128)(2,1)} %router_hbm.1), custom_call_target="tpu_custom_call" | custom-call | flops 83886080 | bytes 1000000 | tf_op jit(solution)/shard_map/pallas_call | solution.py:62
  3.0 2.1 %collective-permute-start = (f32[512,128]{1,0:T(8,128)S(1)}, f32[512,128]{1,0:T(8,128)S(1)}, u32[]{:S(2)}, u32[]{:S(2)}) collective-permute-start(f32[512,128]{1,0:T(8,128)S(1)} %get-tuple-element.44.part), channel_id=1, source_target_pairs={{0,1},{1,0},{2,3},{3,2},{4,5},{5,4},{6,7},{7,6},{8,9},{9,8},{10,11... | collective-permute-start | bytes 786440 | tf_op jit(solution)/shard_map/ppermute | solution.py:275
  5.1 3.2 %shard_map.77 = (bf16[2,256,640]{2,1,0:T(8,128)(2,1)S(1)}, bf16[1,1280,1280]{2,1,0:T(8,128)(2,1)S(1)}, bf16[1,1280,1280]{2,1,0:T(8,128)(2,1)S(1)}, bf16[640,512]...) custom-call(bf16[2,256,640]{2,1,0:T(8,128)(2,1)} %grad_hbm.1, ...), custom_call_target="tpu_custom_call" | custom-call | bytes 14000000 | tf_op jit(solution)/shard_map/pallas_call | solution.py:62
  8.3 1.5 collective-permute-done.other
  9.8 0.7 shard_map.78
  10.5 3.0 %collective-permute-start.1 = (bf16[256,640]{1,0:T(8,128)(2,1)S(1)}, bf16[256,640]{1,0:T(8,128)(2,1)S(1)}, u32[]{:S(2)}, u32[]{:S(2)}) collective-permute-start(bf16[256,640]{1,0:T(8,128)(2,1)S(1)} %get-tuple-element.47), channel_id=1, source_target_pairs={{0,2},{2,0},{1,3},{3,1},{4,6},{6,4},{5,7},{7,5},{8,10},{10,8},{9,1... | collective-permute-start | bytes 983048 | tf_op jit(solution)/shard_map/ppermute | solution.py:275
  13.4 1.3 collective-permute-done.1.got
  14.7 0.6 shard_map.79
  15.3 32.7 %all_to_all.25 = bf16[64,8,640]{2,1,0:T(8,128)(2,1)S(1)} all-to-all(bf16[64,8,640]{2,1,0:T(8,128)(2,1)S(1)} %bitcast.6), channel_id=1, replica_groups=mesh['z2'=2,'z1'=2,'z0'=2,'x_hi'=2,'y'=4,'core'=2,'tp'=2] {'z2','z1','z0..., dimensions={0} | all-to-all | bytes 1310720 | tf_op jit(solution)/shard_map/all_to_all | solution.py:279
  48.0 0.6 shard_map.80
  48.5 0.4 collective-permute-start.2
  48.9 1.2 collective-permute-start.4
  50.1 4.5 %collective-permute-done.2.other = bf16[256,640]{1,0:T(8,128)(2,1)S(1)} collective-permute-done((bf16[256,640]{1,0:T(8,128)(2,1)S(1)}, bf16[256,640]{1,0:T(8,128)(2,1)S(1)}, u32[]{:S(2)}, u32[]{:S(2)}) %collective-permute-start.2) | collective-permute-done | bytes 327712 | tf_op jit(solution)/shard_map/ppermute | solution.py:275
  54.6 4.4 %shard_map.81 = (f32[256,1280]{1,0:T(8,128)S(1)}, f32[256,640]{1,0:T(8,128)S(1)}, bf16[256,640]{1,0:T(8,128)(2,1)S(1)}) custom-call(s32[2]{0:T(128)S(1)} %pad_add_fusion.ids, bf16[256,640]{1,0:T(8,128)(2,1)S(1)} %get-tuple-element.48.own, bf16[256,640]{1,0:T(8,128)(2,1)S(1)} %collective-permute-done.2.other, ...), custom_call_target="tpu_custom_call" | custom-call | flops 1700000000 | bytes 10000000 | tf_op jit(solution)/shard_map/pallas_call | solution.py:62
  58.9 0.3 collective-permute-start.3
  59.3 1.9 %collective-permute-done.4.other = bf16[256,640]{1,0:T(8,128)(2,1)S(1)} collective-permute-done((bf16[256,640]{1,0:T(8,128)(2,1)S(1)}, bf16[256,640]{1,0:T(8,128)(2,1)S(1)}, u32[]{:S(2)}, u32[]{:S(2)}) %collective-permute-start.4) | collective-permute-done | bytes 327712 | tf_op jit(solution)/shard_map/ppermute | solution.py:275
  61.2 3.9 %shard_map.82 = (bf16[256,1280]{1,0:T(8,128)(2,1)S(1)}, f32[256,640]{1,0:T(8,128)S(1)}, bf16[256,640]{1,0:T(8,128)(2,1)S(1)}) custom-call(s32[2]{0:T(128)S(1)} %pad_add_fusion.ids, bf16[256,640]{1,0:T(8,128)(2,1)S(1)} %get-tuple-element.53.own, bf16[256,640]{1,0:T(8,128)(2,1)S(1)} %collective-permute-done.4.other, f32[256,1280]{1,0:T(8,128)S(1)} %get-tuple-element.54.slope, ...), custom_call_target="tpu_custom_call" | custom-call | flops 1700000000 | bytes 10000000 | tf_op jit(solution)/shard_map/pallas_call | solution.py:62
  65.1 0.5 collective-permute-start.5
  65.6 3.3 %shard_map.83 = (bf16[1,1280,1280]{2,1,0:T(8,128)(2,1)}, f32[8,128]{1,0:T(8,128)S(1)}) custom-call(s32[2]{0:T(128)S(1)} %pad_add_fusion.ids, bf16[256,640]{1,0:T(8,128)(2,1)S(1)} %get-tuple-element.48.own, bf16[256,640]{1,0:T(8,128)(2,1)S(1)} %collective-permute-done.2.other, bf16[256,1280]{1,0:T(8,128)(2,1)S(1)} %get-tuple-element.57.pre_grad), custom_call_target="tpu_custom_call" | custom-call | flops 840000000 | bytes 5000000 | tf_op jit(solution)/shard_map/pallas_call | solution.py:62
  68.9 0.0 collective-permute-done.3.out_got
  68.9 5.8 %collective-permute-done.5.in_got = bf16[256,640]{1,0:T(8,128)(2,1)S(1)} collective-permute-done((bf16[256,640]{1,0:T(8,128)(2,1)S(1)}, bf16[256,640]{1,0:T(8,128)(2,1)S(1)}, u32[]{:S(2)}, u32[]{:S(2)}) %collective-permute-start.5) | collective-permute-done | bytes 327712 | tf_op jit(solution)/shard_map/ppermute | solution.py:275
  74.8 0.6 shard_map.84
  75.4 27.1 %all_to_all.26 = bf16[64,8,640]{2,1,0:T(8,128)(2,1)S(1)} all-to-all(bf16[64,8,640]{2,1,0:T(8,128)(2,1)S(1)} %bitcast.9), channel_id=1, replica_groups=mesh['z2'=2,'z1'=2,'z0'=2,'x_hi'=2,'y'=4,'core'=2,'tp'=2] {'z2','z1','z0..., dimensions={0} | all-to-all | bytes 1310720 | tf_op jit(solution)/shard_map/all_to_all | solution.py:279
  102.5 0.6 shard_map.85
  103.0 6.0 %collective-permute-start.6 = (bf16[256,640]{1,0:T(8,128)(2,1)S(1)}, bf16[256,640]{1,0:T(8,128)(2,1)S(1)}, u32[]{:S(2)}, u32[]{:S(2)}) collective-permute-start(bf16[256,640]{1,0:T(8,128)(2,1)S(1)} %get-tuple-element.60), channel_id=1, source_target_pairs={{0,2},{2,0},{1,3},{3,1},{4,6},{6,4},{5,7},{7,5},{8,10},{10,8},{9,1... | collective-permute-start | bytes 983048 | tf_op jit(solution)/shard_map/ppermute | solution.py:275
  109.1 1.3 collective-permute-done.6.got
  110.3 0.6 shard_map.87
  110.9 0.4 collective-permute-start.7
  111.3 0.3 shard_map.86
  111.6 4.1 %collective-permute-done.7.got = bf16[512,128]{1,0:T(8,128)(2,1)S(1)} collective-permute-done((bf16[512,128]{1,0:T(8,128)(2,1)S(1)}, bf16[512,128]{1,0:T(8,128)(2,1)S(1)}, u32[]{:S(2)}, u32[]{:S(2)}) %collective-permute-start.7) | collective-permute-done | bytes 131104 | tf_op jit(solution)/shard_map/ppermute | solution.py:275
  115.7 1.1 shard_map.88
  116.8 1.3 collective-permute-start.8
  118.1 1.2 shard_map.89
  119.3 0.0 collective-permute-done.8.y
  119.3 11.3 %all_to_all.27.x = bf16[8,40,128]{2,1,0:T(8,128)(2,1)S(1)} all-to-all(bf16[8,40,128]{2,1,0:T(8,128)(2,1)S(1)} %shard_map.90), channel_id=1, replica_groups=mesh['z2'=2,'z1'=2,'z0'=2,'x_hi'=2,'y'=4,'core'=2,'tp'=2] {'x_hi','y'}, dimensions={0} | all-to-all | bytes 163840 | tf_op jit(solution)/shard_map/all_to_all | solution.py:279
  130.6 9.0 %all_to_all.28.x = bf16[8,40,128]{2,1,0:T(8,128)(2,1)S(1)} all-to-all(bf16[8,40,128]{2,1,0:T(8,128)(2,1)S(1)} %shard_map.91), channel_id=1, replica_groups=mesh['z2'=2,'z1'=2,'z0'=2,'x_hi'=2,'y'=4,'core'=2,'tp'=2] {'z0','z1','z2'}, dimensions={0} | all-to-all | bytes 163840 | tf_op jit(solution)/shard_map/all_to_all | solution.py:279
  139.6 13.1 %all_to_all.29.x = bf16[16,40,128]{2,1,0:T(8,128)(2,1)S(1)} all-to-all(bf16[16,40,128]{2,1,0:T(8,128)(2,1)S(1)} %shard_map.92), channel_id=1, replica_groups=mesh['z2'=2,'z1'=2,'z0'=2,'x_hi'=2,'y'=4,'core'=2,'tp'=2] {'x_hi','y','c..., dimensions={0} | all-to-all | bytes 327680 | tf_op jit(solution)/shard_map/all_to_all | solution.py:279
  152.7 0.7 shard_map.93
  (3 shorter events, 0.1 us)
Async XLA Ops:
  3.0 6.8 %collective-permute-start = (f32[512,128]{1,0:T(8,128)S(1)}, f32[512,128]{1,0:T(8,128)S(1)}, u32[]{:S(2)}, u32[]{:S(2)}) collective-permute-start(f32[512,128]{1,0:T(8,128)S(1)} %get-tuple-element.44.part), channel_id=1, source_target_pairs={{0,1},{1,0},{2,3},{3,2},{4,5},{5,4},{6,7},{7,6},{8,9},{9,8},{10,11... | collective-permute-start | bytes 786440 | tf_op jit(solution)/shard_map/ppermute | solution.py:275
  10.5 4.2 %collective-permute-start.1 = (bf16[256,640]{1,0:T(8,128)(2,1)S(1)}, bf16[256,640]{1,0:T(8,128)(2,1)S(1)}, u32[]{:S(2)}, u32[]{:S(2)}) collective-permute-start(bf16[256,640]{1,0:T(8,128)(2,1)S(1)} %get-tuple-element.47), channel_id=1, source_target_pairs={{0,2},{2,0},{1,3},{3,1},{4,6},{6,4},{5,7},{7,5},{8,10},{10,8},{9,1... | collective-permute-start | bytes 983048 | tf_op jit(solution)/shard_map/ppermute | solution.py:275
  48.5 6.0 %collective-permute-start.2 = (bf16[256,640]{1,0:T(8,128)(2,1)S(1)}, bf16[256,640]{1,0:T(8,128)(2,1)S(1)}, u32[]{:S(2)}, u32[]{:S(2)}) collective-permute-start(bf16[256,640]{1,0:T(8,128)(2,1)S(1)} %get-tuple-element.48.own), channel_id=1, source_target_pairs={{0,1},{1,0},{2,3},{3,2},{4,5},{5,4},{6,7},{7,6},{8,9},{9,8},{10,11... | collective-permute-start | bytes 983048 | tf_op jit(solution)/shard_map/ppermute | solution.py:275
  48.9 12.3 %collective-permute-start.4 = (bf16[256,640]{1,0:T(8,128)(2,1)S(1)}, bf16[256,640]{1,0:T(8,128)(2,1)S(1)}, u32[]{:S(2)}, u32[]{:S(2)}) collective-permute-start(bf16[256,640]{1,0:T(8,128)(2,1)S(1)} %get-tuple-element.53.own), channel_id=1, source_target_pairs={{0,1},{1,0},{2,3},{3,2},{4,5},{5,4},{6,7},{7,6},{8,9},{9,8},{10,11... | collective-permute-start | bytes 983048 | tf_op jit(solution)/shard_map/ppermute | solution.py:275
  58.9 10.0 %collective-permute-start.3 = (bf16[256,640]{1,0:T(8,128)(2,1)S(1)}, bf16[256,640]{1,0:T(8,128)(2,1)S(1)}, u32[]{:S(2)}, u32[]{:S(2)}) collective-permute-start(bf16[256,640]{1,0:T(8,128)(2,1)S(1)} %get-tuple-element.52), channel_id=1, source_target_pairs={{0,1},{1,0},{2,3},{3,2},{4,5},{5,4},{6,7},{7,6},{8,9},{9,8},{10,11... | collective-permute-start | bytes 983048 | tf_op jit(solution)/shard_map/ppermute | solution.py:275
  65.1 9.7 %collective-permute-start.5 = (bf16[256,640]{1,0:T(8,128)(2,1)S(1)}, bf16[256,640]{1,0:T(8,128)(2,1)S(1)}, u32[]{:S(2)}, u32[]{:S(2)}) collective-permute-start(bf16[256,640]{1,0:T(8,128)(2,1)S(1)} %get-tuple-element.56), channel_id=1, source_target_pairs={{0,1},{1,0},{2,3},{3,2},{4,5},{5,4},{6,7},{7,6},{8,9},{9,8},{10,11... | collective-permute-start | bytes 983048 | tf_op jit(solution)/shard_map/ppermute | solution.py:275
  103.0 7.3 %collective-permute-start.6 = (bf16[256,640]{1,0:T(8,128)(2,1)S(1)}, bf16[256,640]{1,0:T(8,128)(2,1)S(1)}, u32[]{:S(2)}, u32[]{:S(2)}) collective-permute-start(bf16[256,640]{1,0:T(8,128)(2,1)S(1)} %get-tuple-element.60), channel_id=1, source_target_pairs={{0,2},{2,0},{1,3},{3,1},{4,6},{6,4},{5,7},{7,5},{8,10},{10,8},{9,1... | collective-permute-start | bytes 983048 | tf_op jit(solution)/shard_map/ppermute | solution.py:275
  110.9 4.8 %collective-permute-start.7 = (bf16[512,128]{1,0:T(8,128)(2,1)S(1)}, bf16[512,128]{1,0:T(8,128)(2,1)S(1)}, u32[]{:S(2)}, u32[]{:S(2)}) collective-permute-start(bf16[512,128]{1,0:T(8,128)(2,1)S(1)} %get-tuple-element.65), channel_id=1, source_target_pairs={{0,1},{1,0},{2,3},{3,2},{4,5},{5,4},{6,7},{7,6},{8,9},{9,8},{10,11... | collective-permute-start | bytes 393224 | tf_op jit(solution)/shard_map/ppermute | solution.py:275
  116.8 2.5 %collective-permute-start.8 = (bf16[8,40,128]{2,1,0:T(8,128)(2,1)S(1)}, bf16[8,40,128]{2,1,0:T(8,128)(2,1)S(1)}, u32[]{:S(2)}, u32[]{:S(2)}) collective-permute-start(bf16[8,40,128]{2,1,0:T(8,128)(2,1)S(1)} %get-tuple-element.72), channel_id=1, source_target_pairs={{0,2},{2,0},{1,3},{3,1},{4,6},{6,4},{5,7},{7,5},{8,10},{10,8},{9,1... | collective-permute-start | bytes 245768 | tf_op jit(solution)/shard_map/ppermute | solution.py:275

commit v5 on v4

--- a/solution.py
+++ b/solution.py
@@ -20,7 +20,6 @@
 CH = 256
 MIB = 1 << 20
 
-SMEM = pl.BlockSpec(memory_space=pltpu.SMEM)
 VMEM = pl.BlockSpec(memory_space=pltpu.VMEM)
 HBM = pl.BlockSpec(memory_space=pltpu.HBM)
 
@@ -63,7 +62,7 @@
             kernel,
             out_shape=[jax.ShapeDtypeStruct(s, d) for s, d in outs],
             in_specs=[
-                SMEM if a.dtype == I32 else HBM if i in hbm else VMEM for i, a in enumerate(args)
+                HBM if i in hbm else VMEM for i in range(len(args))
             ],
             out_specs=[VMEM for _ in outs],
             scratch_shapes=list(scratch),
@@ -76,7 +75,7 @@
     return run
 
 
-def logits_kernel(ids, tokens_hbm, router_hbm, part, ordered, tokens, router, sems):
+def logits_kernel(tokens_hbm, router_hbm, part, ordered, tokens, router, sems):
     load = pltpu.make_async_copy(router_hbm, router, sems.at[4])
     load.start()
     copies = []
@@ -84,7 +83,7 @@
         at = (i // 2, pl.ds((i % 2) * (M // 2), M // 2))
         copies.append(pltpu.make_async_copy(tokens_hbm.at[at], tokens.at[at], sems.at[i]))
         copies[i].start()
-    order = expert_order(ids[0])
+    order = expert_order(lax.axis_index("core"))
     load.wait()
     r = dot(router[...], order).astype(BF16)
     ordered[...] = r
@@ -94,26 +93,13 @@
         part[b * M : (b + 1) * M, :] = dot(tokens[b], r)
 
 
-def fetch_kernel(grad_hbm, in_hbm, out_hbm, tokens, grad, w_in, w_out, turned, *rest):
-    packing, splitting, merging, unpacking, sems = rest
+def fetch_kernel(grad_hbm, in_hbm, out_hbm, tokens, grad, w_in, w_out, turned, sems):
     pairs = ((grad_hbm, grad), (in_hbm, w_in), (out_hbm, w_out))
     copies = [pltpu.make_async_copy(x, y, sems.at[i]) for i, (x, y) in enumerate(pairs)]
     for c in copies:
         c.start()
     for b in range(B):
         turned[:, b * M : (b + 1) * M] = jnp.transpose(tokens[b])
-    i, j = rows_cols(8 * NQ, 8 * NQ)
-
-    def packed_of_plain(j):
-        return (j & 63) * 8 + (j >> 6)
-
-    def packed_of_split(j):
-        return (j & 63) * 8 + ((j >> 7) & 1) * 4 + (j >> 8) * 2 + ((j >> 6) & 1)
-
-    packing[...] = ones_where(i == packed_of_plain(j))
-    unpacking[...] = ones_where(j == packed_of_plain(i))
-    merging[...] = ones_where(i == packed_of_split(j))
-    splitting[...] = ones_where(j == packed_of_split(i))
     for c in copies:
         c.wait()
 
@@ -135,27 +121,45 @@
             send[k * NQ : (k + 1) * NQ, :] = s[NQ:]
 
 
-def pack_kernel(packing, keep, got, out):
-    n = 4 * NQ
-    out[...] = (dot(packing[:, :n], keep[...]) + dot(packing[:, n:], got[...])).astype(BF16)
-
-
-def split_kernel(splitting, rows, slot_in, slot_grad):
-    n = 4 * NQ
-    slot_in[...] = dot(splitting[:n, :], rows[...]).astype(BF16)
-    slot_grad[...] = dot(splitting[n:, :], rows[...]).astype(BF16)
-
-
-def both_halves(ids):
-    t = ids[1]
+def interleave(pieces, out):
+    i, j = rows_cols(E, E)
+    to = ones_where(i == (j & 15) * 8 + (j >> 4))
+    for g in range(0, NQ, 16):
+        x = jnp.concatenate([x[n + g : n + g + 16, :] for x, n in pieces], axis=0)
+        out[8 * g : 8 * g + E, :] = dot(to, x).astype(BF16)
+
+
+def deinterleave(rows, pieces):
+    i, j = rows_cols(E, E)
+    to = ones_where(j == (i & 15) * 8 + (i >> 4))
+    for g in range(0, NQ, 16):
+        y = dot(to, rows[8 * g : 8 * g + E, :]).astype(BF16)
+        for k, (x, n) in enumerate(pieces):
+            x[n + g : n + g + 16, :] = y[16 * k : 16 * k + 16]
+
+
+def pack_kernel(keep, got, out):
+    interleave([(x, k * NQ) for x in (keep, got) for k in range(4)], out)
+
+
+def by_image(x, y):
+    return [(r, s * 2 * NQ + b * NQ) for s in range(2) for r in (x, y) for b in range(B)]
+
+
+def split_kernel(rows, slot_in, slot_grad):
+    deinterleave(rows, by_image(slot_in, slot_grad))
+
+
+def both_halves():
+    t = lax.axis_index("tp")
     return (
         pl.ds(pl.multiple_of(t * H, 128), H),
         pl.ds(pl.multiple_of((1 - t) * H, 128), H),
     )
 
 
-def up_kernel(ids, own, other, w_in, w_out, slope, out_keep, out_send):
-    mine, theirs = both_halves(ids)
+def up_kernel(own, other, w_in, w_out, slope, out_keep, out_send):
+    mine, theirs = both_halves()
     x, y = own[...], other[...]
     keep = jnp.zeros((4 * NQ, H), F32)
     sent = jnp.zeros((4 * NQ, H), F32)
@@ -174,8 +178,8 @@
     out_send[...] = sent.astype(BF16)
 
 
-def down_kernel(ids, own, other, slope, w_in, w_out, pre_grad, in_keep, in_send):
-    mine, theirs = both_halves(ids)
+def down_kernel(own, other, slope, w_in, w_out, pre_grad, in_keep, in_send):
+    mine, theirs = both_halves()
     x, y = own[...], other[...]
     keep = jnp.zeros((4 * NQ, H), F32)
     sent = jnp.zeros((4 * NQ, H), F32)
@@ -190,23 +194,20 @@
     in_send[...] = sent.astype(BF16)
 
 
-def weight_kernel(ids, own, other, pre_grad, out, done):
-    for x, rows in zip((own, other), both_halves(ids)):
+def weight_kernel(own, other, pre_grad, out, done):
+    for x, rows in zip((own, other), both_halves()):
         out[0, rows, :] = t_dot(x[...], pre_grad[...]).astype(BF16)
     done[...] = jnp.zeros(done.shape, F32)
 
 
-def merge_kernel(merging, out_keep, out_got, in_keep, in_got, done, out):
-    n = 4 * NQ
+def merge_kernel(out_keep, out_got, in_keep, in_got, done, out):
     x = (out_keep[...] + out_got[...].astype(F32)).astype(BF16)
     y = (in_keep[...] + in_got[...].astype(F32)).astype(BF16)
-    out[...] = (dot(merging[:, :n], x) + dot(merging[:, n:], y)).astype(BF16)
-
-
-def unpack_kernel(unpacking, rows, own, send):
-    n = 4 * NQ
-    own[...] = dot(unpacking[:n, :], rows[...]).astype(BF16)
-    send[...] = dot(unpacking[n:, :], rows[...]).astype(BF16)
+    interleave(by_image(x, y), out)
+
+
+def unpack_kernel(rows, own, send):
+    deinterleave(rows, [(x, k * NQ) for x in (own, send) for k in range(4)])
 
 
 def slots_of(own, got, a, b):
@@ -233,16 +234,14 @@
     done[...] = jnp.zeros(done.shape, F32)
 
 
-def logit_kernel(ids, part, got, turned, done, logit, keep, send, whole):
+def logit_kernel(part, got, turned, done, logit, out):
     g = (part[...] + got[...].astype(F32)).astype(BF16)
     logit[...] = g
-    plain = dot_t(g, expert_order(ids[0])).astype(BF16)
-    whole[...] = dot(turned[...], plain)
-    c = ids[0]
+    plain = dot_t(g, expert_order(lax.axis_index("core"))).astype(BF16)
+    total = dot(turned[...], plain)
     n = H // 16
-    for i in range(8):
-        keep[i] = whole[pl.ds(pl.multiple_of((2 * i + c) * n, 8), n), :]
-        send[i] = whole[pl.ds(pl.multiple_of((2 * i + 1 - c) * n, 8), n), :].astype(BF16)
+    for i in range(16):
+        out[i] = total[i * n : (i + 1) * n, :].astype(BF16)
 
 
 def tokens_kernel(first, logit, router, out, done):
@@ -252,15 +251,21 @@
     done[...] = jnp.zeros(done.shape, F32)
 
 
-def add_kernel(x, y, done, out):
-    out[...] = (x[...] + y[...].astype(F32)).astype(BF16)
-
-
-def spread_kernel(x, out):
+def sum_blocks(x):
     total = x[0].astype(F32)
-    for i in range(1, 8):
+    for i in range(1, x.shape[0]):
         total = total + x[i].astype(F32)
-    total = total.astype(BF16)
+    return total.astype(BF16)
+
+
+def early_kernel(x, done, out):
+    total = sum_blocks(x)
+    for i in range(out.shape[0]):
+        out[i] = total
+
+
+def late_kernel(x, out):
+    total = sum_blocks(x)
     for i in range(out.shape[0]):
         out[i] = total
 
@@ -280,7 +285,6 @@
 
 
 def on_device(tokens, router, w_in, w_out, grad_out):
-    ids = jnp.stack([lax.axis_index("core"), lax.axis_index("tp")]).astype(I32)
     half = ((4 * NQ, H), BF16)
     half32 = ((4 * NQ, H), F32)
     done = ((8, E), F32)
@@ -290,15 +294,13 @@
         [((B * M, E), F32), ((H, E), BF16), ((B, M, H), BF16)],
         small,
         1e6,
-        hbm=(1, 2),
+        hbm=(0, 1),
         scratch=[pltpu.VMEM((H, E), BF16), pltpu.SemaphoreType.DMA((5,))],
-    )(ids, tokens, router)
+    )(tokens, router)
     other = swap(part, "tp")
-    onehot = ((8 * NQ, 8 * NQ), BF16)
-    grad_out, w_in, w_out, turned, packing, splitting, merging, unpacking = call(
+    grad_out, w_in, w_out, turned = call(
         fetch_kernel,
-        [((B, M, H), BF16), ((1, D, FH), BF16), ((1, FH, D), BF16), ((H, B * M), BF16)]
-        + [onehot] * 4,
+        [((B, M, H), BF16), ((1, D, FH), BF16), ((1, FH, D), BF16), ((H, B * M), BF16)],
         0,
         1.4e7,
         hbm=(0, 1, 2),
@@ -308,27 +310,27 @@
         slots_kernel, [((B * M, E), F32)] * 2 + [half] * 2, 2 * small, 3e6
     )(part, other, tokens, grad_out)
     got = swap(send, "core")
-    (packed,) = call(pack_kernel, [((8 * NQ, H), BF16)], 3e8, 1.3e6)(packing, keep, got)
+    (packed,) = call(pack_kernel, [((8 * NQ, H), BF16)], 3e8, 1.3e6)(keep, got)
     rows = exchange(packed.reshape(NQ, 8, H), CHIPS).reshape(8 * NQ, H)
-    in_own, grad_own = call(split_kernel, [half] * 2, 3e8, 1.3e6)(splitting, rows)
+    in_own, grad_own = call(split_kernel, [half] * 2, 3e8, 1.3e6)(rows)
     in_other = swap(in_own, "tp")
     grad_other = swap(grad_own, "tp")
     slope, out_keep, out_send = call(
         up_kernel, [((4 * NQ, FH), F32), half32, half], 1.7e9, 1e7
-    )(ids, in_own, in_other, w_in, w_out)
+    )(in_own, in_other, w_in, w_out)
     out_got = swap(out_send, "tp")
     pre_grad, in_keep, in_send = call(
         down_kernel, [((4 * NQ, FH), BF16), half32, half], 1.7e9, 1e7
-    )(ids, grad_own, grad_other, slope, w_in, w_out)
+    )(grad_own, grad_other, slope, w_in, w_out)
     in_got = swap(in_send, "tp")
     grad_weight, weight_done = call(weight_kernel, [((1, D, FH), BF16), done], 8.4e8, 5e6)(
-        ids, in_own, in_other, pre_grad
+        in_own, in_other, pre_grad
     )
     (merged,) = call(merge_kernel, [((8 * NQ, H), BF16)], 3e8, 2.6e6)(
-        merging, out_keep, out_got, in_keep, in_got, weight_done
+        out_keep, out_got, in_keep, in_got, weight_done
     )
     rows = exchange(merged.reshape(NQ, 8, H), CHIPS).reshape(8 * NQ, H)
-    own, send = call(unpack_kernel, [half] * 2, 3e8, 1.3e6)(unpacking, rows)
+    own, send = call(unpack_kernel, [half] * 2, 3e8, 1.3e6)(rows)
     got = swap(send, "core")
     part, send = call(
         dots_kernel, [((B * M, E), F32), ((B * M, E), BF16)], 2 * small, 3e6
@@ -338,25 +340,20 @@
         own, got, dispatch
     )
     eight = ((8, H // 16, E), BF16)
-    eight32 = ((8, H // 16, E), F32)
-    logit, keep, send = call(
-        logit_kernel,
-        [((B * M, E), BF16), eight32, eight],
-        small,
-        3e6,
-        scratch=[pltpu.VMEM((H, E), F32)],
-    )(ids, part, logit_got, turned, first_done)
-    got = swap(send, "core")
+    sixteen = ((16, H // 16, E), BF16)
+    plane = ("x_hi", "y", "core")
+    logit, blocks = call(logit_kernel, [((B * M, E), BF16), sixteen], small, 3e6)(
+        part, logit_got, turned, first_done
+    )
+    blocks = exchange(blocks, plane)
     grad_tokens, tokens_done = call(
         tokens_kernel, [((B, M, H), BF16), done], small, 3e6
     )(first, logit, ordered)
-    (summed,) = call(add_kernel, [eight], 1e5, 5e5)(keep, got, tokens_done)
-    summed = exchange(summed, ("x_hi", "y"))
-    (summed,) = call(spread_kernel, [eight], 1e5, 5e5)(summed)
-    summed = exchange(summed, ("z0", "z1", "z2"))
-    (summed,) = call(spread_kernel, [((16, H // 16, E), BF16)], 1e5, 5e5)(summed)
-    summed = exchange(summed, ("x_hi", "y", "core"))
-    (grad_router,) = call(widen_kernel, [((H, E), F32)], 1e5, 5e5)(summed)
+    (blocks,) = call(early_kernel, [eight], 1e5, 5e5)(blocks, tokens_done)
+    blocks = exchange(blocks, ("z0", "z1", "z2"))
+    (blocks,) = call(late_kernel, [sixteen], 1e5, 5e5)(blocks)
+    blocks = exchange(blocks, plane)
+    (grad_router,) = call(widen_kernel, [((H, E), F32)], 1e5, 5e5)(blocks)
     return grad_tokens, grad_router, grad_weight
 
 

time: 154 us -> 152 us (0.987)
  blocking collectives: 93.1 us -> 81.6 us
  waiting for transfers between devices: 20.3 us -> 28.9 us
  starting transfers between devices: 15.2 us -> 19.9 us
  Pallas kernels: 24 us -> 20.8 us
    all_to_all x5 -> x4, blocking collectives: 93.1 us -> 81.6 us  [exchange(): return lax.all_to_all(x, axes, split_axis=0, concat_axis=0, tiled=True)]
    all_to_all x0 -> x1, waiting for transfers between devices: none -> 6.78 us  [exchange(): return lax.all_to_all(x, axes, split_axis=0, concat_axis=0, tiled=True)]
    all_to_all x0 -> x1, starting transfers between devices: none -> 6.2 us  [exchange(): return lax.all_to_all(x, axes, split_axis=0, concat_axis=0, tiled=True)]
    pallas_call x18 -> x17, Pallas kernels: 24 us -> 20.8 us  [run(): pl.pallas_call(kernel, out_shape=[jax.ShapeDtypeStruct(s, d) for s, d in...]
    ppermute x9 -> x8, waiting for transfers between devices: 20.3 us -> 22.2 us  [swap(): return lax.ppermute(x, axis, [(0, 1), (1, 0)])]
    ppermute x9 -> x8, starting transfers between devices: 15.2 us -> 13.7 us  [swap(): return lax.ppermute(x, axis, [(0, 1), (1, 0)])]
  transfers between devices with their start and end apart: 9 -> 9, of which waited for: 7 -> 9; matrix products, arithmetic and copies ran while one was open for 0% -> 0% of each run, Pallas kernels for 11% -> 10%
where the time goes in v5:
time: 152 us
  blocking collectives  81.6 us (54%)
  waiting for transfers between devices  28.9 us (19%)
  Pallas kernels  20.8 us (14%)
  starting transfers between devices  19.9 us (13%)
    all_to_all x4, blocking collectives, exchange(): return lax.all_to_all(x, axes, split_axis=0, concat_axis=0, tiled=True)  81.6 us
    ppermute x8, waiting for transfers between devices, swap(): return lax.ppermute(x, axis, [(0, 1), (1, 0)])  22.2 us
    pallas_call x17, Pallas kernels, run(): pl.pallas_call(kernel, out_shape=[jax.ShapeDtypeStruct(s, d) for s, d in...  20.8 us
    ppermute x8, starting transfers between devices, swap(): return lax.ppermute(x, axis, [(0, 1), (1, 0)])  13.7 us
    all_to_all x1, waiting for transfers between devices, exchange(): return lax.all_to_all(x, axes, split_axis=0, concat_axis=0, tiled=True)  6.78 us
    all_to_all x1, starting transfers between devices, exchange(): return lax.all_to_all(x, axes, split_axis=0, concat_axis=0, tiled=True)  6.2 us
  transfers between devices with their start and end apart: 9, of which 9 were waited for; matrix products, arithmetic and copies ran while one was open for 0% of the time, Pallas kernels for 10%

profile of v5, /device:TPU:1, one launch (start us, length us, event | category | flops | bytes accessed | tf_op | source)
XLA Modules:
  0.0 151.9 jit_solution(2951141892733467128)
XLA Ops:
  0.6 1.7 %shard_map.76 = (f32[512,128]{1,0:T(8,128)S(1)}, bf16[640,128]{1,0:T(8,128)(2,1)S(1)}, bf16[2,256,640]{2,1,0:T(8,128)(2,1)S(1)}) custom-call(bf16[2,256,640]{2,1,0:T(8,128)(2,1)} %tokens_hbm.1, bf16[640,128]{1,0:T(8,128)(2,1)} %router_hbm.1), custom_call_target="tpu_custom_call" | custom-call | flops 83886080 | bytes 1000000 | tf_op jit(solution)/shard_map/pallas_call | solution.py:61
  2.3 2.1 %collective-permute-start = (f32[512,128]{1,0:T(8,128)S(1)}, f32[512,128]{1,0:T(8,128)S(1)}, u32[]{:S(2)}, u32[]{:S(2)}) collective-permute-start(f32[512,128]{1,0:T(8,128)S(1)} %get-tuple-element.34.part), channel_id=1, source_target_pairs={{0,1},{1,0},{2,3},{3,2},{4,5},{5,4},{6,7},{7,6},{8,9},{9,8},{10,11... | collective-permute-start | bytes 786440 | tf_op jit(solution)/shard_map/ppermute | solution.py:280
  4.5 3.2 %shard_map.77 = (bf16[2,256,640]{2,1,0:T(8,128)(2,1)S(1)}, bf16[1,1280,1280]{2,1,0:T(8,128)(2,1)S(1)}, bf16[1,1280,1280]{2,1,0:T(8,128)(2,1)S(1)}, bf16[640,512]{1,0:T(8,128)(2,1)S(1)}) custom-call(bf16[2,256,640]{2,1,0:T(8,128)(2,1)} %grad_hbm.1, bf16[1,1280,1280]{2,1,0:T(8,128)(2,1)} %in_hbm.1, bf16[1,1280,1280]{2,1,0:T(8,128)(2,1)} %out_hbm.1, ...), custom_call_target="tpu_custom_call" | custom-call | bytes 14000000 | tf_op jit(solution)/shard_map/pallas_call | solution.py:61
  7.6 1.5 collective-permute-done.other
  9.1 0.7 shard_map.78
  9.8 3.0 %collective-permute-start.1 = (bf16[256,640]{1,0:T(8,128)(2,1)S(1)}, bf16[256,640]{1,0:T(8,128)(2,1)S(1)}, u32[]{:S(2)}, u32[]{:S(2)}) collective-permute-start(bf16[256,640]{1,0:T(8,128)(2,1)S(1)} %get-tuple-element.38), channel_id=1, source_target_pairs={{0,2},{2,0},{1,3},{3,1},{4,6},{6,4},{5,7},{7,5},{8,10},{10,8},{9,1... | collective-permute-start | bytes 983048 | tf_op jit(solution)/shard_map/ppermute | solution.py:280
  12.8 1.3 collective-permute-done.1.got
  14.0 0.3 shard_map.79
  14.4 32.7 %all_to_all.25 = bf16[64,8,640]{2,1,0:T(8,128)(2,1)S(1)} all-to-all(bf16[64,8,640]{2,1,0:T(8,128)(2,1)S(1)} %bitcast.5), channel_id=1, replica_groups=mesh['z2'=2,'z1'=2,'z0'=2,'x_hi'=2,'y'=4,'core'=2,'tp'=2] {'z2','z1','z0..., dimensions={0} | all-to-all | bytes 1310720 | tf_op jit(solution)/shard_map/all_to_all | solution.py:284
  47.1 0.3 shard_map.80
  47.4 0.3 collective-permute-start.2
  47.7 1.2 collective-permute-start.4
  48.9 4.5 %collective-permute-done.2.other = bf16[256,640]{1,0:T(8,128)(2,1)S(1)} collective-permute-done((bf16[256,640]{1,0:T(8,128)(2,1)S(1)}, bf16[256,640]{1,0:T(8,128)(2,1)S(1)}, u32[]{:S(2)}, u32[]{:S(2)}) %collective-permute-start.2) | collective-permute-done | bytes 327712 | tf_op jit(solution)/shard_map/ppermute | solution.py:280
  53.4 3.8 %shard_map.81 = (f32[256,1280]{1,0:T(8,128)S(1)}, f32[256,640]{1,0:T(8,128)S(1)}, bf16[256,640]{1,0:T(8,128)(2,1)S(1)}) custom-call(bf16[256,640]{1,0:T(8,128)(2,1)S(1)} %get-tuple-element.39.own, bf16[256,640]{1,0:T(8,128)(2,1)S(1)} %collective-permute-done.2.other, bf16[1,1280,1280]{2,1,0:T(8,128)(2,1)S(1)} %get-tuple-element.40.w_in, ...), custom_call_target="tpu_custom_call" | custom-call | flops 1700000000 | bytes 10000000 | tf_op jit(solution)/shard_map/pallas_call | solution.py:61
  57.2 0.3 collective-permute-start.3
  57.6 2.5 %collective-permute-done.4.other = bf16[256,640]{1,0:T(8,128)(2,1)S(1)} collective-permute-done((bf16[256,640]{1,0:T(8,128)(2,1)S(1)}, bf16[256,640]{1,0:T(8,128)(2,1)S(1)}, u32[]{:S(2)}, u32[]{:S(2)}) %collective-permute-start.4) | collective-permute-done | bytes 327712 | tf_op jit(solution)/shard_map/ppermute | solution.py:280
  60.1 3.3 %shard_map.82 = (bf16[256,1280]{1,0:T(8,128)(2,1)S(1)}, f32[256,640]{1,0:T(8,128)S(1)}, bf16[256,640]{1,0:T(8,128)(2,1)S(1)}) custom-call(bf16[256,640]{1,0:T(8,128)(2,1)S(1)} %get-tuple-element.44.own, bf16[256,640]{1,0:T(8,128)(2,1)S(1)} %collective-permute-done.4.other, f32[256,1280]{1,0:T(8,128)S(1)} %get-tuple-element.45.slope, ...), custom_call_target="tpu_custom_call" | custom-call | flops 1700000000 | bytes 10000000 | tf_op jit(solution)/shard_map/pallas_call | solution.py:61
  63.4 0.3 collective-permute-start.5
  63.7 2.7 %shard_map.83 = (bf16[1,1280,1280]{2,1,0:T(8,128)(2,1)}, f32[8,128]{1,0:T(8,128)S(1)}) custom-call(bf16[256,640]{1,0:T(8,128)(2,1)S(1)} %get-tuple-element.39.own, bf16[256,640]{1,0:T(8,128)(2,1)S(1)} %collective-permute-done.2.other, bf16[256,1280]{1,0:T(8,128)(2,1)S(1)} %get-tuple-element.48.pre_grad), custom_call_target="tpu_custom_call" | custom-call | flops 840000000 | bytes 5000000 | tf_op jit(solution)/shard_map/pallas_call | solution.py:61
  66.4 0.7 collective-permute-done.3.out_got
  67.1 6.5 %collective-permute-done.5.in_got = bf16[256,640]{1,0:T(8,128)(2,1)S(1)} collective-permute-done((bf16[256,640]{1,0:T(8,128)(2,1)S(1)}, bf16[256,640]{1,0:T(8,128)(2,1)S(1)}, u32[]{:S(2)}, u32[]{:S(2)}) %collective-permute-start.5) | collective-permute-done | bytes 327712 | tf_op jit(solution)/shard_map/ppermute | solution.py:280
  73.6 0.3 shard_map.84
  73.9 27.3 %all_to_all.26 = bf16[64,8,640]{2,1,0:T(8,128)(2,1)S(1)} all-to-all(bf16[64,8,640]{2,1,0:T(8,128)(2,1)S(1)} %bitcast.4), channel_id=1, replica_groups=mesh['z2'=2,'z1'=2,'z0'=2,'x_hi'=2,'y'=4,'core'=2,'tp'=2] {'z2','z1','z0..., dimensions={0} | all-to-all | bytes 1310720 | tf_op jit(solution)/shard_map/all_to_all | solution.py:284
  101.2 0.3 shard_map.85
  101.6 6.1 %collective-permute-start.6 = (bf16[256,640]{1,0:T(8,128)(2,1)S(1)}, bf16[256,640]{1,0:T(8,128)(2,1)S(1)}, u32[]{:S(2)}, u32[]{:S(2)}) collective-permute-start(bf16[256,640]{1,0:T(8,128)(2,1)S(1)} %get-tuple-element.51), channel_id=1, source_target_pairs={{0,2},{2,0},{1,3},{3,1},{4,6},{6,4},{5,7},{7,5},{8,10},{10,8},{9,1... | collective-permute-start | bytes 983048 | tf_op jit(solution)/shard_map/ppermute | solution.py:280
  107.6 1.3 collective-permute-done.6.got
  108.9 0.5 shard_map.87
  109.4 0.4 collective-permute-start.7
  109.8 0.3 shard_map.86
  110.2 4.1 %collective-permute-done.7.got = bf16[512,128]{1,0:T(8,128)(2,1)S(1)} collective-permute-done((bf16[512,128]{1,0:T(8,128)(2,1)S(1)}, bf16[512,128]{1,0:T(8,128)(2,1)S(1)}, u32[]{:S(2)}, u32[]{:S(2)}) %collective-permute-start.7) | collective-permute-done | bytes 131104 | tf_op jit(solution)/shard_map/ppermute | solution.py:280
  114.2 1.2 shard_map.88
  115.4 6.2 %all-to-all-start.2 = ((bf16[16,40,128]{2,1,0:T(8,128)(2,1)}), bf16[16,40,128]{2,1,0:T(8,128)(2,1)S(1)}, u32[]{:S(2)}, u32[]{:S(2)}) async-start(bf16[16,40,128]{2,1,0:T(8,128)(2,1)} %get-tuple-element.62), calls=%async_computation.2 | async-start | bytes 327680 | tf_op jit(solution)/shard_map/all_to_all | solution.py:284
  121.6 1.2 shard_map.89
  122.8 6.8 %all-to-all-done.2.x = bf16[16,40,128]{2,1,0:T(8,128)(2,1)S(1)} async-done(((bf16[16,40,128]{2,1,0:T(8,128)(2,1)}), bf16[16,40,128]{2,1,0:T(8,128)(2,1)S(1)}, u32[]{:S(2)}, u32[]{:S(2)}) %all-to-all-start.2) | async-done | bytes 163872 | tf_op jit(solution)/shard_map/all_to_all | solution.py:284
  129.6 9.1 %all_to_all.27.x = bf16[8,40,128]{2,1,0:T(8,128)(2,1)S(1)} all-to-all(bf16[8,40,128]{2,1,0:T(8,128)(2,1)S(1)} %shard_map.90), channel_id=1, replica_groups=mesh['z2'=2,'z1'=2,'z0'=2,'x_hi'=2,'y'=4,'core'=2,'tp'=2] {'z0','z1','z2'}, dimensions={0} | all-to-all | bytes 163840 | tf_op jit(solution)/shard_map/all_to_all | solution.py:284
  138.7 12.5 %all_to_all.28.x = bf16[16,40,128]{2,1,0:T(8,128)(2,1)S(1)} all-to-all(bf16[16,40,128]{2,1,0:T(8,128)(2,1)S(1)} %shard_map.91), channel_id=1, replica_groups=mesh['z2'=2,'z1'=2,'z0'=2,'x_hi'=2,'y'=4,'core'=2,'tp'=2] {'x_hi','y','c..., dimensions={0} | all-to-all | bytes 327680 | tf_op jit(solution)/shard_map/all_to_all | solution.py:284
  151.2 0.7 shard_map.92
  (2 shorter events, 0.1 us)
Async XLA Ops:
  2.3 6.8 %collective-permute-start = (f32[512,128]{1,0:T(8,128)S(1)}, f32[512,128]{1,0:T(8,128)S(1)}, u32[]{:S(2)}, u32[]{:S(2)}) collective-permute-start(f32[512,128]{1,0:T(8,128)S(1)} %get-tuple-element.34.part), channel_id=1, source_target_pairs={{0,1},{1,0},{2,3},{3,2},{4,5},{5,4},{6,7},{7,6},{8,9},{9,8},{10,11... | collective-permute-start | bytes 786440 | tf_op jit(solution)/shard_map/ppermute | solution.py:280
  9.8 4.2 %collective-permute-start.1 = (bf16[256,640]{1,0:T(8,128)(2,1)S(1)}, bf16[256,640]{1,0:T(8,128)(2,1)S(1)}, u32[]{:S(2)}, u32[]{:S(2)}) collective-permute-start(bf16[256,640]{1,0:T(8,128)(2,1)S(1)} %get-tuple-element.38), channel_id=1, source_target_pairs={{0,2},{2,0},{1,3},{3,1},{4,6},{6,4},{5,7},{7,5},{8,10},{10,8},{9,1... | collective-permute-start | bytes 983048 | tf_op jit(solution)/shard_map/ppermute | solution.py:280
  47.4 6.0 %collective-permute-start.2 = (bf16[256,640]{1,0:T(8,128)(2,1)S(1)}, bf16[256,640]{1,0:T(8,128)(2,1)S(1)}, u32[]{:S(2)}, u32[]{:S(2)}) collective-permute-start(bf16[256,640]{1,0:T(8,128)(2,1)S(1)} %get-tuple-element.39.own), channel_id=1, source_target_pairs={{0,1},{1,0},{2,3},{3,2},{4,5},{5,4},{6,7},{7,6},{8,9},{9,8},{10,11... | collective-permute-start | bytes 983048 | tf_op jit(solution)/shard_map/ppermute | solution.py:280
  47.7 12.3 %collective-permute-start.4 = (bf16[256,640]{1,0:T(8,128)(2,1)S(1)}, bf16[256,640]{1,0:T(8,128)(2,1)S(1)}, u32[]{:S(2)}, u32[]{:S(2)}) collective-permute-start(bf16[256,640]{1,0:T(8,128)(2,1)S(1)} %get-tuple-element.44.own), channel_id=1, source_target_pairs={{0,1},{1,0},{2,3},{3,2},{4,5},{5,4},{6,7},{7,6},{8,9},{9,8},{10,11... | collective-permute-start | bytes 983048 | tf_op jit(solution)/shard_map/ppermute | solution.py:280
  57.2 9.8 %collective-permute-start.3 = (bf16[256,640]{1,0:T(8,128)(2,1)S(1)}, bf16[256,640]{1,0:T(8,128)(2,1)S(1)}, u32[]{:S(2)}, u32[]{:S(2)}) collective-permute-start(bf16[256,640]{1,0:T(8,128)(2,1)S(1)} %get-tuple-element.43), channel_id=1, source_target_pairs={{0,1},{1,0},{2,3},{3,2},{4,5},{5,4},{6,7},{7,6},{8,9},{9,8},{10,11... | collective-permute-start | bytes 983048 | tf_op jit(solution)/shard_map/ppermute | solution.py:280
  63.4 10.2 %collective-permute-start.5 = (bf16[256,640]{1,0:T(8,128)(2,1)S(1)}, bf16[256,640]{1,0:T(8,128)(2,1)S(1)}, u32[]{:S(2)}, u32[]{:S(2)}) collective-permute-start(bf16[256,640]{1,0:T(8,128)(2,1)S(1)} %get-tuple-element.47), channel_id=1, source_target_pairs={{0,1},{1,0},{2,3},{3,2},{4,5},{5,4},{6,7},{7,6},{8,9},{9,8},{10,11... | collective-permute-start | bytes 983048 | tf_op jit(solution)/shard_map/ppermute | solution.py:280
  101.6 7.3 %collective-permute-start.6 = (bf16[256,640]{1,0:T(8,128)(2,1)S(1)}, bf16[256,640]{1,0:T(8,128)(2,1)S(1)}, u32[]{:S(2)}, u32[]{:S(2)}) collective-permute-start(bf16[256,640]{1,0:T(8,128)(2,1)S(1)} %get-tuple-element.51), channel_id=1, source_target_pairs={{0,2},{2,0},{1,3},{3,1},{4,6},{6,4},{5,7},{7,5},{8,10},{10,8},{9,1... | collective-permute-start | bytes 983048 | tf_op jit(solution)/shard_map/ppermute | solution.py:280
  109.4 4.8 %collective-permute-start.7 = (bf16[512,128]{1,0:T(8,128)(2,1)S(1)}, bf16[512,128]{1,0:T(8,128)(2,1)S(1)}, u32[]{:S(2)}, u32[]{:S(2)}) collective-permute-start(bf16[512,128]{1,0:T(8,128)(2,1)S(1)} %get-tuple-element.56), channel_id=1, source_target_pairs={{0,1},{1,0},{2,3},{3,2},{4,5},{5,4},{6,7},{7,6},{8,9},{9,8},{10,11... | collective-permute-start | bytes 393224 | tf_op jit(solution)/shard_map/ppermute | solution.py:280
  115.4 14.1 %all-to-all-start.2 = ((bf16[16,40,128]{2,1,0:T(8,128)(2,1)}), bf16[16,40,128]{2,1,0:T(8,128)(2,1)S(1)}, u32[]{:S(2)}, u32[]{:S(2)}) async-start(bf16[16,40,128]{2,1,0:T(8,128)(2,1)} %get-tuple-element.62), calls=%async_computation.2 | async-start | bytes 327680 | tf_op jit(solution)/shard_map/all_to_all | solution.py:284

commit v6 on v5

--- a/solution.py
+++ b/solution.py
@@ -52,7 +52,7 @@
     return ones_where(e == 2 * (p & 63) + (core ^ (p >> 6)))
 
 
-def call(kernel, outs, flops, nbytes, hbm=(), scratch=(), limit=24):
+def call(kernel, outs, flops, nbytes, hbm=(), scratch=(), out_space=VMEM, limit=24):
     def run(*args):
         args = [
             pltpu.with_memory_space_constraint(a, pltpu.HBM) if i in hbm else a
@@ -64,7 +64,7 @@
             in_specs=[
                 HBM if i in hbm else VMEM for i in range(len(args))
             ],
-            out_specs=[VMEM for _ in outs],
+            out_specs=[out_space for _ in outs],
             scratch_shapes=list(scratch),
             cost_estimate=pl.CostEstimate(
                 flops=int(flops), bytes_accessed=int(nbytes), transcendentals=0
@@ -86,7 +86,7 @@
     order = expert_order(lax.axis_index("core"))
     load.wait()
     r = dot(router[...], order).astype(BF16)
-    ordered[...] = r
+    ordered[...] = jnp.transpose(r)
     for b in range(B):
         copies[2 * b].wait()
         copies[2 * b + 1].wait()
@@ -158,11 +158,9 @@
     )
 
 
-def up_kernel(own, other, w_in, w_out, slope, out_keep, out_send):
+def up_kernel(own, other, w_in, w_out, slope, out_keep, out_send, total):
     mine, theirs = both_halves()
     x, y = own[...], other[...]
-    keep = jnp.zeros((4 * NQ, H), F32)
-    sent = jnp.zeros((4 * NQ, H), F32)
     for f in range(0, FH, CH):
         cols = slice(f, f + CH)
         v = dot(x, w_in[0, mine, cols]) + dot(y, w_in[0, theirs, cols])
@@ -172,26 +170,24 @@
         slope[:, cols] = 0.5 * (1.0 + t) + 0.5 * v * (1.0 - t * t) * (
             0.7978845608 * (1.0 + 0.134145 * sq)
         )
-        keep = keep + dot(act, w_out[0, cols, mine])
-        sent = sent + dot(act, w_out[0, cols, theirs])
-    out_keep[...] = keep
-    out_send[...] = sent.astype(BF16)
-
-
-def down_kernel(own, other, slope, w_in, w_out, pre_grad, in_keep, in_send):
+        p = dot(act, w_out[0, cols, :])
+        total[...] = p if f == 0 else total[...] + p
+    out_keep[...] = total[:, mine]
+    out_send[...] = total[:, theirs].astype(BF16)
+
+
+def down_kernel(own, other, slope, w_in, w_out, pre_grad, in_keep, in_send, total):
     mine, theirs = both_halves()
     x, y = own[...], other[...]
-    keep = jnp.zeros((4 * NQ, H), F32)
-    sent = jnp.zeros((4 * NQ, H), F32)
     for f in range(0, FH, CH):
         cols = slice(f, f + CH)
         g = dot_t(x, w_out[0, cols, mine]) + dot_t(y, w_out[0, cols, theirs])
         g = (g * slope[:, cols]).astype(BF16)
         pre_grad[:, cols] = g
-        keep = keep + dot_t(g, w_in[0, mine, cols])
-        sent = sent + dot_t(g, w_in[0, theirs, cols])
-    in_keep[...] = keep
-    in_send[...] = sent.astype(BF16)
+        p = dot_t(g, w_in[0, :, cols])
+        total[...] = p if f == 0 else total[...] + p
+    in_keep[...] = total[:, mine]
+    in_send[...] = total[:, theirs].astype(BF16)
 
 
 def weight_kernel(own, other, pre_grad, out, done):
@@ -244,13 +240,6 @@
         out[i] = total[i * n : (i + 1) * n, :].astype(BF16)
 
 
-def tokens_kernel(first, logit, router, out, done):
-    for b in range(B):
-        g = first[b] + dot_t(logit[b * M : (b + 1) * M, :], router[...])
-        out[b] = g.astype(BF16)
-    done[...] = jnp.zeros(done.shape, F32)
-
-
 def sum_blocks(x):
     total = x[0].astype(F32)
     for i in range(1, x.shape[0]):
@@ -258,22 +247,26 @@
     return total.astype(BF16)
 
 
-def early_kernel(x, done, out):
+def spread_kernel(x, out):
     total = sum_blocks(x)
     for i in range(out.shape[0]):
         out[i] = total
 
 
-def late_kernel(x, out):
-    total = sum_blocks(x)
-    for i in range(out.shape[0]):
-        out[i] = total
-
-
-def widen_kernel(x, out):
+def last_kernel(x, first, logit, ordered, router_hbm, tokens_hbm, router, tokens, sems):
+    copies = []
+    for b in range(B):
+        g = first[b] + dot(logit[b * M : (b + 1) * M, :], ordered[...])
+        tokens[b] = g.astype(BF16)
+        copies.append(pltpu.make_async_copy(tokens.at[b], tokens_hbm.at[b], sems.at[b]))
+        copies[b].start()
     n = H // 16
     for i in range(16):
-        out[i * n : (i + 1) * n, :] = x[i].astype(F32)
+        router[i * n : (i + 1) * n, :] = x[i].astype(F32)
+    copies.append(pltpu.make_async_copy(router, router_hbm, sems.at[2]))
+    copies[2].start()
+    for c in copies:
+        c.wait()
 
 
 def swap(x, axis):
@@ -287,11 +280,12 @@
 def on_device(tokens, router, w_in, w_out, grad_out):
     half = ((4 * NQ, H), BF16)
     half32 = ((4 * NQ, H), F32)
+    total = [pltpu.VMEM((4 * NQ, D), F32)]
     done = ((8, E), F32)
     small = 2 * B * M * H * E
     part, ordered, tokens = call(
         logits_kernel,
-        [((B * M, E), F32), ((H, E), BF16), ((B, M, H), BF16)],
+        [((B * M, E), F32), ((E, H), BF16), ((B, M, H), BF16)],
         small,
         1e6,
         hbm=(0, 1),
@@ -316,11 +310,11 @@
     in_other = swap(in_own, "tp")
     grad_other = swap(grad_own, "tp")
     slope, out_keep, out_send = call(
-        up_kernel, [((4 * NQ, FH), F32), half32, half], 1.7e9, 1e7
+        up_kernel, [((4 * NQ, FH), F32), half32, half], 1.7e9, 1e7, scratch=total
     )(in_own, in_other, w_in, w_out)
     out_got = swap(out_send, "tp")
     pre_grad, in_keep, in_send = call(
-        down_kernel, [((4 * NQ, FH), BF16), half32, half], 1.7e9, 1e7
+        down_kernel, [((4 * NQ, FH), BF16), half32, half], 1.7e9, 1e7, scratch=total
     )(grad_own, grad_other, slope, w_in, w_out)
     in_got = swap(in_send, "tp")
     grad_weight, weight_done = call(weight_kernel, [((1, D, FH), BF16), done], 8.4e8, 5e6)(
@@ -346,14 +340,22 @@
         part, logit_got, turned, first_done
     )
     blocks = exchange(blocks, plane)
-    grad_tokens, tokens_done = call(
-        tokens_kernel, [((B, M, H), BF16), done], small, 3e6
-    )(first, logit, ordered)
-    (blocks,) = call(early_kernel, [eight], 1e5, 5e5)(blocks, tokens_done)
+    (blocks,) = call(spread_kernel, [eight], 1e5, 5e5)(blocks)
     blocks = exchange(blocks, ("z0", "z1", "z2"))
-    (blocks,) = call(late_kernel, [sixteen], 1e5, 5e5)(blocks)
+    (blocks,) = call(spread_kernel, [sixteen], 1e5, 5e5)(blocks)
     blocks = exchange(blocks, plane)
-    (grad_router,) = call(widen_kernel, [((H, E), F32)], 1e5, 5e5)(blocks)
+    grad_router, grad_tokens = call(
+        last_kernel,
+        [((H, E), F32), ((B, M, H), BF16)],
+        small,
+        3e6,
+        scratch=[
+            pltpu.VMEM((H, E), F32),
+            pltpu.VMEM((B, M, H), BF16),
+            pltpu.SemaphoreType.DMA((3,)),
+        ],
+        out_space=HBM,
+    )(blocks, first, logit, ordered)
     return grad_tokens, grad_router, grad_weight
 
 

time: 152 us -> 152 us (level)
  blocking collectives: 81.6 us -> 95.1 us
  starting transfers between devices: 19.9 us -> 13.9 us
  waiting for transfers between devices: 28.9 us -> 24 us
  Pallas kernels: 20.8 us -> 18.1 us
    all_to_all x4 -> x5, blocking collectives: 81.6 us -> 95.1 us  [exchange(): return lax.all_to_all(x, axes, split_axis=0, concat_axis=0, tiled=True)]
    all_to_all x1 -> x0, waiting for transfers between devices: 6.78 us -> none  [exchange(): return lax.all_to_all(x, axes, split_axis=0, concat_axis=0, tiled=True)]
    all_to_all x1 -> x0, starting transfers between devices: 6.2 us -> none  [exchange(): return lax.all_to_all(x, axes, split_axis=0, concat_axis=0, tiled=True)]
    pallas_call x17 -> x16, Pallas kernels: 20.8 us -> 18.1 us  [run(): pl.pallas_call(kernel, out_shape=[jax.ShapeDtypeStruct(s, d) for s, d in...]
    ppermute x8, waiting for transfers between devices: 22.2 us -> 24 us  [swap(): return lax.ppermute(x, axis, [(0, 1), (1, 0)])]
  transfers between devices with their start and end apart: 9 -> 8, of which waited for: 9 -> 8; matrix products, arithmetic and copies ran while one was open for 0% -> 0% of each run, Pallas kernels for 10% -> 8%
where the time goes in v6:
time: 152 us
  blocking collectives  95.1 us (63%)
  waiting for transfers between devices  24 us (16%)
  Pallas kernels  18.1 us (12%)
  starting transfers between devices  13.9 us (9%)
    all_to_all x5, blocking collectives, exchange(): return lax.all_to_all(x, axes, split_axis=0, concat_axis=0, tiled=True)  95.1 us
    ppermute x8, waiting for transfers between devices, swap(): return lax.ppermute(x, axis, [(0, 1), (1, 0)])  24 us
    pallas_call x16, Pallas kernels, run(): pl.pallas_call(kernel, out_shape=[jax.ShapeDtypeStruct(s, d) for s, d in...  18.1 us
    ppermute x8, starting transfers between devices, swap(): return lax.ppermute(x, axis, [(0, 1), (1, 0)])  13.9 us
  transfers between devices with their start and end apart: 8, of which 8 were waited for; matrix products, arithmetic and copies ran while one was open for 0% of the time, Pallas kernels for 8%

profile of v6, /device:TPU:1, one launch (start us, length us, event | category | flops | bytes accessed | tf_op | source)
XLA Modules:
  0.0 152.0 jit_solution(1636927038508832935)
XLA Ops:
  0.6 1.8 %shard_map.76 = (f32[512,128]{1,0:T(8,128)S(1)}, bf16[128,640]{1,0:T(8,128)(2,1)S(1)}, bf16[2,256,640]{2,1,0:T(8,128)(2,1)S(1)}) custom-call(bf16[2,256,640]{2,1,0:T(8,128)(2,1)} %tokens_hbm.1, bf16[640,128]{1,0:T(8,128)(2,1)} %router_hbm.1), custom_call_target="tpu_custom_call" | custom-call | flops 83886080 | bytes 1000000 | tf_op jit(solution)/shard_map/pallas_call | solution.py:61
  2.4 2.1 %collective-permute-start = (f32[512,128]{1,0:T(8,128)S(1)}, f32[512,128]{1,0:T(8,128)S(1)}, u32[]{:S(2)}, u32[]{:S(2)}) collective-permute-start(f32[512,128]{1,0:T(8,128)S(1)} %get-tuple-element.34.part), channel_id=1, source_target_pairs={{0,1},{1,0},{2,3},{3,2},{4,5},{5,4},{6,7},{7,6},{8,9},{9,8},{10,11... | collective-permute-start | bytes 786440 | tf_op jit(solution)/shard_map/ppermute | solution.py:273
  4.5 3.2 %shard_map.77 = (bf16[2,256,640]{2,1,0:T(8,128)(2,1)S(1)}, bf16[1,1280,1280]{2,1,0:T(8,128)(2,1)S(1)}, bf16[1,1280,1280]{2,1,0:T(8,128)(2,1)S(1)}, bf16[640,512]{1,0:T(8,128)(2,1)S(1)}) custom-call(bf16[2,256,640]{2,1,0:T(8,128)(2,1)} %grad_hbm.1, bf16[1,1280,1280]{2,1,0:T(8,128)(2,1)} %in_hbm.1, bf16[1,1280,1280]{2,1,0:T(8,128)(2,1)} %out_hbm.1, ...), custom_call_target="tpu_custom_call" | custom-call | bytes 14000000 | tf_op jit(solution)/shard_map/pallas_call | solution.py:61
  7.7 1.5 collective-permute-done.other
  9.2 0.7 shard_map.78
  9.9 3.0 %collective-permute-start.1 = (bf16[256,640]{1,0:T(8,128)(2,1)S(1)}, bf16[256,640]{1,0:T(8,128)(2,1)S(1)}, u32[]{:S(2)}, u32[]{:S(2)}) collective-permute-start(bf16[256,640]{1,0:T(8,128)(2,1)S(1)} %get-tuple-element.38), channel_id=1, source_target_pairs={{0,2},{2,0},{1,3},{3,1},{4,6},{6,4},{5,7},{7,5},{8,10},{10,8},{9,1... | collective-permute-start | bytes 983048 | tf_op jit(solution)/shard_map/ppermute | solution.py:273
  12.8 1.3 collective-permute-done.1.got
  14.1 0.3 shard_map.79
  14.4 32.7 %all_to_all.25 = bf16[64,8,640]{2,1,0:T(8,128)(2,1)S(1)} all-to-all(bf16[64,8,640]{2,1,0:T(8,128)(2,1)S(1)} %bitcast.5), channel_id=1, replica_groups=mesh['z2'=2,'z1'=2,'z0'=2,'x_hi'=2,'y'=4,'core'=2,'tp'=2] {'z2','z1','z0..., dimensions={0} | all-to-all | bytes 1310720 | tf_op jit(solution)/shard_map/all_to_all | solution.py:277
  47.1 0.3 shard_map.80
  47.5 0.3 collective-permute-start.2
  47.8 1.2 collective-permute-start.4
  49.0 4.5 %collective-permute-done.2.other = bf16[256,640]{1,0:T(8,128)(2,1)S(1)} collective-permute-done((bf16[256,640]{1,0:T(8,128)(2,1)S(1)}, bf16[256,640]{1,0:T(8,128)(2,1)S(1)}, u32[]{:S(2)}, u32[]{:S(2)}) %collective-permute-start.2) | collective-permute-done | bytes 327712 | tf_op jit(solution)/shard_map/ppermute | solution.py:273
  53.5 3.0 %shard_map.81 = (f32[256,1280]{1,0:T(8,128)S(1)}, f32[256,640]{1,0:T(8,128)S(1)}, bf16[256,640]{1,0:T(8,128)(2,1)S(1)}) custom-call(bf16[256,640]{1,0:T(8,128)(2,1)S(1)} %get-tuple-element.39.own, bf16[256,640]{1,0:T(8,128)(2,1)S(1)} %collective-permute-done.2.other, bf16[1,1280,1280]{2,1,0:T(8,128)(2,1)S(1)} %get-tuple-element.40.w_in, ...), custom_call_target="tpu_custom_call" | custom-call | flops 1700000000 | bytes 10000000 | tf_op jit(solution)/shard_map/pallas_call | solution.py:61
  56.5 0.4 collective-permute-start.3
  56.8 3.3 %collective-permute-done.4.other = bf16[256,640]{1,0:T(8,128)(2,1)S(1)} collective-permute-done((bf16[256,640]{1,0:T(8,128)(2,1)S(1)}, bf16[256,640]{1,0:T(8,128)(2,1)S(1)}, u32[]{:S(2)}, u32[]{:S(2)}) %collective-permute-start.4) | collective-permute-done | bytes 327712 | tf_op jit(solution)/shard_map/ppermute | solution.py:273
  60.1 2.8 %shard_map.82 = (bf16[256,1280]{1,0:T(8,128)(2,1)S(1)}, f32[256,640]{1,0:T(8,128)S(1)}, bf16[256,640]{1,0:T(8,128)(2,1)S(1)}) custom-call(bf16[256,640]{1,0:T(8,128)(2,1)S(1)} %get-tuple-element.44.own, bf16[256,640]{1,0:T(8,128)(2,1)S(1)} %collective-permute-done.4.other, f32[256,1280]{1,0:T(8,128)S(1)} %get-tuple-element.45.slope, ...), custom_call_target="tpu_custom_call" | custom-call | flops 1700000000 | bytes 10000000 | tf_op jit(solution)/shard_map/pallas_call | solution.py:61
  62.9 0.3 collective-permute-start.5
  63.2 2.7 %shard_map.83 = (bf16[1,1280,1280]{2,1,0:T(8,128)(2,1)}, f32[8,128]{1,0:T(8,128)S(1)}) custom-call(bf16[256,640]{1,0:T(8,128)(2,1)S(1)} %get-tuple-element.39.own, bf16[256,640]{1,0:T(8,128)(2,1)S(1)} %collective-permute-done.2.other, bf16[256,1280]{1,0:T(8,128)(2,1)S(1)} %get-tuple-element.48.pre_grad), custom_call_target="tpu_custom_call" | custom-call | flops 840000000 | bytes 5000000 | tf_op jit(solution)/shard_map/pallas_call | solution.py:61
  66.0 1.2 collective-permute-done.3.out_got
  67.1 7.0 %collective-permute-done.5.in_got = bf16[256,640]{1,0:T(8,128)(2,1)S(1)} collective-permute-done((bf16[256,640]{1,0:T(8,128)(2,1)S(1)}, bf16[256,640]{1,0:T(8,128)(2,1)S(1)}, u32[]{:S(2)}, u32[]{:S(2)}) %collective-permute-start.5) | collective-permute-done | bytes 327712 | tf_op jit(solution)/shard_map/ppermute | solution.py:273
  74.2 0.4 shard_map.84
  74.5 27.5 %all_to_all.26 = bf16[64,8,640]{2,1,0:T(8,128)(2,1)S(1)} all-to-all(bf16[64,8,640]{2,1,0:T(8,128)(2,1)S(1)} %bitcast.4), channel_id=1, replica_groups=mesh['z2'=2,'z1'=2,'z0'=2,'x_hi'=2,'y'=4,'core'=2,'tp'=2] {'z2','z1','z0..., dimensions={0} | all-to-all | bytes 1310720 | tf_op jit(solution)/shard_map/all_to_all | solution.py:277
  102.0 0.3 shard_map.85
  102.3 6.1 %collective-permute-start.6 = (bf16[256,640]{1,0:T(8,128)(2,1)S(1)}, bf16[256,640]{1,0:T(8,128)(2,1)S(1)}, u32[]{:S(2)}, u32[]{:S(2)}) collective-permute-start(bf16[256,640]{1,0:T(8,128)(2,1)S(1)} %get-tuple-element.51), channel_id=1, source_target_pairs={{0,2},{2,0},{1,3},{3,1},{4,6},{6,4},{5,7},{7,5},{8,10},{10,8},{9,1... | collective-permute-start | bytes 983048 | tf_op jit(solution)/shard_map/ppermute | solution.py:273
  108.5 1.3 collective-permute-done.6.got
  109.7 0.5 shard_map.86
  110.3 0.4 collective-permute-start.7
  110.7 0.3 shard_map.87
  111.0 4.0 %collective-permute-done.7.got = bf16[512,128]{1,0:T(8,128)(2,1)S(1)} collective-permute-done((bf16[512,128]{1,0:T(8,128)(2,1)S(1)}, bf16[512,128]{1,0:T(8,128)(2,1)S(1)}, u32[]{:S(2)}, u32[]{:S(2)}) %collective-permute-start.7) | collective-permute-done | bytes 131104 | tf_op jit(solution)/shard_map/ppermute | solution.py:273
  115.1 0.5 shard_map.88
  115.6 13.7 %all_to_all.27.x = bf16[16,40,128]{2,1,0:T(8,128)(2,1)S(1)} all-to-all(bf16[16,40,128]{2,1,0:T(8,128)(2,1)S(1)} %get-tuple-element.58), channel_id=1, replica_groups=mesh['z2'=2,'z1'=2,'z0'=2,'x_hi'=2,'y'=4,'core'=2,'tp'=2] {'x_hi','y','c..., dimensions={0} | all-to-all | bytes 327680 | tf_op jit(solution)/shard_map/all_to_all | solution.py:277
  129.3 9.0 %all_to_all.28.x = bf16[8,40,128]{2,1,0:T(8,128)(2,1)S(1)} all-to-all(bf16[8,40,128]{2,1,0:T(8,128)(2,1)S(1)} %shard_map.89), channel_id=1, replica_groups=mesh['z2'=2,'z1'=2,'z0'=2,'x_hi'=2,'y'=4,'core'=2,'tp'=2] {'z0','z1','z2'}, dimensions={0} | all-to-all | bytes 163840 | tf_op jit(solution)/shard_map/all_to_all | solution.py:277
  138.3 12.3 %all_to_all.29.x = bf16[16,40,128]{2,1,0:T(8,128)(2,1)S(1)} all-to-all(bf16[16,40,128]{2,1,0:T(8,128)(2,1)S(1)} %shard_map.90), channel_id=1, replica_groups=mesh['z2'=2,'z1'=2,'z0'=2,'x_hi'=2,'y'=4,'core'=2,'tp'=2] {'x_hi','y','c..., dimensions={0} | all-to-all | bytes 327680 | tf_op jit(solution)/shard_map/all_to_all | solution.py:277
  150.6 1.2 shard_map.91
  (2 shorter events, 0.1 us)
Async XLA Ops:
  2.4 6.8 %collective-permute-start = (f32[512,128]{1,0:T(8,128)S(1)}, f32[512,128]{1,0:T(8,128)S(1)}, u32[]{:S(2)}, u32[]{:S(2)}) collective-permute-start(f32[512,128]{1,0:T(8,128)S(1)} %get-tuple-element.34.part), channel_id=1, source_target_pairs={{0,1},{1,0},{2,3},{3,2},{4,5},{5,4},{6,7},{7,6},{8,9},{9,8},{10,11... | collective-permute-start | bytes 786440 | tf_op jit(solution)/shard_map/ppermute | solution.py:273
  9.9 4.2 %collective-permute-start.1 = (bf16[256,640]{1,0:T(8,128)(2,1)S(1)}, bf16[256,640]{1,0:T(8,128)(2,1)S(1)}, u32[]{:S(2)}, u32[]{:S(2)}) collective-permute-start(bf16[256,640]{1,0:T(8,128)(2,1)S(1)} %get-tuple-element.38), channel_id=1, source_target_pairs={{0,2},{2,0},{1,3},{3,1},{4,6},{6,4},{5,7},{7,5},{8,10},{10,8},{9,1... | collective-permute-start | bytes 983048 | tf_op jit(solution)/shard_map/ppermute | solution.py:273
  47.5 6.0 %collective-permute-start.2 = (bf16[256,640]{1,0:T(8,128)(2,1)S(1)}, bf16[256,640]{1,0:T(8,128)(2,1)S(1)}, u32[]{:S(2)}, u32[]{:S(2)}) collective-permute-start(bf16[256,640]{1,0:T(8,128)(2,1)S(1)} %get-tuple-element.39.own), channel_id=1, source_target_pairs={{0,1},{1,0},{2,3},{3,2},{4,5},{5,4},{6,7},{7,6},{8,9},{9,8},{10,11... | collective-permute-start | bytes 983048 | tf_op jit(solution)/shard_map/ppermute | solution.py:273
  47.8 12.3 %collective-permute-start.4 = (bf16[256,640]{1,0:T(8,128)(2,1)S(1)}, bf16[256,640]{1,0:T(8,128)(2,1)S(1)}, u32[]{:S(2)}, u32[]{:S(2)}) collective-permute-start(bf16[256,640]{1,0:T(8,128)(2,1)S(1)} %get-tuple-element.44.own), channel_id=1, source_target_pairs={{0,1},{1,0},{2,3},{3,2},{4,5},{5,4},{6,7},{7,6},{8,9},{9,8},{10,11... | collective-permute-start | bytes 983048 | tf_op jit(solution)/shard_map/ppermute | solution.py:273
  56.5 10.6 %collective-permute-start.3 = (bf16[256,640]{1,0:T(8,128)(2,1)S(1)}, bf16[256,640]{1,0:T(8,128)(2,1)S(1)}, u32[]{:S(2)}, u32[]{:S(2)}) collective-permute-start(bf16[256,640]{1,0:T(8,128)(2,1)S(1)} %get-tuple-element.43), channel_id=1, source_target_pairs={{0,1},{1,0},{2,3},{3,2},{4,5},{5,4},{6,7},{7,6},{8,9},{9,8},{10,11... | collective-permute-start | bytes 983048 | tf_op jit(solution)/shard_map/ppermute | solution.py:273
  62.9 11.3 %collective-permute-start.5 = (bf16[256,640]{1,0:T(8,128)(2,1)S(1)}, bf16[256,640]{1,0:T(8,128)(2,1)S(1)}, u32[]{:S(2)}, u32[]{:S(2)}) collective-permute-start(bf16[256,640]{1,0:T(8,128)(2,1)S(1)} %get-tuple-element.47), channel_id=1, source_target_pairs={{0,1},{1,0},{2,3},{3,2},{4,5},{5,4},{6,7},{7,6},{8,9},{9,8},{10,11... | collective-permute-start | bytes 983048 | tf_op jit(solution)/shard_map/ppermute | solution.py:273
  102.3 7.4 %collective-permute-start.6 = (bf16[256,640]{1,0:T(8,128)(2,1)S(1)}, bf16[256,640]{1,0:T(8,128)(2,1)S(1)}, u32[]{:S(2)}, u32[]{:S(2)}) collective-permute-start(bf16[256,640]{1,0:T(8,128)(2,1)S(1)} %get-tuple-element.51), channel_id=1, source_target_pairs={{0,2},{2,0},{1,3},{3,1},{4,6},{6,4},{5,7},{7,5},{8,10},{10,8},{9,1... | collective-permute-start | bytes 983048 | tf_op jit(solution)/shard_map/ppermute | solution.py:273
  110.3 4.8 %collective-permute-start.7 = (bf16[512,128]{1,0:T(8,128)(2,1)S(1)}, bf16[512,128]{1,0:T(8,128)(2,1)S(1)}, u32[]{:S(2)}, u32[]{:S(2)}) collective-permute-start(bf16[512,128]{1,0:T(8,128)(2,1)S(1)} %get-tuple-element.55), channel_id=1, source_target_pairs={{0,1},{1,0},{2,3},{3,2},{4,5},{5,4},{6,7},{7,6},{8,9},{9,8},{10,11... | collective-permute-start | bytes 393224 | tf_op jit(solution)/shard_map/ppermute | solution.py:273

commit v7 on v5

--- a/solution.py
+++ b/solution.py
@@ -158,11 +158,9 @@
     )
 
 
-def up_kernel(own, other, w_in, w_out, slope, out_keep, out_send):
+def up_kernel(own, other, w_in, w_out, slope, out_keep, out_send, total):
     mine, theirs = both_halves()
     x, y = own[...], other[...]
-    keep = jnp.zeros((4 * NQ, H), F32)
-    sent = jnp.zeros((4 * NQ, H), F32)
     for f in range(0, FH, CH):
         cols = slice(f, f + CH)
         v = dot(x, w_in[0, mine, cols]) + dot(y, w_in[0, theirs, cols])
@@ -172,26 +170,24 @@
         slope[:, cols] = 0.5 * (1.0 + t) + 0.5 * v * (1.0 - t * t) * (
             0.7978845608 * (1.0 + 0.134145 * sq)
         )
-        keep = keep + dot(act, w_out[0, cols, mine])
-        sent = sent + dot(act, w_out[0, cols, theirs])
-    out_keep[...] = keep
-    out_send[...] = sent.astype(BF16)
-
-
-def down_kernel(own, other, slope, w_in, w_out, pre_grad, in_keep, in_send):
+        p = dot(act, w_out[0, cols, :])
+        total[...] = p if f == 0 else total[...] + p
+    out_keep[...] = total[:, mine]
+    out_send[...] = total[:, theirs].astype(BF16)
+
+
+def down_kernel(own, other, slope, w_in, w_out, pre_grad, in_keep, in_send, total):
     mine, theirs = both_halves()
     x, y = own[...], other[...]
-    keep = jnp.zeros((4 * NQ, H), F32)
-    sent = jnp.zeros((4 * NQ, H), F32)
     for f in range(0, FH, CH):
         cols = slice(f, f + CH)
         g = dot_t(x, w_out[0, cols, mine]) + dot_t(y, w_out[0, cols, theirs])
         g = (g * slope[:, cols]).astype(BF16)
         pre_grad[:, cols] = g
-        keep = keep + dot_t(g, w_in[0, mine, cols])
-        sent = sent + dot_t(g, w_in[0, theirs, cols])
-    in_keep[...] = keep
-    in_send[...] = sent.astype(BF16)
+        p = dot_t(g, w_in[0, :, cols])
+        total[...] = p if f == 0 else total[...] + p
+    in_keep[...] = total[:, mine]
+    in_send[...] = total[:, theirs].astype(BF16)
 
 
 def weight_kernel(own, other, pre_grad, out, done):
@@ -287,6 +283,7 @@
 def on_device(tokens, router, w_in, w_out, grad_out):
     half = ((4 * NQ, H), BF16)
     half32 = ((4 * NQ, H), F32)
+    total = [pltpu.VMEM((4 * NQ, D), F32)]
     done = ((8, E), F32)
     small = 2 * B * M * H * E
     part, ordered, tokens = call(
@@ -316,11 +313,11 @@
     in_other = swap(in_own, "tp")
     grad_other = swap(grad_own, "tp")
     slope, out_keep, out_send = call(
-        up_kernel, [((4 * NQ, FH), F32), half32, half], 1.7e9, 1e7
+        up_kernel, [((4 * NQ, FH), F32), half32, half], 1.7e9, 1e7, scratch=total
     )(in_own, in_other, w_in, w_out)
     out_got = swap(out_send, "tp")
     pre_grad, in_keep, in_send = call(
-        down_kernel, [((4 * NQ, FH), BF16), half32, half], 1.7e9, 1e7
+        down_kernel, [((4 * NQ, FH), BF16), half32, half], 1.7e9, 1e7, scratch=total
     )(grad_own, grad_other, slope, w_in, w_out)
     in_got = swap(in_send, "tp")
     grad_weight, weight_done = call(weight_kernel, [((1, D, FH), BF16), done], 8.4e8, 5e6)(

time: 152 us -> 153 us (level)
  waiting for transfers between devices: 28.9 us -> 30.8 us
    ppermute x8, waiting for transfers between devices: 22.2 us -> 24 us  [swap(): return lax.ppermute(x, axis, [(0, 1), (1, 0)])]
  transfers between devices with their start and end apart: 9 -> 9, of which waited for: 9 -> 9; matrix products, arithmetic and copies ran while one was open for 0% -> 0% of each run, Pallas kernels for 10% -> 9%
where the time goes in v7:
time: 153 us; the launch traced here: 152 us
  blocking collectives  81.7 us (53%)
  waiting for transfers between devices  30.8 us (20%)
  starting transfers between devices  19.8 us (13%)
  Pallas kernels  19.4 us (13%)
    all_to_all x4, blocking collectives, exchange(): return lax.all_to_all(x, axes, split_axis=0, concat_axis=0, tiled=True)  81.7 us
    ppermute x8, waiting for transfers between devices, swap(): return lax.ppermute(x, axis, [(0, 1), (1, 0)])  24 us
    pallas_call x17, Pallas kernels, run(): pl.pallas_call(kernel, out_shape=[jax.ShapeDtypeStruct(s, d) for s, d in...  19.4 us
    ppermute x8, starting transfers between devices, swap(): return lax.ppermute(x, axis, [(0, 1), (1, 0)])  13.9 us
    all_to_all x1, waiting for transfers between devices, exchange(): return lax.all_to_all(x, axes, split_axis=0, concat_axis=0, tiled=True)  6.78 us
    all_to_all x1, starting transfers between devices, exchange(): return lax.all_to_all(x, axes, split_axis=0, concat_axis=0, tiled=True)  5.94 us
  transfers between devices with their start and end apart: 9, of which 9 were waited for; matrix products, arithmetic and copies ran while one was open for 0% of the time, Pallas kernels for 9%

profile of v7, /device:TPU:1, one launch (start us, length us, event | category | flops | bytes accessed | tf_op | source)
XLA Modules:
  0.0 152.5 jit_solution(12274255109969724988)
XLA Ops:
  0.6 1.7 %shard_map.76 = (f32[512,128]{1,0:T(8,128)S(1)}, bf16[640,128]{1,0:T(8,128)(2,1)S(1)}, bf16[2,256,640]{2,1,0:T(8,128)(2,1)S(1)}) custom-call(bf16[2,256,640]{2,1,0:T(8,128)(2,1)} %tokens_hbm.1, bf16[640,128]{1,0:T(8,128)(2,1)} %router_hbm.1), custom_call_target="tpu_custom_call" | custom-call | flops 83886080 | bytes 1000000 | tf_op jit(solution)/shard_map/pallas_call | solution.py:61
  2.3 2.1 %collective-permute-start = (f32[512,128]{1,0:T(8,128)S(1)}, f32[512,128]{1,0:T(8,128)S(1)}, u32[]{:S(2)}, u32[]{:S(2)}) collective-permute-start(f32[512,128]{1,0:T(8,128)S(1)} %get-tuple-element.34.part), channel_id=1, source_target_pairs={{0,1},{1,0},{2,3},{3,2},{4,5},{5,4},{6,7},{7,6},{8,9},{9,8},{10,11... | collective-permute-start | bytes 786440 | tf_op jit(solution)/shard_map/ppermute | solution.py:276
  4.5 3.2 %shard_map.77 = (bf16[2,256,640]{2,1,0:T(8,128)(2,1)S(1)}, bf16[1,1280,1280]{2,1,0:T(8,128)(2,1)S(1)}, bf16[1,1280,1280]{2,1,0:T(8,128)(2,1)S(1)}, bf16[640,512]{1,0:T(8,128)(2,1)S(1)}) custom-call(bf16[2,256,640]{2,1,0:T(8,128)(2,1)} %grad_hbm.1, bf16[1,1280,1280]{2,1,0:T(8,128)(2,1)} %in_hbm.1, bf16[1,1280,1280]{2,1,0:T(8,128)(2,1)} %out_hbm.1, ...), custom_call_target="tpu_custom_call" | custom-call | bytes 14000000 | tf_op jit(solution)/shard_map/pallas_call | solution.py:61
  7.6 1.5 collective-permute-done.other
  9.1 0.7 shard_map.78
  9.8 3.0 %collective-permute-start.1 = (bf16[256,640]{1,0:T(8,128)(2,1)S(1)}, bf16[256,640]{1,0:T(8,128)(2,1)S(1)}, u32[]{:S(2)}, u32[]{:S(2)}) collective-permute-start(bf16[256,640]{1,0:T(8,128)(2,1)S(1)} %get-tuple-element.38), channel_id=1, source_target_pairs={{0,2},{2,0},{1,3},{3,1},{4,6},{6,4},{5,7},{7,5},{8,10},{10,8},{9,1... | collective-permute-start | bytes 983048 | tf_op jit(solution)/shard_map/ppermute | solution.py:276
  12.8 1.3 collective-permute-done.1.got
  14.0 0.3 shard_map.79
  14.4 32.7 %all_to_all.25 = bf16[64,8,640]{2,1,0:T(8,128)(2,1)S(1)} all-to-all(bf16[64,8,640]{2,1,0:T(8,128)(2,1)S(1)} %bitcast.5), channel_id=1, replica_groups=mesh['z2'=2,'z1'=2,'z0'=2,'x_hi'=2,'y'=4,'core'=2,'tp'=2] {'z2','z1','z0..., dimensions={0} | all-to-all | bytes 1310720 | tf_op jit(solution)/shard_map/all_to_all | solution.py:280
  47.1 0.3 shard_map.80
  47.4 0.3 collective-permute-start.2
  47.7 1.2 collective-permute-start.4
  48.9 4.5 %collective-permute-done.2.other = bf16[256,640]{1,0:T(8,128)(2,1)S(1)} collective-permute-done((bf16[256,640]{1,0:T(8,128)(2,1)S(1)}, bf16[256,640]{1,0:T(8,128)(2,1)S(1)}, u32[]{:S(2)}, u32[]{:S(2)}) %collective-permute-start.2) | collective-permute-done | bytes 327712 | tf_op jit(solution)/shard_map/ppermute | solution.py:276
  53.4 3.0 %shard_map.81 = (f32[256,1280]{1,0:T(8,128)S(1)}, f32[256,640]{1,0:T(8,128)S(1)}, bf16[256,640]{1,0:T(8,128)(2,1)S(1)}) custom-call(bf16[256,640]{1,0:T(8,128)(2,1)S(1)} %get-tuple-element.39.own, bf16[256,640]{1,0:T(8,128)(2,1)S(1)} %collective-permute-done.2.other, bf16[1,1280,1280]{2,1,0:T(8,128)(2,1)S(1)} %get-tuple-element.40.w_in, ...), custom_call_target="tpu_custom_call" | custom-call | flops 1700000000 | bytes 10000000 | tf_op jit(solution)/shard_map/pallas_call | solution.py:61
  56.4 0.4 collective-permute-start.3
  56.8 3.3 %collective-permute-done.4.other = bf16[256,640]{1,0:T(8,128)(2,1)S(1)} collective-permute-done((bf16[256,640]{1,0:T(8,128)(2,1)S(1)}, bf16[256,640]{1,0:T(8,128)(2,1)S(1)}, u32[]{:S(2)}, u32[]{:S(2)}) %collective-permute-start.4) | collective-permute-done | bytes 327712 | tf_op jit(solution)/shard_map/ppermute | solution.py:276
  60.1 2.8 %shard_map.82 = (bf16[256,1280]{1,0:T(8,128)(2,1)S(1)}, f32[256,640]{1,0:T(8,128)S(1)}, bf16[256,640]{1,0:T(8,128)(2,1)S(1)}) custom-call(bf16[256,640]{1,0:T(8,128)(2,1)S(1)} %get-tuple-element.44.own, bf16[256,640]{1,0:T(8,128)(2,1)S(1)} %collective-permute-done.4.other, f32[256,1280]{1,0:T(8,128)S(1)} %get-tuple-element.45.slope, ...), custom_call_target="tpu_custom_call" | custom-call | flops 1700000000 | bytes 10000000 | tf_op jit(solution)/shard_map/pallas_call | solution.py:61
  62.9 0.3 collective-permute-start.5
  63.2 2.7 %shard_map.83 = (bf16[1,1280,1280]{2,1,0:T(8,128)(2,1)}, f32[8,128]{1,0:T(8,128)S(1)}) custom-call(bf16[256,640]{1,0:T(8,128)(2,1)S(1)} %get-tuple-element.39.own, bf16[256,640]{1,0:T(8,128)(2,1)S(1)} %collective-permute-done.2.other, bf16[256,1280]{1,0:T(8,128)(2,1)S(1)} %get-tuple-element.48.pre_grad), custom_call_target="tpu_custom_call" | custom-call | flops 840000000 | bytes 5000000 | tf_op jit(solution)/shard_map/pallas_call | solution.py:61
  65.9 1.2 collective-permute-done.3.out_got
  67.1 7.0 %collective-permute-done.5.in_got = bf16[256,640]{1,0:T(8,128)(2,1)S(1)} collective-permute-done((bf16[256,640]{1,0:T(8,128)(2,1)S(1)}, bf16[256,640]{1,0:T(8,128)(2,1)S(1)}, u32[]{:S(2)}, u32[]{:S(2)}) %collective-permute-start.5) | collective-permute-done | bytes 327712 | tf_op jit(solution)/shard_map/ppermute | solution.py:276
  74.1 0.3 shard_map.84
  74.5 27.5 %all_to_all.26 = bf16[64,8,640]{2,1,0:T(8,128)(2,1)S(1)} all-to-all(bf16[64,8,640]{2,1,0:T(8,128)(2,1)S(1)} %bitcast.4), channel_id=1, replica_groups=mesh['z2'=2,'z1'=2,'z0'=2,'x_hi'=2,'y'=4,'core'=2,'tp'=2] {'z2','z1','z0..., dimensions={0} | all-to-all | bytes 1310720 | tf_op jit(solution)/shard_map/all_to_all | solution.py:280
  102.0 0.3 shard_map.85
  102.3 6.1 %collective-permute-start.6 = (bf16[256,640]{1,0:T(8,128)(2,1)S(1)}, bf16[256,640]{1,0:T(8,128)(2,1)S(1)}, u32[]{:S(2)}, u32[]{:S(2)}) collective-permute-start(bf16[256,640]{1,0:T(8,128)(2,1)S(1)} %get-tuple-element.51), channel_id=1, source_target_pairs={{0,2},{2,0},{1,3},{3,1},{4,6},{6,4},{5,7},{7,5},{8,10},{10,8},{9,1... | collective-permute-start | bytes 983048 | tf_op jit(solution)/shard_map/ppermute | solution.py:276
  108.4 1.3 collective-permute-done.6.got
  109.7 0.5 shard_map.87
  110.2 0.4 collective-permute-start.7
  110.7 0.3 shard_map.86
  111.0 4.1 %collective-permute-done.7.got = bf16[512,128]{1,0:T(8,128)(2,1)S(1)} collective-permute-done((bf16[512,128]{1,0:T(8,128)(2,1)S(1)}, bf16[512,128]{1,0:T(8,128)(2,1)S(1)}, u32[]{:S(2)}, u32[]{:S(2)}) %collective-permute-start.7) | collective-permute-done | bytes 131104 | tf_op jit(solution)/shard_map/ppermute | solution.py:276
  115.0 1.2 shard_map.88
  116.2 5.9 %all-to-all-start.2 = ((bf16[16,40,128]{2,1,0:T(8,128)(2,1)}), bf16[16,40,128]{2,1,0:T(8,128)(2,1)S(1)}, u32[]{:S(2)}, u32[]{:S(2)}) async-start(bf16[16,40,128]{2,1,0:T(8,128)(2,1)} %get-tuple-element.62), calls=%async_computation.2 | async-start | bytes 327680 | tf_op jit(solution)/shard_map/all_to_all | solution.py:280
  122.2 1.2 shard_map.89
  123.3 6.8 %all-to-all-done.2.x = bf16[16,40,128]{2,1,0:T(8,128)(2,1)S(1)} async-done(((bf16[16,40,128]{2,1,0:T(8,128)(2,1)}), bf16[16,40,128]{2,1,0:T(8,128)(2,1)S(1)}, u32[]{:S(2)}, u32[]{:S(2)}) %all-to-all-start.2) | async-done | bytes 163872 | tf_op jit(solution)/shard_map/all_to_all | solution.py:280
  130.2 9.1 %all_to_all.27.x = bf16[8,40,128]{2,1,0:T(8,128)(2,1)S(1)} all-to-all(bf16[8,40,128]{2,1,0:T(8,128)(2,1)S(1)} %shard_map.90), channel_id=1, replica_groups=mesh['z2'=2,'z1'=2,'z0'=2,'x_hi'=2,'y'=4,'core'=2,'tp'=2] {'z0','z1','z2'}, dimensions={0} | all-to-all | bytes 163840 | tf_op jit(solution)/shard_map/all_to_all | solution.py:280
  139.3 12.5 %all_to_all.28.x = bf16[16,40,128]{2,1,0:T(8,128)(2,1)S(1)} all-to-all(bf16[16,40,128]{2,1,0:T(8,128)(2,1)S(1)} %shard_map.91), channel_id=1, replica_groups=mesh['z2'=2,'z1'=2,'z0'=2,'x_hi'=2,'y'=4,'core'=2,'tp'=2] {'x_hi','y','c..., dimensions={0} | all-to-all | bytes 327680 | tf_op jit(solution)/shard_map/all_to_all | solution.py:280
  151.7 0.7 shard_map.92
  (2 shorter events, 0.1 us)
Async XLA Ops:
  2.3 6.8 %collective-permute-start = (f32[512,128]{1,0:T(8,128)S(1)}, f32[512,128]{1,0:T(8,128)S(1)}, u32[]{:S(2)}, u32[]{:S(2)}) collective-permute-start(f32[512,128]{1,0:T(8,128)S(1)} %get-tuple-element.34.part), channel_id=1, source_target_pairs={{0,1},{1,0},{2,3},{3,2},{4,5},{5,4},{6,7},{7,6},{8,9},{9,8},{10,11... | collective-permute-start | bytes 786440 | tf_op jit(solution)/shard_map/ppermute | solution.py:276
  9.8 4.2 %collective-permute-start.1 = (bf16[256,640]{1,0:T(8,128)(2,1)S(1)}, bf16[256,640]{1,0:T(8,128)(2,1)S(1)}, u32[]{:S(2)}, u32[]{:S(2)}) collective-permute-start(bf16[256,640]{1,0:T(8,128)(2,1)S(1)} %get-tuple-element.38), channel_id=1, source_target_pairs={{0,2},{2,0},{1,3},{3,1},{4,6},{6,4},{5,7},{7,5},{8,10},{10,8},{9,1... | collective-permute-start | bytes 983048 | tf_op jit(solution)/shard_map/ppermute | solution.py:276
  47.4 6.0 %collective-permute-start.2 = (bf16[256,640]{1,0:T(8,128)(2,1)S(1)}, bf16[256,640]{1,0:T(8,128)(2,1)S(1)}, u32[]{:S(2)}, u32[]{:S(2)}) collective-permute-start(bf16[256,640]{1,0:T(8,128)(2,1)S(1)} %get-tuple-element.39.own), channel_id=1, source_target_pairs={{0,1},{1,0},{2,3},{3,2},{4,5},{5,4},{6,7},{7,6},{8,9},{9,8},{10,11... | collective-permute-start | bytes 983048 | tf_op jit(solution)/shard_map/ppermute | solution.py:276
  47.7 12.3 %collective-permute-start.4 = (bf16[256,640]{1,0:T(8,128)(2,1)S(1)}, bf16[256,640]{1,0:T(8,128)(2,1)S(1)}, u32[]{:S(2)}, u32[]{:S(2)}) collective-permute-start(bf16[256,640]{1,0:T(8,128)(2,1)S(1)} %get-tuple-element.44.own), channel_id=1, source_target_pairs={{0,1},{1,0},{2,3},{3,2},{4,5},{5,4},{6,7},{7,6},{8,9},{9,8},{10,11... | collective-permute-start | bytes 983048 | tf_op jit(solution)/shard_map/ppermute | solution.py:276
  56.4 10.7 %collective-permute-start.3 = (bf16[256,640]{1,0:T(8,128)(2,1)S(1)}, bf16[256,640]{1,0:T(8,128)(2,1)S(1)}, u32[]{:S(2)}, u32[]{:S(2)}) collective-permute-start(bf16[256,640]{1,0:T(8,128)(2,1)S(1)} %get-tuple-element.43), channel_id=1, source_target_pairs={{0,1},{1,0},{2,3},{3,2},{4,5},{5,4},{6,7},{7,6},{8,9},{9,8},{10,11... | collective-permute-start | bytes 983048 | tf_op jit(solution)/shard_map/ppermute | solution.py:276
  62.9 11.2 %collective-permute-start.5 = (bf16[256,640]{1,0:T(8,128)(2,1)S(1)}, bf16[256,640]{1,0:T(8,128)(2,1)S(1)}, u32[]{:S(2)}, u32[]{:S(2)}) collective-permute-start(bf16[256,640]{1,0:T(8,128)(2,1)S(1)} %get-tuple-element.47), channel_id=1, source_target_pairs={{0,1},{1,0},{2,3},{3,2},{4,5},{5,4},{6,7},{7,6},{8,9},{9,8},{10,11... | collective-permute-start | bytes 983048 | tf_op jit(solution)/shard_map/ppermute | solution.py:276
  102.3 7.4 %collective-permute-start.6 = (bf16[256,640]{1,0:T(8,128)(2,1)S(1)}, bf16[256,640]{1,0:T(8,128)(2,1)S(1)}, u32[]{:S(2)}, u32[]{:S(2)}) collective-permute-start(bf16[256,640]{1,0:T(8,128)(2,1)S(1)} %get-tuple-element.51), channel_id=1, source_target_pairs={{0,2},{2,0},{1,3},{3,1},{4,6},{6,4},{5,7},{7,5},{8,10},{10,8},{9,1... | collective-permute-start | bytes 983048 | tf_op jit(solution)/shard_map/ppermute | solution.py:276
  110.2 4.8 %collective-permute-start.7 = (bf16[512,128]{1,0:T(8,128)(2,1)S(1)}, bf16[512,128]{1,0:T(8,128)(2,1)S(1)}, u32[]{:S(2)}, u32[]{:S(2)}) collective-permute-start(bf16[512,128]{1,0:T(8,128)(2,1)S(1)} %get-tuple-element.56), channel_id=1, source_target_pairs={{0,1},{1,0},{2,3},{3,2},{4,5},{5,4},{6,7},{7,6},{8,9},{9,8},{10,11... | collective-permute-start | bytes 393224 | tf_op jit(solution)/shard_map/ppermute | solution.py:276
  116.2 13.9 %all-to-all-start.2 = ((bf16[16,40,128]{2,1,0:T(8,128)(2,1)}), bf16[16,40,128]{2,1,0:T(8,128)(2,1)S(1)}, u32[]{:S(2)}, u32[]{:S(2)}) async-start(bf16[16,40,128]{2,1,0:T(8,128)(2,1)} %get-tuple-element.62), calls=%async_computation.2 | async-start | bytes 327680 | tf_op jit(solution)/shard_map/all_to_all | solution.py:280

commit v8 on v6

--- a/solution.py
+++ b/solution.py
@@ -158,9 +158,11 @@
     )
 
 
-def up_kernel(own, other, w_in, w_out, slope, out_keep, out_send, total):
+def up_kernel(own, other, w_in, w_out, slope, out_keep, out_send):
     mine, theirs = both_halves()
     x, y = own[...], other[...]
+    keep = jnp.zeros((4 * NQ, H), F32)
+    sent = jnp.zeros((4 * NQ, H), F32)
     for f in range(0, FH, CH):
         cols = slice(f, f + CH)
         v = dot(x, w_in[0, mine, cols]) + dot(y, w_in[0, theirs, cols])
@@ -170,24 +172,26 @@
         slope[:, cols] = 0.5 * (1.0 + t) + 0.5 * v * (1.0 - t * t) * (
             0.7978845608 * (1.0 + 0.134145 * sq)
         )
-        p = dot(act, w_out[0, cols, :])
-        total[...] = p if f == 0 else total[...] + p
-    out_keep[...] = total[:, mine]
-    out_send[...] = total[:, theirs].astype(BF16)
-
-
-def down_kernel(own, other, slope, w_in, w_out, pre_grad, in_keep, in_send, total):
+        keep = keep + dot(act, w_out[0, cols, mine])
+        sent = sent + dot(act, w_out[0, cols, theirs])
+    out_keep[...] = keep
+    out_send[...] = sent.astype(BF16)
+
+
+def down_kernel(own, other, slope, w_in, w_out, pre_grad, in_keep, in_send):
     mine, theirs = both_halves()
     x, y = own[...], other[...]
+    keep = jnp.zeros((4 * NQ, H), F32)
+    sent = jnp.zeros((4 * NQ, H), F32)
     for f in range(0, FH, CH):
         cols = slice(f, f + CH)
         g = dot_t(x, w_out[0, cols, mine]) + dot_t(y, w_out[0, cols, theirs])
         g = (g * slope[:, cols]).astype(BF16)
         pre_grad[:, cols] = g
-        p = dot_t(g, w_in[0, :, cols])
-        total[...] = p if f == 0 else total[...] + p
-    in_keep[...] = total[:, mine]
-    in_send[...] = total[:, theirs].astype(BF16)
+        keep = keep + dot_t(g, w_in[0, mine, cols])
+        sent = sent + dot_t(g, w_in[0, theirs, cols])
+    in_keep[...] = keep
+    in_send[...] = sent.astype(BF16)
 
 
 def weight_kernel(own, other, pre_grad, out, done):
@@ -280,7 +284,6 @@
 def on_device(tokens, router, w_in, w_out, grad_out):
     half = ((4 * NQ, H), BF16)
     half32 = ((4 * NQ, H), F32)
-    total = [pltpu.VMEM((4 * NQ, D), F32)]
     done = ((8, E), F32)
     small = 2 * B * M * H * E
     part, ordered, tokens = call(
@@ -310,11 +313,11 @@
     in_other = swap(in_own, "tp")
     grad_other = swap(grad_own, "tp")
     slope, out_keep, out_send = call(
-        up_kernel, [((4 * NQ, FH), F32), half32, half], 1.7e9, 1e7, scratch=total
+        up_kernel, [((4 * NQ, FH), F32), half32, half], 1.7e9, 1e7
     )(in_own, in_other, w_in, w_out)
     out_got = swap(out_send, "tp")
     pre_grad, in_keep, in_send = call(
-        down_kernel, [((4 * NQ, FH), BF16), half32, half], 1.7e9, 1e7, scratch=total
+        down_kernel, [((4 * NQ, FH), BF16), half32, half], 1.7e9, 1e7
     )(grad_own, grad_other, slope, w_in, w_out)
     in_got = swap(in_send, "tp")
     grad_weight, weight_done = call(weight_kernel, [((1, D, FH), BF16), done], 8.4e8, 5e6)(

time: 152 us -> 152 us (level)
  waiting for transfers between devices: 24 us -> 22.1 us
    ppermute x8, waiting for transfers between devices: 24 us -> 22.1 us  [swap(): return lax.ppermute(x, axis, [(0, 1), (1, 0)])]
  transfers between devices with their start and end apart: 8 -> 8, of which waited for: 8 -> 8; matrix products, arithmetic and copies ran while one was open for 0% -> 0% of each run, Pallas kernels for 8% -> 9%
where the time goes in v8:
time: 152 us; the launch traced here: 151 us
  blocking collectives  95.2 us (63%)
  waiting for transfers between devices  22.1 us (15%)
  Pallas kernels  19.5 us (13%)
  starting transfers between devices  13.7 us (9%)
    all_to_all x5, blocking collectives, exchange(): return lax.all_to_all(x, axes, split_axis=0, concat_axis=0, tiled=True)  95.2 us
    ppermute x8, waiting for transfers between devices, swap(): return lax.ppermute(x, axis, [(0, 1), (1, 0)])  22.1 us
    pallas_call x16, Pallas kernels, run(): pl.pallas_call(kernel, out_shape=[jax.ShapeDtypeStruct(s, d) for s, d in...  19.5 us
    ppermute x8, starting transfers between devices, swap(): return lax.ppermute(x, axis, [(0, 1), (1, 0)])  13.7 us
  transfers between devices with their start and end apart: 8, of which 8 were waited for; matrix products, arithmetic and copies ran while one was open for 0% of the time, Pallas kernels for 9%

profile of v8, /device:TPU:1, one launch (start us, length us, event | category | flops | bytes accessed | tf_op | source)
XLA Modules:
  0.0 151.5 jit_solution(7133348576792835134)
XLA Ops:
  0.6 1.8 %shard_map.76 = (f32[512,128]{1,0:T(8,128)S(1)}, bf16[128,640]{1,0:T(8,128)(2,1)S(1)}, bf16[2,256,640]{2,1,0:T(8,128)(2,1)S(1)}) custom-call(bf16[2,256,640]{2,1,0:T(8,128)(2,1)} %tokens_hbm.1, bf16[640,128]{1,0:T(8,128)(2,1)} %router_hbm.1), custom_call_target="tpu_custom_call" | custom-call | flops 83886080 | bytes 1000000 | tf_op jit(solution)/shard_map/pallas_call | solution.py:61
  2.4 2.1 %collective-permute-start = (f32[512,128]{1,0:T(8,128)S(1)}, f32[512,128]{1,0:T(8,128)S(1)}, u32[]{:S(2)}, u32[]{:S(2)}) collective-permute-start(f32[512,128]{1,0:T(8,128)S(1)} %get-tuple-element.34.part), channel_id=1, source_target_pairs={{0,1},{1,0},{2,3},{3,2},{4,5},{5,4},{6,7},{7,6},{8,9},{9,8},{10,11... | collective-permute-start | bytes 786440 | tf_op jit(solution)/shard_map/ppermute | solution.py:277
  4.5 3.2 %shard_map.77 = (bf16[2,256,640]{2,1,0:T(8,128)(2,1)S(1)}, bf16[1,1280,1280]{2,1,0:T(8,128)(2,1)S(1)}, bf16[1,1280,1280]{2,1,0:T(8,128)(2,1)S(1)}, bf16[640,512]{1,0:T(8,128)(2,1)S(1)}) custom-call(bf16[2,256,640]{2,1,0:T(8,128)(2,1)} %grad_hbm.1, bf16[1,1280,1280]{2,1,0:T(8,128)(2,1)} %in_hbm.1, bf16[1,1280,1280]{2,1,0:T(8,128)(2,1)} %out_hbm.1, ...), custom_call_target="tpu_custom_call" | custom-call | bytes 14000000 | tf_op jit(solution)/shard_map/pallas_call | solution.py:61
  7.7 1.5 collective-permute-done.other
  9.2 0.7 shard_map.78
  9.9 3.0 %collective-permute-start.1 = (bf16[256,640]{1,0:T(8,128)(2,1)S(1)}, bf16[256,640]{1,0:T(8,128)(2,1)S(1)}, u32[]{:S(2)}, u32[]{:S(2)}) collective-permute-start(bf16[256,640]{1,0:T(8,128)(2,1)S(1)} %get-tuple-element.38), channel_id=1, source_target_pairs={{0,2},{2,0},{1,3},{3,1},{4,6},{6,4},{5,7},{7,5},{8,10},{10,8},{9,1... | collective-permute-start | bytes 983048 | tf_op jit(solution)/shard_map/ppermute | solution.py:277
  12.8 1.3 collective-permute-done.1.got
  14.1 0.3 shard_map.79
  14.4 32.7 %all_to_all.25 = bf16[64,8,640]{2,1,0:T(8,128)(2,1)S(1)} all-to-all(bf16[64,8,640]{2,1,0:T(8,128)(2,1)S(1)} %bitcast.5), channel_id=1, replica_groups=mesh['z2'=2,'z1'=2,'z0'=2,'x_hi'=2,'y'=4,'core'=2,'tp'=2] {'z2','z1','z0..., dimensions={0} | all-to-all | bytes 1310720 | tf_op jit(solution)/shard_map/all_to_all | solution.py:281
  47.1 0.3 shard_map.80
  47.5 0.3 collective-permute-start.2
  47.8 1.2 collective-permute-start.4
  49.0 4.5 %collective-permute-done.2.other = bf16[256,640]{1,0:T(8,128)(2,1)S(1)} collective-permute-done((bf16[256,640]{1,0:T(8,128)(2,1)S(1)}, bf16[256,640]{1,0:T(8,128)(2,1)S(1)}, u32[]{:S(2)}, u32[]{:S(2)}) %collective-permute-start.2) | collective-permute-done | bytes 327712 | tf_op jit(solution)/shard_map/ppermute | solution.py:277
  53.5 3.8 %shard_map.81 = (f32[256,1280]{1,0:T(8,128)S(1)}, f32[256,640]{1,0:T(8,128)S(1)}, bf16[256,640]{1,0:T(8,128)(2,1)S(1)}) custom-call(bf16[256,640]{1,0:T(8,128)(2,1)S(1)} %get-tuple-element.39.own, bf16[256,640]{1,0:T(8,128)(2,1)S(1)} %collective-permute-done.2.other, bf16[1,1280,1280]{2,1,0:T(8,128)(2,1)S(1)} %get-tuple-element.40.w_in, ...), custom_call_target="tpu_custom_call" | custom-call | flops 1700000000 | bytes 10000000 | tf_op jit(solution)/shard_map/pallas_call | solution.py:61
  57.3 0.3 collective-permute-start.3
  57.6 2.5 %collective-permute-done.4.other = bf16[256,640]{1,0:T(8,128)(2,1)S(1)} collective-permute-done((bf16[256,640]{1,0:T(8,128)(2,1)S(1)}, bf16[256,640]{1,0:T(8,128)(2,1)S(1)}, u32[]{:S(2)}, u32[]{:S(2)}) %collective-permute-start.4) | collective-permute-done | bytes 327712 | tf_op jit(solution)/shard_map/ppermute | solution.py:277
  60.1 3.3 %shard_map.82 = (bf16[256,1280]{1,0:T(8,128)(2,1)S(1)}, f32[256,640]{1,0:T(8,128)S(1)}, bf16[256,640]{1,0:T(8,128)(2,1)S(1)}) custom-call(bf16[256,640]{1,0:T(8,128)(2,1)S(1)} %get-tuple-element.44.own, bf16[256,640]{1,0:T(8,128)(2,1)S(1)} %collective-permute-done.4.other, f32[256,1280]{1,0:T(8,128)S(1)} %get-tuple-element.45.slope, ...), custom_call_target="tpu_custom_call" | custom-call | flops 1700000000 | bytes 10000000 | tf_op jit(solution)/shard_map/pallas_call | solution.py:61
  63.5 0.3 collective-permute-start.5
  63.7 2.7 %shard_map.83 = (bf16[1,1280,1280]{2,1,0:T(8,128)(2,1)}, f32[8,128]{1,0:T(8,128)S(1)}) custom-call(bf16[256,640]{1,0:T(8,128)(2,1)S(1)} %get-tuple-element.39.own, bf16[256,640]{1,0:T(8,128)(2,1)S(1)} %collective-permute-done.2.other, bf16[256,1280]{1,0:T(8,128)(2,1)S(1)} %get-tuple-element.48.pre_grad), custom_call_target="tpu_custom_call" | custom-call | flops 840000000 | bytes 5000000 | tf_op jit(solution)/shard_map/pallas_call | solution.py:61
  66.5 0.7 collective-permute-done.3.out_got
  67.1 6.5 %collective-permute-done.5.in_got = bf16[256,640]{1,0:T(8,128)(2,1)S(1)} collective-permute-done((bf16[256,640]{1,0:T(8,128)(2,1)S(1)}, bf16[256,640]{1,0:T(8,128)(2,1)S(1)}, u32[]{:S(2)}, u32[]{:S(2)}) %collective-permute-start.5) | collective-permute-done | bytes 327712 | tf_op jit(solution)/shard_map/ppermute | solution.py:277
  73.6 0.3 shard_map.84
  74.0 27.3 %all_to_all.26 = bf16[64,8,640]{2,1,0:T(8,128)(2,1)S(1)} all-to-all(bf16[64,8,640]{2,1,0:T(8,128)(2,1)S(1)} %bitcast.4), channel_id=1, replica_groups=mesh['z2'=2,'z1'=2,'z0'=2,'x_hi'=2,'y'=4,'core'=2,'tp'=2] {'z2','z1','z0..., dimensions={0} | all-to-all | bytes 1310720 | tf_op jit(solution)/shard_map/all_to_all | solution.py:281
  101.3 0.3 shard_map.85
  101.6 6.0 %collective-permute-start.6 = (bf16[256,640]{1,0:T(8,128)(2,1)S(1)}, bf16[256,640]{1,0:T(8,128)(2,1)S(1)}, u32[]{:S(2)}, u32[]{:S(2)}) collective-permute-start(bf16[256,640]{1,0:T(8,128)(2,1)S(1)} %get-tuple-element.51), channel_id=1, source_target_pairs={{0,2},{2,0},{1,3},{3,1},{4,6},{6,4},{5,7},{7,5},{8,10},{10,8},{9,1... | collective-permute-start | bytes 983048 | tf_op jit(solution)/shard_map/ppermute | solution.py:277
  107.6 1.3 collective-permute-done.6.got
  108.9 0.5 shard_map.86
  109.4 0.5 collective-permute-start.7
  109.9 0.3 shard_map.87
  110.2 4.0 %collective-permute-done.7.got = bf16[512,128]{1,0:T(8,128)(2,1)S(1)} collective-permute-done((bf16[512,128]{1,0:T(8,128)(2,1)S(1)}, bf16[512,128]{1,0:T(8,128)(2,1)S(1)}, u32[]{:S(2)}, u32[]{:S(2)}) %collective-permute-start.7) | collective-permute-done | bytes 131104 | tf_op jit(solution)/shard_map/ppermute | solution.py:277
  114.2 0.5 shard_map.88
  114.8 14.0 %all_to_all.27.x = bf16[16,40,128]{2,1,0:T(8,128)(2,1)S(1)} all-to-all(bf16[16,40,128]{2,1,0:T(8,128)(2,1)S(1)} %get-tuple-element.58), channel_id=1, replica_groups=mesh['z2'=2,'z1'=2,'z0'=2,'x_hi'=2,'y'=4,'core'=2,'tp'=2] {'x_hi','y','c..., dimensions={0} | all-to-all | bytes 327680 | tf_op jit(solution)/shard_map/all_to_all | solution.py:281
  128.8 9.0 %all_to_all.28.x = bf16[8,40,128]{2,1,0:T(8,128)(2,1)S(1)} all-to-all(bf16[8,40,128]{2,1,0:T(8,128)(2,1)S(1)} %shard_map.89), channel_id=1, replica_groups=mesh['z2'=2,'z1'=2,'z0'=2,'x_hi'=2,'y'=4,'core'=2,'tp'=2] {'z0','z1','z2'}, dimensions={0} | all-to-all | bytes 163840 | tf_op jit(solution)/shard_map/all_to_all | solution.py:281
  137.8 12.3 %all_to_all.29.x = bf16[16,40,128]{2,1,0:T(8,128)(2,1)S(1)} all-to-all(bf16[16,40,128]{2,1,0:T(8,128)(2,1)S(1)} %shard_map.90), channel_id=1, replica_groups=mesh['z2'=2,'z1'=2,'z0'=2,'x_hi'=2,'y'=4,'core'=2,'tp'=2] {'x_hi','y','c..., dimensions={0} | all-to-all | bytes 327680 | tf_op jit(solution)/shard_map/all_to_all | solution.py:281
  150.1 1.2 shard_map.91
  (2 shorter events, 0.1 us)
Async XLA Ops:
  2.4 6.8 %collective-permute-start = (f32[512,128]{1,0:T(8,128)S(1)}, f32[512,128]{1,0:T(8,128)S(1)}, u32[]{:S(2)}, u32[]{:S(2)}) collective-permute-start(f32[512,128]{1,0:T(8,128)S(1)} %get-tuple-element.34.part), channel_id=1, source_target_pairs={{0,1},{1,0},{2,3},{3,2},{4,5},{5,4},{6,7},{7,6},{8,9},{9,8},{10,11... | collective-permute-start | bytes 786440 | tf_op jit(solution)/shard_map/ppermute | solution.py:277
  9.9 4.2 %collective-permute-start.1 = (bf16[256,640]{1,0:T(8,128)(2,1)S(1)}, bf16[256,640]{1,0:T(8,128)(2,1)S(1)}, u32[]{:S(2)}, u32[]{:S(2)}) collective-permute-start(bf16[256,640]{1,0:T(8,128)(2,1)S(1)} %get-tuple-element.38), channel_id=1, source_target_pairs={{0,2},{2,0},{1,3},{3,1},{4,6},{6,4},{5,7},{7,5},{8,10},{10,8},{9,1... | collective-permute-start | bytes 983048 | tf_op jit(solution)/shard_map/ppermute | solution.py:277
  47.5 6.0 %collective-permute-start.2 = (bf16[256,640]{1,0:T(8,128)(2,1)S(1)}, bf16[256,640]{1,0:T(8,128)(2,1)S(1)}, u32[]{:S(2)}, u32[]{:S(2)}) collective-permute-start(bf16[256,640]{1,0:T(8,128)(2,1)S(1)} %get-tuple-element.39.own), channel_id=1, source_target_pairs={{0,1},{1,0},{2,3},{3,2},{4,5},{5,4},{6,7},{7,6},{8,9},{9,8},{10,11... | collective-permute-start | bytes 983048 | tf_op jit(solution)/shard_map/ppermute | solution.py:277
  47.8 12.3 %collective-permute-start.4 = (bf16[256,640]{1,0:T(8,128)(2,1)S(1)}, bf16[256,640]{1,0:T(8,128)(2,1)S(1)}, u32[]{:S(2)}, u32[]{:S(2)}) collective-permute-start(bf16[256,640]{1,0:T(8,128)(2,1)S(1)} %get-tuple-element.44.own), channel_id=1, source_target_pairs={{0,1},{1,0},{2,3},{3,2},{4,5},{5,4},{6,7},{7,6},{8,9},{9,8},{10,11... | collective-permute-start | bytes 983048 | tf_op jit(solution)/shard_map/ppermute | solution.py:277
  57.3 9.8 %collective-permute-start.3 = (bf16[256,640]{1,0:T(8,128)(2,1)S(1)}, bf16[256,640]{1,0:T(8,128)(2,1)S(1)}, u32[]{:S(2)}, u32[]{:S(2)}) collective-permute-start(bf16[256,640]{1,0:T(8,128)(2,1)S(1)} %get-tuple-element.43), channel_id=1, source_target_pairs={{0,1},{1,0},{2,3},{3,2},{4,5},{5,4},{6,7},{7,6},{8,9},{9,8},{10,11... | collective-permute-start | bytes 983048 | tf_op jit(solution)/shard_map/ppermute | solution.py:277
  63.5 10.2 %collective-permute-start.5 = (bf16[256,640]{1,0:T(8,128)(2,1)S(1)}, bf16[256,640]{1,0:T(8,128)(2,1)S(1)}, u32[]{:S(2)}, u32[]{:S(2)}) collective-permute-start(bf16[256,640]{1,0:T(8,128)(2,1)S(1)} %get-tuple-element.47), channel_id=1, source_target_pairs={{0,1},{1,0},{2,3},{3,2},{4,5},{5,4},{6,7},{7,6},{8,9},{9,8},{10,11... | collective-permute-start | bytes 983048 | tf_op jit(solution)/shard_map/ppermute | solution.py:277
  101.6 7.3 %collective-permute-start.6 = (bf16[256,640]{1,0:T(8,128)(2,1)S(1)}, bf16[256,640]{1,0:T(8,128)(2,1)S(1)}, u32[]{:S(2)}, u32[]{:S(2)}) collective-permute-start(bf16[256,640]{1,0:T(8,128)(2,1)S(1)} %get-tuple-element.51), channel_id=1, source_target_pairs={{0,2},{2,0},{1,3},{3,1},{4,6},{6,4},{5,7},{7,5},{8,10},{10,8},{9,1... | collective-permute-start | bytes 983048 | tf_op jit(solution)/shard_map/ppermute | solution.py:277
  109.4 4.8 %collective-permute-start.7 = (bf16[512,128]{1,0:T(8,128)(2,1)S(1)}, bf16[512,128]{1,0:T(8,128)(2,1)S(1)}, u32[]{:S(2)}, u32[]{:S(2)}) collective-permute-start(bf16[512,128]{1,0:T(8,128)(2,1)S(1)} %get-tuple-element.55), channel_id=1, source_target_pairs={{0,1},{1,0},{2,3},{3,2},{4,5},{5,4},{6,7},{7,6},{8,9},{9,8},{10,11... | collective-permute-start | bytes 393224 | tf_op jit(solution)/shard_map/ppermute | solution.py:277
